TPU v7x, 32 devices: a whole 2x2x4 slice. The times are simulated.
32 devices in a mesh: tm: 8 (over z, x), rows: 4 (over y, core).
Axes of the slice: x: 2, y: 2, z: 4, core: 2. Of those that a mesh axis runs over, the one named last changes fastest.
Arguments:
- frames: bfloat16 [8, 32, 32, 640], P('tm', 'rows'), may hold values from -24 to 24
- conv_weight: bfloat16 [3, 3, 640, 640], replicated, may hold values from -0.078125 to 0.078125
- conv_bias: float32 [640], replicated, may hold values from -1.5 to 1.5
- ref_features: bfloat16 [1024, 640], P('tm'), may hold values from -6 to 6
- w_query: bfloat16 [640, 640], replicated, may hold values from -0.25 to 0.25
- w_key: bfloat16 [640, 640], replicated, may hold values from -0.25 to 0.25
- w_value: bfloat16 [640, 640], replicated, may hold values from -0.25 to 0.25
- w_out: bfloat16 [640, 640], replicated, may hold values from -0.25 to 0.25
- out_bias: float32 [640], replicated, may hold values from -1.5 to 1.5
Outputs:
- hidden: bfloat16 [8, 32, 32, 640], P('tm', 'rows')
- attended: bfloat16 [8, 32, 32, 640], P('tm', 'rows')
All inputs are finite; a program needn't handle non-finite values.
Results may differ from a plain program's by a relative error of at most 0.025.
Values may be sent and summed in bfloat16 or wider, within the bound.
No kernel may reach another device: no remote copies, remote signals or barrier semaphores. Data moves between devices by JAX's collectives and lax.ppermute only.
A program may use at most 128 MiB of HBM per device.

v0:
```python
import jax
import jax.numpy as jnp
from jax import lax
from jax.sharding import PartitionSpec as P

HD = 80


key_block = 1024


def extended(value, sides, width):
    for axis, dim in sides:
        size, length = (lax.axis_size(axis), value.shape[dim])
        up = [(i, (i + 1) % size) for i in range(size - 1)]
        down = [(j, i) for i, j in up]
        last = lax.slice_in_dim(value, length - width, length, axis=dim)
        initial = lax.slice_in_dim(value, 0, width, axis=dim)
        before = lax.ppermute(last, axis, up)
        after = lax.ppermute(initial, axis, down)
        value = jnp.concatenate([before, value, after], axis=dim)
    return value


def attend_update(carry, query_heads, keys, values, heads):
    top, total, summed = carry
    count, band = (query_heads.shape[0], query_heads.shape[1])
    length = keys.shape[1]
    summed = summed.reshape(count, band, heads, HD)
    width = min(key_block, length)
    key_part = keys.reshape(keys.shape[0], width, heads, HD)
    value_part = values.reshape(values.shape[0], width, heads, HD)
    scores = jnp.einsum(
        "fqhd,khd->fhqk", query_heads, key_part[0], preferred_element_type=jnp.float32
    )
    scores = scores * HD ** (-0.5)
    new_top = jnp.maximum(top, jnp.max(scores, axis=3))
    factor = jnp.exp(top - new_top)
    weights = jnp.exp(scores - new_top[..., None])
    total = total * factor + jnp.sum(weights, axis=3)
    product = jnp.einsum(
        "fhqk,khd->fqhd",
        weights.astype(jnp.bfloat16),
        value_part[0],
        preferred_element_type=jnp.float32,
    )
    summed = summed * jnp.transpose(factor, (0, 2, 1))[..., None] + product
    return (new_top, total, summed.reshape(count, band, heads * HD))


def project_pair(source, w_key, w_value, count, channels):
    key = (
        jnp.dot(source, w_key, preferred_element_type=jnp.float32)
        .astype(jnp.bfloat16)
        .reshape(count, -1, channels)
    )
    value = (
        jnp.dot(source, w_value, preferred_element_type=jnp.float32)
        .astype(jnp.bfloat16)
        .reshape(count, -1, channels)
    )
    return (key, value)


def shards(frames, conv_weight, conv_bias, ref_features, w_query, w_key, w_value, w_out, out_bias):
    count, band_rows, width, channels = frames.shape
    heads = channels // HD
    band = band_rows * width
    activated = jax.nn.silu(frames.astype(jnp.float32)).astype(jnp.bfloat16)
    padded = extended(activated, (("rows", 1),), 1)
    padded = jnp.pad(padded, ((0, 0), (0, 0), (1, 1), (0, 0)))
    convolved = jnp.zeros((count * band, channels), jnp.float32)
    for row_tap in range(3):
        for col_tap in range(3):
            window = padded[:, row_tap : row_tap + band_rows, col_tap : col_tap + width].reshape(
                count * band, channels
            )
            convolved = convolved + jnp.dot(
                window, conv_weight[row_tap, col_tap], preferred_element_type=jnp.float32
            )
    hidden = (
        frames.reshape(count * band, channels).astype(jnp.float32) + convolved + conv_bias
    ).astype(jnp.bfloat16)
    query = jnp.dot(hidden, w_query, preferred_element_type=jnp.float32).astype(jnp.bfloat16)
    query_heads = query.reshape(count, band, heads, HD)
    start_state = (
        jnp.full((count, heads, band), -1e30, jnp.float32),
        jnp.zeros((count, heads, band), jnp.float32),
        jnp.zeros((count, band, channels), jnp.float32),
    )
    key, value = project_pair(hidden, w_key, w_value, count, channels)
    all_keys, all_values = (
        lax.all_gather(key, "rows", axis=1, tiled=True),
        lax.all_gather(value, "rows", axis=1, tiled=True),
    )
    state = attend_update(start_state, query_heads, all_keys, all_values, heads)
    ref_key = jnp.dot(ref_features, w_key, preferred_element_type=jnp.float32).astype(jnp.bfloat16)
    ref_value = jnp.dot(ref_features, w_value, preferred_element_type=jnp.float32).astype(
        jnp.bfloat16
    )
    every_key, every_value = (
        lax.all_gather(ref_key, "tm", axis=0, tiled=True),
        lax.all_gather(ref_value, "tm", axis=0, tiled=True),
    )
    state = attend_update(state, query_heads, every_key[None], every_value[None], heads)
    top, total, summed = state
    mixed = summed.reshape(count, band, heads, HD) / jnp.transpose(total, (0, 2, 1))[..., None]
    mixed = mixed.reshape(count * band, channels).astype(jnp.bfloat16)
    attended = (jnp.dot(mixed, w_out, preferred_element_type=jnp.float32) + out_bias).astype(
        jnp.bfloat16
    )
    return (
        hidden.reshape(count, band_rows, width, channels),
        attended.reshape(count, band_rows, width, channels),
    )


def solution(mesh):
    return jax.shard_map(
        shards,
        mesh=mesh,
        in_specs=(P("tm", "rows", None, None), P(), P(), P("tm", None), P(), P(), P(), P(), P()),
        out_specs=(P("tm", "rows", None, None), P("tm", "rows", None, None)),
        check_vma=False,
    )
```

profile of v0, /device:TPU:0, one launch (start us, length us, event | category | flops | bytes accessed | tf_op | source)
XLA Modules:
  0.0 166.1 jit_solution(15787326503942143759)
XLA Ops:
  7.2 1.3 multiply_convert_fusion
  8.6 2.6 %collective-permute-start = (bf16[1,1,32,640]{3,2,1,0:T(8,128)(2,1)S(1)}, bf16[1,1,32,640]{3,2,1,0:T(8,128)(2,1)S(1)}, u32[]{:S(2)}, u32[]{:S(2)}) collective-permute-start(bf16[1,1,32,640]{3,2,1,0:T(8,128)(2,1)S(1)} %get-tuple-element.10), channel_id=1, source_target_pairs={{0,1},{1,2},{2,3},{4,5},{5,6},{6,7},{8,9},{9,10},{10,11},{12,13},{... | collective-permute-start | bytes 122888 | tf_op jit(solution)/shard_map/ppermute | solution.py:19
  11.2 1.3 collective-permute-start.1
  12.5 3.9 %collective-permute-done.1 = bf16[1,1,32,640]{3,2,1,0:T(8,128)(2,1)S(1)} collective-permute-done((bf16[1,1,32,640]{3,2,1,0:T(8,128)(2,1)S(1)}, bf16[1,1,32,640]{3,2,1,0:T(8,128)(2,1)S(1)}, u32[]{:S(2)}, u32[]{:S(2)}) %collective-permute-start.1) | collective-permute-done | bytes 40992 | tf_op jit(solution)/shard_map/ppermute | solution.py:20
  16.8 1.6 fusion.52
  22.4 1.2 convolution_convert_fusion.2
  23.6 1.2 convolution_convert_fusion
  24.9 1.0 convolution_convert_fusion.4
  26.1 1.0 convolution_convert_fusion.3
  27.8 16.8 %all-gather.11.cloned.1.call-done = bf16[1024,640]{1,0:T(8,128)(2,1)} async-done(((bf16[256,640]{1,0:T(8,128)(2,1)}), bf16[1024,640]{1,0:T(8,128)(2,1)}) %all-gather.11.cloned.1.call-update) | async-done | bytes 1310736 | tf_op jit(solution)/shard_map/all_gather | solution.py:93
  44.6 1.6 copy.19
  46.2 4.6 %bitcast_reduce_fusion.1 = (f32[8,256]{1,0:T(8,128)S(1)}, f32[8,1024,256]{2,1,0:T(8,128)}) fusion(bf16[1024,8,80]{0,2,1:T(8,128)(2,1)S(1)} %bitcast.200, bf16[256,8,80]{0,2,1:T(8,128)(2,1)S(1)} %bitcast.201), kind=kOutput, calls=%fused_computation.4 | convolution fusion | flops 339736576 | bytes 10035200 | tf_op jit(solution)/shard_map/fqhd,khd->fhqk/dot_general | solution.py:33
  50.7 14.2 %all-gather.13.cloned.1.call-done = bf16[1024,640]{1,0:T(8,128)(2,1)} async-done(((bf16[256,640]{1,0:T(8,128)(2,1)}), bf16[1024,640]{1,0:T(8,128)(2,1)}) %all-gather.13.cloned.1.call-update) | async-done | bytes 1310736 | tf_op jit(solution)/shard_map/all_gather | solution.py:94
  64.9 1.6 copy.21
  66.6 42.7 %all-gather.7.cloned.1.call-done = bf16[1024,640]{1,0:T(8,128)(2,1)} async-done(((bf16[128,640]{1,0:T(8,128)(2,1)}), bf16[1024,640]{1,0:T(8,128)(2,1)}) %all-gather.7.cloned.1.call-update) | async-done | bytes 1310736 | tf_op jit(solution)/shard_map/all_gather | solution.py:102
  109.2 1.6 copy.23
  110.8 2.4 %bitcast_reduce_fusion = (f32[8,256]{1,0:T(8,128)S(1)}, f32[8,1024,256]{2,1,0:T(8,128)S(1)}) fusion(bf16[1024,8,80]{0,2,1:T(8,128)(2,1)S(1)} %bitcast.199, bf16[256,8,80]{0,2,1:T(8,128)(2,1)} %bitcast.202), kind=kOutput, calls=%fused_computation.1 | convolution fusion | flops 339736576 | bytes 10035200 | tf_op jit(solution)/shard_map/fqhd,khd->fhqk/dot_general | solution.py:33
  113.3 1.1 copy-done.1
  114.3 2.7 %fusion.2 = (f32[8,256]{1,0:T(8,128)S(1)}, f32[8,256]{1,0:T(8,128)S(1)}) fusion(f32[8,1024,256]{2,1,0:T(8,128)S(1)} %copy-done.1, f32[8,256]{1,0:T(8,128)S(1)} %get-tuple-element.16, f32[8,256]{1,0:T(8,128)S(1)} %get-tuple-element.15, f32[8,1024,256]{2,1,0:T(8,128)S(1)} %get-tuple-element.18), kind=kLoop, calls=%fused_computation.6 | loop fusion | flops 12578816 | bytes 16809984 | tf_op jit(solution)/shard_map/reduce_sum | solution.py:40
  117.1 1.6 fusion.31
  118.7 33.0 %all-gather.9.cloned.1.call-done = bf16[1024,640]{1,0:T(8,128)(2,1)} async-done(((bf16[128,640]{1,0:T(8,128)(2,1)}), bf16[1024,640]{1,0:T(8,128)(2,1)}) %all-gather.9.cloned.1.call-update) | async-done | bytes 1310736 | tf_op jit(solution)/shard_map/all_gather | solution.py:103
  151.7 1.6 copy.24
  153.3 5.0 %fusion.40 = bf16[1,256,8,80]{1,3,2,0:T(8,128)(2,1)S(1)} fusion(f32[1,256,8,80]{1,3,2,0:T(8,128)S(1)} %fusion.31, bf16[1024,8,80]{0,2,1:T(8,128)(2,1)S(1)} %bitcast.206, f32[8,1024,256]{2,1,0:T(8,128)} %copy-done.2, f32[8,256]{1,0:T(8,128)S(1)} %get-tuple-element.15, f32[256,8]{0,1:T(8,128)S(1)} %get-tuple-element.12), kind=kOutput, calls=%fused_computation.45 | convolution fusion | flops 342327296 | bytes 10698752 | tf_op jit(solution)/shard_map/fhqk,khd->fqhd/dot_general | solution.py:41
  158.3 1.2 fusion.34
  (50 shorter events, 5.3 us)
Async XLA Ops:
  7.2 15.2 %copy-start = (bf16[640,640]{1,0:T(8,128)(2,1)S(1)}, bf16[640,640]{1,0:T(8,128)(2,1)}, u32[]{:S(2)}) copy-start(bf16[640,640]{1,0:T(8,128)(2,1)} %param.14) | copy-start | bytes 2457604
  7.2 37.4 %all-gather.11.cloned.1.call-start = ((), (), s32[]{:S(2)}) async-start(), calls=%async_computation.2 | async-start | bytes 1638400 | tf_op jit(solution)/shard_map/all_gather | solution.py:93
  7.2 11.2 %copy-start.3 = (bf16[3,3,640,640]{3,2,1,0:T(8,128)(2,1)S(1)}, bf16[3,3,640,640]{3,2,1,0:T(8,128)(2,1)}, u32[]{:S(2)}) copy-start(bf16[3,3,640,640]{3,2,1,0:T(8,128)(2,1)} %param.10) | copy-start | bytes 22118404
  8.6 3.9 %collective-permute-start = (bf16[1,1,32,640]{3,2,1,0:T(8,128)(2,1)S(1)}, bf16[1,1,32,640]{3,2,1,0:T(8,128)(2,1)S(1)}, u32[]{:S(2)}, u32[]{:S(2)}) collective-permute-start(bf16[1,1,32,640]{3,2,1,0:T(8,128)(2,1)S(1)} %get-tuple-element.10), channel_id=1, source_target_pairs={{0,1},{1,2},{2,3},{4,5},{5,6},{6,7},{8,9},{9,10},{10,11},{12,13},{... | collective-permute-start | bytes 122888 | tf_op jit(solution)/shard_map/ppermute | solution.py:19
  11.2 5.2 %collective-permute-start.1 = (bf16[1,1,32,640]{3,2,1,0:T(8,128)(2,1)S(1)}, bf16[1,1,32,640]{3,2,1,0:T(8,128)(2,1)S(1)}, u32[]{:S(2)}, u32[]{:S(2)}) collective-permute-start(bf16[1,1,32,640]{3,2,1,0:T(8,128)(2,1)S(1)} %get-tuple-element.11), channel_id=1, source_target_pairs={{1,0},{2,1},{3,2},{5,4},{6,5},{7,6},{9,8},{10,9},{11,10},{13,12},{... | collective-permute-start | bytes 122888 | tf_op jit(solution)/shard_map/ppermute | solution.py:20
  19.0 2.9 %copy-start.7 = (bf16[1,8,32,640]{3,2,1,0:T(8,128)(2,1)S(1)}, bf16[1,8,32,640]{3,2,1,0:T(8,128)(2,1)}, u32[]{:S(2)}) copy-start(bf16[1,8,32,640]{3,2,1,0:T(8,128)(2,1)} %param.9) | copy-start | bytes 983044
  19.0 2.9 %copy-start.10 = (f32[640]{0:T(1024)S(1)}, f32[640]{0:T(1024)}, u32[]{:S(2)}) copy-start(f32[640]{0:T(1024)} %param.11) | copy-start | bytes 7684
  19.9 3.7 %copy-start.5 = (bf16[640,640]{1,0:T(8,128)(2,1)S(1)}, bf16[640,640]{1,0:T(8,128)(2,1)}, u32[]{:S(2)}) copy-start(bf16[640,640]{1,0:T(8,128)(2,1)} %param.15) | copy-start | bytes 2457604
  20.4 4.5 %copy-start.9 = (bf16[128,640]{1,0:T(8,128)(2,1)S(1)}, bf16[128,640]{1,0:T(8,128)(2,1)}, u32[]{:S(2)}) copy-start(bf16[128,640]{1,0:T(8,128)(2,1)} %param.12) | copy-start | bytes 491524
  20.9 6.3 %copy-start.8 = (bf16[640,640]{1,0:T(8,128)(2,1)S(1)}, bf16[640,640]{1,0:T(8,128)(2,1)}, u32[]{:S(2)}) copy-start(bf16[640,640]{1,0:T(8,128)(2,1)} %param.13) | copy-start | bytes 2457604
  22.4 28.4 %copy-start.4 = (bf16[256,640]{1,0:T(8,128)(2,1)}, bf16[256,640]{1,0:T(8,128)(2,1)S(1)}, u32[]{:S(2)}) copy-start(bf16[256,640]{1,0:T(8,128)(2,1)S(1)} %fusion.35) | copy-start | bytes 983044
  23.6 41.4 %all-gather.13.cloned.1.call-start = ((), (), s32[]{:S(2)}) async-start(), calls=%async_computation.3 | async-start | bytes 1638400 | tf_op jit(solution)/shard_map/all_gather | solution.py:94
  24.8 84.4 %all-gather.7.cloned.1.call-start = ((), (), s32[]{:S(2)}) async-start(), calls=%async_computation | async-start | bytes 1474560 | tf_op jit(solution)/shard_map/all_gather | solution.py:102
  25.9 125.8 %all-gather.9.cloned.1.call-start = ((), (), s32[]{:S(2)}) async-start(), calls=%async_computation.1 | async-start | bytes 1474560 | tf_op jit(solution)/shard_map/all_gather | solution.py:103
  27.8 38.7 %copy-start.6 = (bf16[256,640]{0,1:T(8,128)(2,1)}, bf16[256,640]{0,1:T(8,128)(2,1)S(1)}, u32[]{:S(2)}) copy-start(bf16[256,640]{0,1:T(8,128)(2,1)S(1)} %copy.20) | copy-start | bytes 983044
  110.8 3.5 %copy-start.1 = (f32[8,1024,256]{2,1,0:T(8,128)S(1)}, f32[8,1024,256]{2,1,0:T(8,128)}, u32[]{:S(2)}) copy-start(f32[8,1024,256]{2,1,0:T(8,128)} %get-tuple-element.20) | copy-start | bytes 25165828
  113.3 3.8 %copy-start.2 = (f32[8,1024,256]{2,1,0:T(8,128)}, f32[8,1024,256]{2,1,0:T(8,128)S(1)}, u32[]{:S(2)}) copy-start(f32[8,1024,256]{2,1,0:T(8,128)S(1)} %get-tuple-element.18) | copy-start | bytes 25165828
  118.7 39.6 %copy-start.12 = (f32[640]{0:T(1024)S(1)}, f32[640]{0:T(1024)}, u32[]{:S(2)}) copy-start(f32[640]{0:T(1024)} %param.17) | copy-start | bytes 7684
  153.3 5.0 %copy-start.11 = (bf16[640,640]{1,0:T(8,128)(2,1)S(1)}, bf16[640,640]{1,0:T(8,128)(2,1)}, u32[]{:S(2)}) copy-start(bf16[640,640]{1,0:T(8,128)(2,1)} %param.16) | copy-start | bytes 2457604
Sparse Core Ops, SparseCore 0:
  23.7 20.8 all-gather.10
  46.7 18.1 all-gather.12
  67.1 42.0 all-gather.6
  111.2 40.4 all-gather.8
where the time goes:
time: 166 us
  waiting for transfers between devices  111 us (67%)
  matrix products  24.8 us (15%)
  between operations  14.1 us (8%)
  local copies, waits for them, and re-layouts  7.93 us (5%)
  other arithmetic  4.31 us (3%)
  starting transfers between devices  4.26 us (3%)
    all_gather x1, waiting for transfers between devices, shards(): lax.all_gather(ref_key, 'tm', axis=0, tiled=True)  42.7 us
    all_gather x1, waiting for transfers between devices, shards(): lax.all_gather(ref_value, 'tm', axis=0, tiled=True)  33 us
    all_gather x1, waiting for transfers between devices, shards(): lax.all_gather(key, 'rows', axis=1, tiled=True)  16.8 us
    all_gather x1, waiting for transfers between devices, shards(): lax.all_gather(value, 'rows', axis=1, tiled=True)  14.2 us
    dot_general x2, matrix products, attend_update(): jnp.einsum('fqhd,khd->fhqk', query_heads, key_part[0], preferred_element_...  6.99 us
    dot_general x2, matrix products, attend_update(): jnp.einsum('fhqk,khd->fqhd', weights.astype(jnp.bfloat16), value_part[0],...  6.54 us
    dot_general x9, matrix products, shards(): jnp.dot(window, conv_weight[row_tap, col_tap], preferred_element_type=jnp...  5.3 us
    ppermute x1, waiting for transfers between devices, extended(): after = lax.ppermute(initial, axis, down)  3.94 us
  transfers between devices with their start and end apart: 6, of which 5 were waited for; matrix products, arithmetic and copies ran while one was open for 12% of the time, Pallas kernels for 0%

commit v1 on v0

v1 whole, which is shorter than its diff:
```python
import functools

import jax
import jax.numpy as jnp
from jax import lax
from jax.experimental import pallas as pl
from jax.experimental.pallas import tpu as pltpu
from jax.sharding import PartitionSpec as P

HD = 80
LANES = 128
SCALE = HD ** (-0.5) * 1.4426950408889634
BF = jnp.bfloat16
F32 = jnp.float32
VMEM_LIMIT = 24 << 20


def vmem_call(body, outs, scratch, *operands, flops=0):
    moved = sum(v.size * v.dtype.itemsize for v in list(operands) + jax.tree.leaves(outs))
    cost = pl.CostEstimate(flops=flops, bytes_accessed=moved, transcendentals=0)
    whole = pl.BlockSpec(memory_space=pltpu.VMEM)
    return pl.pallas_call(
        body,
        out_shape=outs,
        in_specs=[whole] * len(operands),
        out_specs=jax.tree.map(lambda _: whole, outs),
        scratch_shapes=scratch,
        cost_estimate=cost,
        compiler_params=pltpu.CompilerParams(vmem_limit_bytes=VMEM_LIMIT),
    )(*operands)


def silu(value):
    value = value.astype(F32)
    return value / (1.0 + jnp.exp(-value))


def opening_kernel(
    width, core, x_in, core_row, cross_row, weight_in, bias, wq_in, wk_in, wv_in, wo_in,
    hidden_out, hidden_work, query_out, wk_out, wv_out, wo_out,
    x, weight, square, shifted, wq, x_sem, weight_sem, square_sem,
):
    band, channels = x.shape
    heads = channels // HD
    x_copy = pltpu.make_async_copy(x_in, x, x_sem)
    square_copies = [
        pltpu.make_async_copy(source, square.at[i], square_sem.at[i])
        for i, source in enumerate((wk_in, wv_in, wq_in, wo_in))
    ]
    tap_copies = [
        pltpu.make_async_copy(weight_in.at[row], weight.at[row], weight_sem.at[row])
        for row in range(3)
    ]
    x_copy.start()
    for copy in square_copies:
        copy.start()
    wo_out[...] = jnp.zeros_like(wo_out)
    wq[...] = jnp.zeros_like(wq)
    is_first = core[0] == 0
    above = jnp.where(is_first, cross_row[...], core_row[...])
    below = jnp.where(is_first, core_row[...], cross_row[...])
    x_copy.wait()
    active = jnp.concatenate([silu(above), silu(x[...]), silu(below)], axis=0)
    rows = active.shape[0]
    column = lax.broadcasted_iota(jnp.int32, active.shape, 0) % width
    shifted[0] = jnp.where(column == 0, 0.0, pltpu.roll(active, 1, 0)).astype(BF)
    shifted[1] = active.astype(BF)
    shifted[2] = jnp.where(column == width - 1, 0.0, pltpu.roll(active, rows - 1, 0)).astype(BF)
    for copy in square_copies[:2]:
        copy.wait()
    tap_copies[0].start()
    wk_out[...] = square[0].T
    wv_out[...] = square[1].T
    for copy in square_copies[2:]:
        copy.wait()
    tap_copies[1].start()
    for head in range(heads):
        own, padded = slice(head * HD, (head + 1) * HD), slice(head * LANES, head * LANES + HD)
        wq[:, padded] = square[2, :, own]
        wo_out[padded, :] = square[3, own, :]
    total = x[...].astype(F32) + bias[...][None, :]
    for row in range(3):
        tap_copies[row].wait()
        if row == 0:
            tap_copies[2].start()
        for col in range(3):
            total = total + jnp.dot(
                shifted[col, row * width : row * width + band],
                weight[row, col],
                preferred_element_type=F32,
            )
    hidden = total.astype(BF)
    hidden_out[...] = hidden
    hidden_work[...] = hidden
    query_out[...] = (
        jnp.dot(hidden, wq[...], preferred_element_type=F32) * SCALE
    ).astype(BF)


def opening(core, x, core_row, cross_row, weight, bias, wq, wk, wv, wo, width):
    band, channels = x.shape
    heads = channels // HD
    shape = jax.ShapeDtypeStruct
    far = pl.BlockSpec(memory_space=pltpu.HBM)
    near = pl.BlockSpec(memory_space=pltpu.VMEM)
    outs = (
        shape((band, channels), BF),
        shape((band, channels), BF),
        shape((band, heads * LANES), BF),
        shape((channels, channels), BF),
        shape((channels, channels), BF),
        shape((heads * LANES, channels), BF),
    )
    x, weight, wq, wk, wv, wo = [
        pltpu.with_memory_space_constraint(v, pltpu.HBM) for v in (x, weight, wq, wk, wv, wo)
    ]
    return pl.pallas_call(
        functools.partial(opening_kernel, width),
        out_shape=outs,
        in_specs=[pl.BlockSpec(memory_space=pltpu.SMEM), far, near, near, far, near] + [far] * 4,
        out_specs=(near,) * len(outs),
        scratch_shapes=[
            pltpu.VMEM((band, channels), BF),
            pltpu.VMEM(weight.shape, BF),
            pltpu.VMEM((4, channels, channels), BF),
            pltpu.VMEM((3, band + 2 * width, channels), BF),
            pltpu.VMEM((channels, heads * LANES), BF),
            pltpu.SemaphoreType.DMA,
            pltpu.SemaphoreType.DMA((3,)),
            pltpu.SemaphoreType.DMA((4,)),
        ],
        cost_estimate=pl.CostEstimate(
            flops=18 * band * channels * channels, bytes_accessed=16 << 20, transcendentals=0
        ),
        compiler_params=pltpu.CompilerParams(vmem_limit_bytes=VMEM_LIMIT),
    )(core, x, core_row, cross_row, weight, bias, wq, wk, wv, wo)


def attend_kernel(pieces, first, last, *refs):
    refs = list(refs)
    sources = [refs.pop(0) for _ in range(pieces)]
    wk, wv, query = [refs.pop(0) for _ in range(3)]
    if not first:
        top_in, sum_in = refs.pop(0), refs.pop(0)
    if last:
        wo, bias, out, keys, values, mixed = refs
    else:
        top_out, sum_out, keys, values = refs
    channels = wk.shape[0]
    heads = channels // HD
    band = query.shape[0]
    tokens = keys.shape[1]
    keys[channels:, :] = jnp.zeros((keys.shape[0] - channels, tokens), BF)
    start = 0
    for source in sources:
        part = source[...]
        length = part.shape[0]
        here = slice(start, start + length)
        contract = (((1,), (1,)), ((), ()))
        keys[:channels, here] = lax.dot_general(
            wk[...], part, contract, preferred_element_type=F32
        ).astype(BF)
        value = lax.dot_general(wv[...], part, contract, preferred_element_type=F32).astype(BF)
        for head in range(heads):
            values[head * LANES : head * LANES + HD, here] = value[head * HD : (head + 1) * HD]
            values[head * LANES + HD : (head + 1) * LANES, here] = jnp.ones(
                (LANES - HD, length), BF
            )
        start += length

    def score(head):
        return jnp.dot(
            query[:, head * LANES : (head + 1) * LANES],
            keys[head * HD : head * HD + LANES, :],
            preferred_element_type=F32,
        )

    def weigh(scores, head):
        top = jnp.broadcast_to(jnp.max(scores, axis=1, keepdims=True), (band, LANES))
        if not first:
            top = jnp.maximum(top, top_in[head])
        weights = jnp.concatenate(
            [
                jnp.exp2(scores[:, at : at + LANES] - top).astype(BF)
                for at in range(0, tokens, LANES)
            ],
            axis=1,
        )
        return top, weights

    def finish(head, top, weights):
        product = lax.dot_general(
            weights,
            values[head * LANES : (head + 1) * LANES, :],
            (((1,), (1,)), ((), ())),
            preferred_element_type=F32,
        )
        if not first:
            product = product + sum_in[head] * jnp.exp2(top_in[head] - top)
        if last:
            mixed[:, head * LANES : (head + 1) * LANES] = (
                product / product[:, HD : HD + 1]
            ).astype(BF)
        else:
            top_out[head] = top
            sum_out[head] = product

    scores, ready = score(0), None
    for head in range(heads + 1):
        upcoming = score(head + 1) if head + 1 < heads else None
        weighed = weigh(scores, head) if head < heads else None
        if ready is not None:
            finish(head - 1, *ready)
        scores, ready = upcoming, weighed
    if last:
        out[...] = (
            jnp.dot(mixed[...], wo[...], preferred_element_type=F32) + bias[...][None, :]
        ).astype(BF)


def attend(sources, wk, wv, query, state=None, final=None):
    channels = wk.shape[0]
    heads = channels // HD
    band = query.shape[0]
    tokens = sum(source.shape[0] for source in sources)
    shape = jax.ShapeDtypeStruct
    scratch = [
        pltpu.VMEM((channels - HD + LANES, tokens), BF),
        pltpu.VMEM((heads * LANES, tokens), BF),
    ]
    operands = list(sources) + [wk, wv, query]
    if state is not None:
        operands += list(state)
    if final is not None:
        operands += list(final)
        outs = shape((band, channels), BF)
        scratch.append(pltpu.VMEM((band, heads * LANES), BF))
    else:
        outs = (shape((heads, band, LANES), F32), shape((heads, band, LANES), F32))
    return vmem_call(
        functools.partial(attend_kernel, len(sources), state is None, final is not None),
        outs,
        scratch,
        *operands,
        flops=4 * tokens * channels * (channels + 2 * band),
    )


def swap(value, axis, bit):
    size = lax.axis_size(axis)
    return lax.ppermute(value, axis, [(i, i ^ bit) for i in range(size)])


def shards(frames, conv_weight, conv_bias, ref_features, w_query, w_key, w_value, w_out, out_bias):
    count, band_rows, width, channels = frames.shape
    band = band_rows * width
    x = frames.reshape(count * band, channels)
    core = (lax.axis_index("rows") % 2).reshape(1).astype(jnp.int32)
    is_first = core[0] == 0
    first_row, last_row = x[:width], x[band - width :]
    between = [(i, i + 1) for i in range(1, lax.axis_size("rows") - 1, 2)]
    cross_row = lax.ppermute(
        jnp.where(is_first, first_row, last_row), "rows", between + [(j, i) for i, j in between]
    )
    core_row = swap(jnp.where(is_first, last_row, first_row), "rows", 1)
    half = ref_features.shape[0] // 2
    gathered = lax.dynamic_slice_in_dim(ref_features, core[0] * half, half, 0)
    bit = lax.axis_size("tm") // 2
    received = swap(gathered, "tm", bit)
    hidden_final, hidden, query, wk, wv, wo = opening(
        core,
        x,
        core_row,
        cross_row,
        conv_weight,
        conv_bias,
        w_query,
        w_key,
        w_value,
        w_out,
        width,
    )
    received, hidden = lax.optimization_barrier((received, hidden))
    hidden_y = swap(hidden, "rows", 2)
    hidden_core = swap(hidden, "rows", 1)
    while bit > 2:
        bit //= 2
        earlier = jnp.concatenate([gathered, received])
        received = swap(earlier, "tm", bit)
        gathered = earlier
    beside = swap(gathered, "tm", 1)
    state = attend([hidden, hidden_core], wk, wv, query)
    state, received, beside, hidden_y = lax.optimization_barrier((state, received, beside, hidden_y))
    beside_late = swap(received, "tm", 1)
    ref_early = jnp.concatenate([gathered, received, beside])
    ref_early_core = swap(ref_early, "rows", 1)
    hidden_far = swap(hidden_y, "rows", 1)
    state = attend([ref_early, ref_early_core], wk, wv, query, state)
    state, beside_late = lax.optimization_barrier((state, beside_late))
    ref_late_core = swap(beside_late, "rows", 1)
    attended = attend(
        [hidden_y, hidden_far, beside_late, ref_late_core],
        wk,
        wv,
        query,
        state,
        (wo, out_bias),
    )
    return (
        hidden_final.reshape(count, band_rows, width, channels),
        attended.reshape(count, band_rows, width, channels),
    )


def solution(mesh):
    return jax.shard_map(
        shards,
        mesh=mesh,
        in_specs=(P("tm", "rows", None, None), P(), P(), P("tm", None), P(), P(), P(), P(), P()),
        out_specs=(P("tm", "rows", None, None), P("tm", "rows", None, None)),
        check_vma=False,
    )
```

time: 166 us -> 41.3 us (0.25)
  waiting for transfers between devices: 111 us -> 5.25 us
  matrix products: 24.8 us -> 0 us
  Pallas kernels: 0 us -> 19.9 us
  between operations: 14.1 us -> 0.75 us
  starting transfers between devices: 4.26 us -> 13.5 us
  local copies, waits for them, and re-layouts: 7.93 us -> 0.71 us
  other arithmetic: 4.31 us -> 0.91 us
    all_gather x4 -> x0, waiting for transfers between devices: 107 us -> none  [the longest x1 42.7 us: shards(): lax.all_gather(ref_key, 'tm', axis=0, tiled=True)]
    dot_general x19 -> x0, matrix products: 24.8 us -> none  [the longest x2 6.99 us: attend_update(): jnp.einsum('fqhd,khd->fhqk', query_heads, key_part[0], preferred_element_...]
    pallas_call x0 -> x4, Pallas kernels: none -> 19.9 us  [the longest x3 11.9 us: vmem_call(): pl.pallas_call(body, out_shape=outs, in_specs=[whole] * len(operands), ou...]
    ppermute x2 -> x11, starting transfers between devices: 3.91 us -> 13.5 us  [the longest x10 12.9 us: swap(): return lax.ppermute(value, axis, [(i, i ^ bit) for i in range(size)])]
    all_gather x4 -> x0, local copies, waits for them, and re-layouts: 6.41 us -> none  [the longest x1 1.6 us: shards(): lax.all_gather(key, 'rows', axis=1, tiled=True)]
    reduce_sum x1 -> x0, other arithmetic: 2.75 us -> none  [attend_update(): total = total * factor + jnp.sum(weights, axis=3)]
    ppermute x2 -> x11, waiting for transfers between devices: 3.94 us -> 5.25 us  [the longest x10 5.25 us: swap(): return lax.ppermute(value, axis, [(i, i ^ bit) for i in range(size)])]
  transfers between devices with their start and end apart: 6 -> 11, of which waited for: 5 -> 5; matrix products, arithmetic and copies ran while one was open for 12% -> 0% of each run, Pallas kernels for 0% -> 35%
where the time goes in v1:
time: 41.3 us; the launch traced here: 41.1 us
  Pallas kernels  19.9 us (48%)
  starting transfers between devices  13.5 us (33%)
  waiting for transfers between devices  5.25 us (13%)
  other arithmetic  0.91 us (2%)
  between operations  0.75 us (2%)
  local copies, waits for them, and re-layouts  0.71 us (2%)
    ppermute x10, starting transfers between devices, swap(): return lax.ppermute(value, axis, [(i, i ^ bit) for i in range(size)])  12.9 us
    pallas_call x3, Pallas kernels, vmem_call(): pl.pallas_call(body, out_shape=outs, in_specs=[whole] * len(operands), ou...  11.9 us
    pallas_call x1, Pallas kernels, opening(): pl.pallas_call(functools.partial(opening_kernel, width), out_shape=outs,...  8 us
    ppermute x10, waiting for transfers between devices, swap(): return lax.ppermute(value, axis, [(i, i ^ bit) for i in range(size)])  5.25 us
    select_n x1, other arithmetic, shards(): jnp.where(is_first, first_row, last_row)  0.85 us
  transfers between devices with their start and end apart: 11, of which 5 were waited for; matrix products, arithmetic and copies ran while one was open for 0% of the time, Pallas kernels for 35%

profile of v1, /device:TPU:0, one launch (start us, length us, event | category | flops | bytes accessed | tf_op | source)
XLA Modules:
  0.0 41.1 jit_solution(353344815019157975)
XLA Ops:
  0.6 0.0 copy-start
  0.7 0.8 %select_bitcast_fusion = (bf16[32,640]{1,0:T(8,128)(2,1)S(1)}, bf16[32,640]{1,0:T(8,128)(2,1)S(1)}) fusion(pred[]{:T(512)S(6)} %eq.5, bf16[1,8,32,640]{3,2,1,0:T(8,128)(2,1)} %param.9), kind=kLoop, calls=%fused_computation.2 | loop fusion | flops 40960 | bytes 163841 | tf_op jit(solution)/shard_map/jit(_where)/select_n | solution.py:263
  1.5 0.5 %collective-permute-start = (bf16[32,640]{1,0:T(8,128)(2,1)S(1)}, bf16[32,640]{1,0:T(8,128)(2,1)S(1)}, u32[]{:S(2)}, u32[]{:S(2)}) collective-permute-start(bf16[32,640]{1,0:T(8,128)(2,1)S(1)} %get-tuple-element.43), channel_id=1, source_target_pairs={{0,1},{1,0},{2,3},{3,2},{4,5},{5,4},{6,7},{7,6},{8,9},{9,8},{10,11... | collective-permute-start | bytes 122888 | tf_op jit(solution)/shard_map/ppermute | solution.py:251
  2.0 0.7 %collective-permute-start.1 = (bf16[32,640]{1,0:T(8,128)(2,1)S(1)}, bf16[32,640]{1,0:T(8,128)(2,1)S(1)}, u32[]{:S(2)}, u32[]{:S(2)}) collective-permute-start(bf16[32,640]{1,0:T(8,128)(2,1)S(1)} %get-tuple-element.42), channel_id=1, source_target_pairs={{1,2},{2,1},{5,6},{6,5},{9,10},{10,9},{13,14},{14,13},{17,18},{18,... | collective-permute-start | bytes 122888 | tf_op jit(solution)/shard_map/ppermute | solution.py:262
  2.7 3.7 %collective-permute-start.2 = (bf16[64,640]{1,0:T(8,128)(2,1)S(1)}, bf16[64,640]{1,0:T(8,128)(2,1)S(1)}, u32[]{:S(2)}, u32[]{:S(2)}) collective-permute-start(bf16[64,640]{1,0:T(8,128)(2,1)S(1)} %constant_dynamic-slice_fusion), channel_id=1, source_target_pairs={{0,16},{4,20},{8,24},{12,28},{16,0},{20,4},{24,8},{28,12},{1,17},{... | collective-permute-start | bytes 245768 | tf_op jit(solution)/shard_map/ppermute | solution.py:251
  6.4 0.0 collective-permute-done.core_row
  6.4 0.7 %copy-done.1 = f32[640]{0:T(1024)S(1)} copy-done((f32[640]{0:T(1024)S(1)}, f32[640]{0:T(1024)}, u32[]{:S(2)}) %copy-start.1) | copy-done | bytes 2584
  7.1 8.0 %shard_map.104 = (bf16[256,640]{1,0:T(8,128)(2,1)}, bf16[256,640]{1,0:T(8,128)(2,1)S(1)}, bf16[256,1024]{1,0:T(8,128)(2,1)S(1)}, bf16[640,640]{1,0:T(8,128)(2,1)...) custom-call(s32[1]{0:T(128)} %bitcast.core, bf16[256,640]{1,0:T(8,128)(2,1)} %bitcast.8, ...), custom_call_target="tpu_custom_call" | custom-call | flops 1887436800 | bytes 16777216 | tf_op jit(solution)/shard_map/pallas_call | solution.py:117
  15.1 0.0 collective-permute-done.2
  15.1 2.7 %collective-permute-start.3 = (bf16[256,640]{1,0:T(8,128)(2,1)S(1)}, bf16[256,640]{1,0:T(8,128)(2,1)S(1)}, u32[]{:S(2)}, u32[]{:S(2)}) collective-permute-start(bf16[256,640]{1,0:T(8,128)(2,1)S(1)} %get-tuple-element.24.refs_0_), channel_id=1, source_target_pairs={{0,1},{1,0},{2,3},{3,2},{4,5},{5,4},{6,7},{7,6},{8,9},{9,8},{10,11... | collective-permute-start | bytes 983048 | tf_op jit(solution)/shard_map/ppermute | solution.py:251
  17.8 0.9 %collective-permute-start.6 = (bf16[256,640]{1,0:T(8,128)(2,1)S(1)}, bf16[256,640]{1,0:T(8,128)(2,1)S(1)}, u32[]{:S(2)}, u32[]{:S(2)}) collective-permute-start(bf16[256,640]{1,0:T(8,128)(2,1)S(1)} %get-tuple-element.24.refs_0_), channel_id=1, source_target_pairs={{0,2},{1,3},{2,0},{3,1},{4,6},{5,7},{6,4},{7,5},{8,10},{9,11},{10,... | collective-permute-start | bytes 983048 | tf_op jit(solution)/shard_map/ppermute | solution.py:251
  18.7 1.6 %collective-permute-start.4 = (bf16[128,640]{1,0:T(8,128)(2,1)S(1)}, bf16[128,640]{1,0:T(8,128)(2,1)S(1)}, u32[]{:S(2)}, u32[]{:S(2)}) collective-permute-start(bf16[128,640]{1,0:T(8,128)(2,1)S(1)} %pad_maximum_fusion.1), channel_id=1, source_target_pairs={{0,8},{4,12},{8,0},{12,4},{16,24},{20,28},{24,16},{28,20},{1,9},{5... | collective-permute-start | bytes 491528 | tf_op jit(solution)/shard_map/ppermute | solution.py:251
  20.4 1.5 %collective-permute-start.5 = (bf16[128,640]{1,0:T(8,128)(2,1)S(1)}, bf16[128,640]{1,0:T(8,128)(2,1)S(1)}, u32[]{:S(2)}, u32[]{:S(2)}) collective-permute-start(bf16[128,640]{1,0:T(8,128)(2,1)S(1)} %pad_maximum_fusion.1), channel_id=1, source_target_pairs={{0,4},{4,0},{8,12},{12,8},{16,20},{20,16},{24,28},{28,24},{1,5},{5... | collective-permute-start | bytes 491528 | tf_op jit(solution)/shard_map/ppermute | solution.py:251
  21.9 2.5 %shard_map.105 = (f32[8,256,128]{2,1,0:T(8,128)S(1)}, f32[8,256,128]{2,1,0:T(8,128)S(1)}) custom-call(bf16[256,640]{1,0:T(8,128)(2,1)S(1)} %get-tuple-element.24.refs_0_, bf16[256,640]{1,0:T(8,128)(2,1)S(1)} %collective-permute-done.3.refs_1_, bf16[640,640]{1,0:T(8,128)(2,1)S(1)} %get-tuple-element.25.refs_2_.refs_4_, ...), custom_call_target="tpu_custom_call" | custom-call | flops 1509949440 | bytes 4915200 | tf_op jit(solution)/shard_map/pallas_call | solution.py:22
  24.4 0.7 %collective-permute-done.4 = bf16[128,640]{1,0:T(8,128)(2,1)S(1)} collective-permute-done((bf16[128,640]{1,0:T(8,128)(2,1)S(1)}, bf16[128,640]{1,0:T(8,128)(2,1)S(1)}, u32[]{:S(2)}, u32[]{:S(2)}) %collective-permute-start.4) | collective-permute-done | bytes 163872 | tf_op jit(solution)/shard_map/ppermute | solution.py:251
  25.1 1.3 %collective-permute-done.5 = bf16[128,640]{1,0:T(8,128)(2,1)S(1)} collective-permute-done((bf16[128,640]{1,0:T(8,128)(2,1)S(1)}, bf16[128,640]{1,0:T(8,128)(2,1)S(1)}, u32[]{:S(2)}, u32[]{:S(2)}) %collective-permute-start.5) | collective-permute-done | bytes 163872 | tf_op jit(solution)/shard_map/ppermute | solution.py:251
  26.4 1.1 %collective-permute-done.6.refs_0_ = bf16[256,640]{1,0:T(8,128)(2,1)S(1)} collective-permute-done((bf16[256,640]{1,0:T(8,128)(2,1)S(1)}, bf16[256,640]{1,0:T(8,128)(2,1)S(1)}, u32[]{:S(2)}, u32[]{:S(2)}) %collective-permute-start.6) | collective-permute-done | bytes 327712 | tf_op jit(solution)/shard_map/ppermute | solution.py:251
  27.5 0.1 collective-permute-start.8
  27.6 1.7 %collective-permute-start.9 = (bf16[128,640]{1,0:T(8,128)(2,1)S(1)}, bf16[128,640]{1,0:T(8,128)(2,1)S(1)}, u32[]{:S(2)}, u32[]{:S(2)}) collective-permute-start(bf16[128,640]{1,0:T(8,128)(2,1)S(1)} %collective-permute-done.4), channel_id=1, source_target_pairs={{0,4},{4,0},{8,12},{12,8},{16,20},{20,16},{24,28},{28,24},{1,5},{5... | collective-permute-start | bytes 491528 | tf_op jit(solution)/shard_map/ppermute | solution.py:251
  29.3 0.2 collective-permute-start.7
  29.5 4.0 %shard_map.106 = (f32[8,256,128]{2,1,0:T(8,128)S(1)}, f32[8,256,128]{2,1,0:T(8,128)S(1)}) custom-call(bf16[384,640]{1,0:T(8,128)(2,1)S(1)} %pad_maximum_fusion.refs_0_, bf16[384,640]{1,0:T(8,128)(2,1)S(1)} %collective-permute-done.8.refs_1_, bf16[640,640]{1,0:T(8,128)(2,1)S(1)} %get-tuple-element.25.refs_2_.refs_4_, ...), custom_call_target="tpu_custom_call" | custom-call | flops 2264924160 | bytes 7340032 | tf_op jit(solution)/shard_map/pallas_call | solution.py:22
  33.5 0.8 %collective-permute-done.9.refs_2_ = bf16[128,640]{1,0:T(8,128)(2,1)S(1)} collective-permute-done((bf16[128,640]{1,0:T(8,128)(2,1)S(1)}, bf16[128,640]{1,0:T(8,128)(2,1)S(1)}, u32[]{:S(2)}, u32[]{:S(2)}) %collective-permute-start.9) | collective-permute-done | bytes 163872 | tf_op jit(solution)/shard_map/ppermute | solution.py:251
  34.2 1.4 %collective-permute-done.10.refs_3_ = bf16[128,640]{1,0:T(8,128)(2,1)S(1)} collective-permute-done((bf16[128,640]{1,0:T(8,128)(2,1)S(1)}, bf16[128,640]{1,0:T(8,128)(2,1)S(1)}, u32[]{:S(2)}, u32[]{:S(2)}) %collective-permute-start.10) | collective-permute-done | bytes 163872 | tf_op jit(solution)/shard_map/ppermute | solution.py:251
  35.6 5.5 %shard_map.107 = bf16[256,640]{1,0:T(8,128)(2,1)} custom-call(bf16[256,640]{1,0:T(8,128)(2,1)S(1)} %collective-permute-done.6.refs_0_, bf16[256,640]{1,0:T(8,128)(2,1)S(1)} %collective-permute-done.7.refs_1_, bf16[128,640]{1,0:T(8,128)(2,1)S(1)} %collective-permute-done.9.refs_2_, bf16[128,640]{1,0:T(8,128)(2,1)S(1)} %collective-permute-done.10.refs_3_, ...), custom_call_target="tpu_custom_call" | custom-call | flops 2264924160 | bytes 6883840 | tf_op jit(solution)/shard_map/pallas_call | solution.py:22
  (12 shorter events, 0.1 us)
Async XLA Ops:
  0.6 2.1 %copy-start = (bf16[128,640]{1,0:T(8,128)(2,1)S(1)}, bf16[128,640]{1,0:T(8,128)(2,1)}, u32[]{:S(2)}) copy-start(bf16[128,640]{1,0:T(8,128)(2,1)} %param.12) | copy-start | bytes 491524
  1.5 4.9 %collective-permute-start = (bf16[32,640]{1,0:T(8,128)(2,1)S(1)}, bf16[32,640]{1,0:T(8,128)(2,1)S(1)}, u32[]{:S(2)}, u32[]{:S(2)}) collective-permute-start(bf16[32,640]{1,0:T(8,128)(2,1)S(1)} %get-tuple-element.43), channel_id=1, source_target_pairs={{0,1},{1,0},{2,3},{3,2},{4,5},{5,4},{6,7},{7,6},{8,9},{9,8},{10,11... | collective-permute-start | bytes 122888 | tf_op jit(solution)/shard_map/ppermute | solution.py:251
  2.0 4.4 %collective-permute-start.1 = (bf16[32,640]{1,0:T(8,128)(2,1)S(1)}, bf16[32,640]{1,0:T(8,128)(2,1)S(1)}, u32[]{:S(2)}, u32[]{:S(2)}) collective-permute-start(bf16[32,640]{1,0:T(8,128)(2,1)S(1)} %get-tuple-element.42), channel_id=1, source_target_pairs={{1,2},{2,1},{5,6},{6,5},{9,10},{10,9},{13,14},{14,13},{17,18},{18,... | collective-permute-start | bytes 122888 | tf_op jit(solution)/shard_map/ppermute | solution.py:262
  2.7 12.4 %collective-permute-start.2 = (bf16[64,640]{1,0:T(8,128)(2,1)S(1)}, bf16[64,640]{1,0:T(8,128)(2,1)S(1)}, u32[]{:S(2)}, u32[]{:S(2)}) collective-permute-start(bf16[64,640]{1,0:T(8,128)(2,1)S(1)} %constant_dynamic-slice_fusion), channel_id=1, source_target_pairs={{0,16},{4,20},{8,24},{12,28},{16,0},{20,4},{24,8},{28,12},{1,17},{... | collective-permute-start | bytes 245768 | tf_op jit(solution)/shard_map/ppermute | solution.py:251
  6.4 0.7 %copy-start.1 = (f32[640]{0:T(1024)S(1)}, f32[640]{0:T(1024)}, u32[]{:S(2)}) copy-start(f32[640]{0:T(1024)} %bias.1) | copy-start | bytes 7684
  15.1 6.8 %collective-permute-start.3 = (bf16[256,640]{1,0:T(8,128)(2,1)S(1)}, bf16[256,640]{1,0:T(8,128)(2,1)S(1)}, u32[]{:S(2)}, u32[]{:S(2)}) collective-permute-start(bf16[256,640]{1,0:T(8,128)(2,1)S(1)} %get-tuple-element.24.refs_0_), channel_id=1, source_target_pairs={{0,1},{1,0},{2,3},{3,2},{4,5},{5,4},{6,7},{7,6},{8,9},{9,8},{10,11... | collective-permute-start | bytes 983048 | tf_op jit(solution)/shard_map/ppermute | solution.py:251
  17.8 9.7 %collective-permute-start.6 = (bf16[256,640]{1,0:T(8,128)(2,1)S(1)}, bf16[256,640]{1,0:T(8,128)(2,1)S(1)}, u32[]{:S(2)}, u32[]{:S(2)}) collective-permute-start(bf16[256,640]{1,0:T(8,128)(2,1)S(1)} %get-tuple-element.24.refs_0_), channel_id=1, source_target_pairs={{0,2},{1,3},{2,0},{3,1},{4,6},{5,7},{6,4},{7,5},{8,10},{9,11},{10,... | collective-permute-start | bytes 983048 | tf_op jit(solution)/shard_map/ppermute | solution.py:251
  18.7 6.3 %collective-permute-start.4 = (bf16[128,640]{1,0:T(8,128)(2,1)S(1)}, bf16[128,640]{1,0:T(8,128)(2,1)S(1)}, u32[]{:S(2)}, u32[]{:S(2)}) collective-permute-start(bf16[128,640]{1,0:T(8,128)(2,1)S(1)} %pad_maximum_fusion.1), channel_id=1, source_target_pairs={{0,8},{4,12},{8,0},{12,4},{16,24},{20,28},{24,16},{28,20},{1,9},{5... | collective-permute-start | bytes 491528 | tf_op jit(solution)/shard_map/ppermute | solution.py:251
  20.4 6.0 %collective-permute-start.5 = (bf16[128,640]{1,0:T(8,128)(2,1)S(1)}, bf16[128,640]{1,0:T(8,128)(2,1)S(1)}, u32[]{:S(2)}, u32[]{:S(2)}) collective-permute-start(bf16[128,640]{1,0:T(8,128)(2,1)S(1)} %pad_maximum_fusion.1), channel_id=1, source_target_pairs={{0,4},{4,0},{8,12},{12,8},{16,20},{20,16},{24,28},{28,24},{1,5},{5... | collective-permute-start | bytes 491528 | tf_op jit(solution)/shard_map/ppermute | solution.py:251
  21.9 13.7 %copy-start.2 = (f32[640]{0:T(1024)S(1)}, f32[640]{0:T(1024)}, u32[]{:S(2)}) copy-start(f32[640]{0:T(1024)} %refs_10_.1) | copy-start | bytes 7684
  27.5 1.9 %collective-permute-start.8 = (bf16[384,640]{1,0:T(8,128)(2,1)S(1)}, bf16[384,640]{1,0:T(8,128)(2,1)S(1)}, u32[]{:S(2)}, u32[]{:S(2)}) collective-permute-start(bf16[384,640]{1,0:T(8,128)(2,1)S(1)} %pad_maximum_fusion.refs_0_), channel_id=1, source_target_pairs={{0,1},{1,0},{2,3},{3,2},{4,5},{5,4},{6,7},{7,6},{8,9},{9,8},{10,11... | collective-permute-start | bytes 1474568 | tf_op jit(solution)/shard_map/ppermute | solution.py:251
  27.6 6.6 %collective-permute-start.9 = (bf16[128,640]{1,0:T(8,128)(2,1)S(1)}, bf16[128,640]{1,0:T(8,128)(2,1)S(1)}, u32[]{:S(2)}, u32[]{:S(2)}) collective-permute-start(bf16[128,640]{1,0:T(8,128)(2,1)S(1)} %collective-permute-done.4), channel_id=1, source_target_pairs={{0,4},{4,0},{8,12},{12,8},{16,20},{20,16},{24,28},{28,24},{1,5},{5... | collective-permute-start | bytes 491528 | tf_op jit(solution)/shard_map/ppermute | solution.py:251
  29.3 4.9 %collective-permute-start.7 = (bf16[256,640]{1,0:T(8,128)(2,1)S(1)}, bf16[256,640]{1,0:T(8,128)(2,1)S(1)}, u32[]{:S(2)}, u32[]{:S(2)}) collective-permute-start(bf16[256,640]{1,0:T(8,128)(2,1)S(1)} %collective-permute-done.6.refs_0_), channel_id=1, source_target_pairs={{0,1},{1,0},{2,3},{3,2},{4,5},{5,4},{6,7},{7,6},{8,9},{9,8},{10,11... | collective-permute-start | bytes 983048 | tf_op jit(solution)/shard_map/ppermute | solution.py:251
  34.2 1.4 %collective-permute-start.10 = (bf16[128,640]{1,0:T(8,128)(2,1)S(1)}, bf16[128,640]{1,0:T(8,128)(2,1)S(1)}, u32[]{:S(2)}, u32[]{:S(2)}) collective-permute-start(bf16[128,640]{1,0:T(8,128)(2,1)S(1)} %collective-permute-done.9.refs_2_), channel_id=1, source_target_pairs={{0,1},{1,0},{2,3},{3,2},{4,5},{5,4},{6,7},{7,6},{8,9},{9,8},{10,11... | collective-permute-start | bytes 491528 | tf_op jit(solution)/shard_map/ppermute | solution.py:251

commit v2 on v1

v2 whole, which is shorter than its diff:
```python
import functools

import jax
import jax.numpy as jnp
from jax import lax
from jax.experimental import pallas as pl
from jax.experimental.pallas import tpu as pltpu
from jax.sharding import PartitionSpec as P

HD = 80
LANES = 128
SCALE = HD ** (-0.5) * 1.4426950408889634
BF = jnp.bfloat16
F32 = jnp.float32
VMEM_LIMIT = 24 << 20
LONG = pl.CostEstimate(flops=20 << 30, bytes_accessed=32 << 20, transcendentals=0)
COST = pl.CostEstimate(flops=1 << 10, bytes_accessed=1 << 10, transcendentals=0)


def vmem_call(body, outs, scratch, *operands):
    whole = pl.BlockSpec(memory_space=pltpu.VMEM)
    return pl.pallas_call(
        body,
        out_shape=outs,
        in_specs=[whole] * len(operands),
        out_specs=jax.tree.map(lambda _: whole, outs),
        scratch_shapes=scratch,
        cost_estimate=COST,
        compiler_params=pltpu.CompilerParams(vmem_limit_bytes=VMEM_LIMIT),
    )(*operands)


def silu(value):
    value = value.astype(F32)
    return value / (1.0 + jnp.exp(-value))


def shift_columns(active, width):
    rows = active.shape[0]
    column = lax.broadcasted_iota(jnp.int32, active.shape, 0) % width
    left = jnp.where(column == 0, 0.0, pltpu.roll(active, 1, 0))
    right = jnp.where(column == width - 1, 0.0, pltpu.roll(active, rows - 1, 0))
    return left.astype(BF), active.astype(BF), right.astype(BF)


def sending_kernel(
    core, x_in, ref_in, core_out, cross_out, ref_out, rows, ref, row_sem, ref_sem
):
    width = core_out.shape[0]
    band = x_in.shape[0]
    half = ref_out.shape[0]
    copies = [
        pltpu.make_async_copy(x_in.at[:width], rows.at[0], row_sem.at[0]),
        pltpu.make_async_copy(x_in.at[band - width :], rows.at[1], row_sem.at[1]),
        pltpu.make_async_copy(ref_in, ref, ref_sem),
    ]
    for copy in copies:
        copy.start()
    for copy in copies:
        copy.wait()
    is_first = core[0] == 0
    first, last = rows[0], rows[1]
    core_out[...] = jnp.where(is_first, last, first)
    cross_out[...] = jnp.where(is_first, first, last)
    whole = ref[...]
    ref_out[...] = jnp.where(is_first, whole[:half], whole[half:])


def sending(core, x, ref, width):
    band, channels = x.shape
    shape = jax.ShapeDtypeStruct
    near = pl.BlockSpec(memory_space=pltpu.VMEM)
    return pl.pallas_call(
        sending_kernel,
        out_shape=(
            shape((width, channels), BF),
            shape((width, channels), BF),
            shape((ref.shape[0] // 2, channels), BF),
        ),
        in_specs=[pl.BlockSpec(memory_space=pltpu.SMEM)]
        + [pl.BlockSpec(memory_space=pltpu.HBM)] * 2,
        out_specs=(near,) * 3,
        scratch_shapes=[
            pltpu.VMEM((2, width, channels), BF),
            pltpu.VMEM(ref.shape, BF),
            pltpu.SemaphoreType.DMA((2,)),
            pltpu.SemaphoreType.DMA,
        ],
        cost_estimate=LONG,
        compiler_params=pltpu.CompilerParams(vmem_limit_bytes=4 << 20),
    )(core, *[pltpu.with_memory_space_constraint(v, pltpu.HBM) for v in (x, ref)])


def opening_kernel(width, x, weight, bias, wk, wv, wo, total_out, wk_out, wv_out, wo_out, shifted):
    band, channels = x.shape
    heads = channels // HD
    for col, part in enumerate(shift_columns(silu(x[...]), width)):
        shifted[col] = part
    wk_out[...] = wk[...].T
    wv_out[...] = wv[...].T
    wo_out[...] = jnp.zeros_like(wo_out)
    for head in range(heads):
        wo_out[head * LANES : head * LANES + HD, :] = wo[head * HD : (head + 1) * HD, :]
    total = x[...].astype(F32) + bias[...][None, :]
    for col in range(3):
        total = total + jnp.dot(shifted[col], weight[1, col], preferred_element_type=F32)
    total_out[...] = total
    for row, source, target in (
        (0, slice(0, band - width), slice(width, band)),
        (2, slice(width, band), slice(0, band - width)),
    ):
        part = total_out[target]
        for col in range(3):
            part = part + jnp.dot(
                shifted[col, source], weight[row, col], preferred_element_type=F32
            )
        total_out[target] = part


def opening(x, weight, bias, wk, wv, wo, width):
    band, channels = x.shape
    heads = channels // HD
    shape = jax.ShapeDtypeStruct
    square = shape((channels, channels), BF)
    return vmem_call(
        functools.partial(opening_kernel, width),
        (shape((band, channels), F32), square, square, shape((heads * LANES, channels), BF)),
        [pltpu.VMEM((3, band, channels), BF)],
        x,
        weight,
        bias,
        wk,
        wv,
        wo,
    )


def conv_kernel(
    width, core, core_row, cross_row, total, weight, wq, hidden_out, query_out
):
    band, channels = total.shape
    heads = channels // HD
    query_out[...] = jnp.zeros_like(query_out)
    is_first = core[0] == 0
    core_part, cross_part = core_row[...], cross_row[...]
    above = shift_columns(silu(jnp.where(is_first, cross_part, core_part)), width)
    below = shift_columns(silu(jnp.where(is_first, core_part, cross_part)), width)
    top, bottom = total[:width], total[band - width :]
    for col in range(3):
        top = top + jnp.dot(above[col], weight[0, col], preferred_element_type=F32)
        bottom = bottom + jnp.dot(below[col], weight[2, col], preferred_element_type=F32)
    hidden_out[width : band - width] = total[width : band - width].astype(BF)
    hidden_out[:width] = top.astype(BF)
    hidden_out[band - width :] = bottom.astype(BF)
    query = (
        jnp.dot(hidden_out[...], wq[...], preferred_element_type=F32) * SCALE
    ).astype(BF)
    for head in range(heads):
        query_out[:, head * LANES : head * LANES + HD] = query[:, head * HD : (head + 1) * HD]


def conv(core, core_row, cross_row, total, weight, wq, width):
    band, channels = total.shape
    heads = channels // HD
    shape = jax.ShapeDtypeStruct
    near = pl.BlockSpec(memory_space=pltpu.VMEM)
    return pl.pallas_call(
        functools.partial(conv_kernel, width),
        out_shape=(shape((band, channels), BF), shape((band, heads * LANES), BF)),
        in_specs=[pl.BlockSpec(memory_space=pltpu.SMEM)] + [near] * 5,
        out_specs=(near,) * 2,
        cost_estimate=COST,
        compiler_params=pltpu.CompilerParams(vmem_limit_bytes=VMEM_LIMIT),
    )(core, core_row, cross_row, total, weight, wq)


def attend_kernel(pieces, first, last, *refs):
    refs = list(refs)
    sources = [refs.pop(0) for _ in range(pieces)]
    wk, wv, query = [refs.pop(0) for _ in range(3)]
    if not first:
        top_in, sum_in = refs.pop(0), refs.pop(0)
    if last:
        wo, bias, hidden, out, hidden_out, keys, values, mixed = refs
    else:
        top_out, sum_out, keys, values = refs
    channels = wk.shape[0]
    heads = channels // HD
    band = query.shape[0]
    tokens = keys.shape[1]
    keys[channels:, :] = jnp.zeros((keys.shape[0] - channels, tokens), BF)
    start = 0
    for source in sources:
        part = source[...]
        length = part.shape[0]
        here = slice(start, start + length)
        contract = (((1,), (1,)), ((), ()))
        keys[:channels, here] = lax.dot_general(
            wk[...], part, contract, preferred_element_type=F32
        ).astype(BF)
        value = lax.dot_general(wv[...], part, contract, preferred_element_type=F32).astype(BF)
        for head in range(heads):
            values[head * LANES : head * LANES + HD, here] = value[head * HD : (head + 1) * HD]
            values[head * LANES + HD : (head + 1) * LANES, here] = jnp.ones(
                (LANES - HD, length), BF
            )
        start += length

    def score(head):
        return jnp.dot(
            query[:, head * LANES : (head + 1) * LANES],
            keys[head * HD : head * HD + LANES, :],
            preferred_element_type=F32,
        )

    def weigh(scores, head):
        top = jnp.broadcast_to(jnp.max(scores, axis=1, keepdims=True), (band, LANES))
        if not first:
            top = jnp.maximum(top, top_in[head])
        weights = jnp.concatenate(
            [
                jnp.exp2(scores[:, at : at + LANES] - top).astype(BF)
                for at in range(0, tokens, LANES)
            ],
            axis=1,
        )
        return top, weights

    def finish(head, top, weights):
        product = lax.dot_general(
            weights,
            values[head * LANES : (head + 1) * LANES, :],
            (((1,), (1,)), ((), ())),
            preferred_element_type=F32,
        )
        if not first:
            product = product + sum_in[head] * jnp.exp2(top_in[head] - top)
        if last:
            mixed[:, head * LANES : (head + 1) * LANES] = (
                product / product[:, HD : HD + 1]
            ).astype(BF)
        else:
            top_out[head] = top
            sum_out[head] = product

    scores, ready = score(0), None
    for head in range(heads + 1):
        upcoming = score(head + 1) if head + 1 < heads else None
        weighed = weigh(scores, head) if head < heads else None
        if ready is not None:
            finish(head - 1, *ready)
        scores, ready = upcoming, weighed
    if last:
        hidden_out[...] = hidden[...]
        out[...] = (
            jnp.dot(mixed[...], wo[...], preferred_element_type=F32) + bias[...][None, :]
        ).astype(BF)


def attend(sources, wk, wv, query, state=None, final=None):
    channels = wk.shape[0]
    heads = channels // HD
    band = query.shape[0]
    tokens = sum(source.shape[0] for source in sources)
    shape = jax.ShapeDtypeStruct
    scratch = [
        pltpu.VMEM((channels - HD + LANES, tokens), BF),
        pltpu.VMEM((heads * LANES, tokens), BF),
    ]
    operands = list(sources) + [wk, wv, query]
    if state is not None:
        operands += list(state)
    if final is not None:
        operands += list(final)
        outs = (shape((band, channels), BF), shape((band, channels), BF))
        scratch.append(pltpu.VMEM((band, heads * LANES), BF))
    else:
        outs = (shape((heads, band, LANES), F32), shape((heads, band, LANES), F32))
    return vmem_call(
        functools.partial(attend_kernel, len(sources), state is None, final is not None),
        outs,
        scratch,
        *operands,
    )


def swap(value, axis, bit):
    size = lax.axis_size(axis)
    return lax.ppermute(value, axis, [(i, i ^ bit) for i in range(size)])


def shards(frames, conv_weight, conv_bias, ref_features, w_query, w_key, w_value, w_out, out_bias):
    count, band_rows, width, channels = frames.shape
    band = band_rows * width
    x = frames.reshape(count * band, channels)
    core = (lax.axis_index("rows") % 2).reshape(1).astype(jnp.int32)
    core_row, cross_row, gathered = sending(core, x, ref_features, width)
    between = [(i, i + 1) for i in range(1, lax.axis_size("rows") - 1, 2)]
    cross_row = lax.ppermute(cross_row, "rows", between + [(j, i) for i, j in between])
    core_row = swap(core_row, "rows", 1)
    bit = lax.axis_size("tm") // 2
    while bit > 4:
        gathered = jnp.concatenate([gathered, swap(gathered, "tm", bit)])
        bit //= 2
    beside = swap(gathered, "tm", 1)
    column = [swap(gathered, "tm", part) for part in (4, 2, 6)]
    total, wk, wv, wo = opening(
        x, conv_weight, conv_bias, w_key, w_value, w_out, width
    )
    hidden, query = conv(core, core_row, cross_row, total, conv_weight, w_query, width)
    column, beside, hidden = lax.optimization_barrier((column, beside, hidden))
    others = jnp.concatenate(column)
    column = jnp.concatenate([gathered, others])
    column_core = swap(column, "rows", 1)
    hidden_core = swap(hidden, "rows", 1)
    others = swap(others, "tm", 1)
    hidden_y = swap(hidden, "rows", 2)
    state = attend([hidden, hidden_core, column, column_core], wk, wv, query)
    state, hidden_y, others = lax.optimization_barrier((state, hidden_y, others))
    beside = jnp.concatenate([beside, others])
    hidden_far = swap(hidden_y, "rows", 1)
    beside_core = swap(beside, "rows", 1)
    state = attend([hidden_y, beside], wk, wv, query, state)
    attended, hidden = attend(
        [hidden_far, beside_core], wk, wv, query, state, (wo, out_bias, hidden)
    )
    return (
        hidden.reshape(count, band_rows, width, channels),
        attended.reshape(count, band_rows, width, channels),
    )


def solution(mesh):
    return jax.shard_map(
        shards,
        mesh=mesh,
        in_specs=(P("tm", "rows", None, None), P(), P(), P("tm", None), P(), P(), P(), P(), P()),
        out_specs=(P("tm", "rows", None, None), P("tm", "rows", None, None)),
        check_vma=False,
    )
```

time: 41.3 us -> 33.5 us (0.81)
  Pallas kernels: 19.9 us -> 16.6 us
  starting transfers between devices: 13.5 us -> 11.7 us
  waiting for transfers between devices: 5.25 us -> 3.93 us
  other arithmetic: 0.91 us -> 0.02 us
  local copies, waits for them, and re-layouts: 0.71 us -> 0.13 us
    pallas_call x1 -> x2, Pallas kernels: 8 us -> 2.47 us  [the longest x1 1.32 us: conv(): pl.pallas_call(functools.partial(conv_kernel, width), out_shape=(shape((b...]
    pallas_call x3 -> x4, Pallas kernels: 11.9 us -> 14.1 us  [vmem_call(): pl.pallas_call(body, out_shape=outs, in_specs=[whole] * len(operands), ou...]
    ppermute x10 -> x11, starting transfers between devices: 12.9 us -> 11.1 us  [swap(): return lax.ppermute(value, axis, [(i, i ^ bit) for i in range(size)])]
    ppermute x10 -> x11, waiting for transfers between devices: 5.25 us -> 3.93 us  [swap(): return lax.ppermute(value, axis, [(i, i ^ bit) for i in range(size)])]
    select_n x1 -> x0, other arithmetic: 0.85 us -> none  [shards(): jnp.where(is_first, first_row, last_row)]
    unnamed x6 -> x20, local copies, waits for them, and re-layouts: 0.7 us -> 0.08 us
  transfers between devices with their start and end apart: 11 -> 12, of which waited for: 5 -> 4; matrix products, arithmetic and copies ran while one was open for 0% -> 0% of each run, Pallas kernels for 35% -> 35%
where the time goes in v2:
time: 33.5 us; the launch traced here: 33.3 us
  Pallas kernels  16.6 us (50%)
  starting transfers between devices  11.7 us (35%)
  waiting for transfers between devices  3.93 us (12%)
  between operations  0.89 us (3%)
    pallas_call x4, Pallas kernels, vmem_call(): pl.pallas_call(body, out_shape=outs, in_specs=[whole] * len(operands), ou...  14.1 us
    ppermute x11, starting transfers between devices, swap(): return lax.ppermute(value, axis, [(i, i ^ bit) for i in range(size)])  11.1 us
    ppermute x11, waiting for transfers between devices, swap(): return lax.ppermute(value, axis, [(i, i ^ bit) for i in range(size)])  3.93 us
    pallas_call x1, Pallas kernels, conv(): pl.pallas_call(functools.partial(conv_kernel, width), out_shape=(shape((b...  1.32 us
    pallas_call x1, Pallas kernels, sending(): pl.pallas_call(sending_kernel, out_shape=(shape((width, channels), BF), s...  1.15 us
  transfers between devices with their start and end apart: 12, of which 4 were waited for; matrix products, arithmetic and copies ran while one was open for 0% of the time, Pallas kernels for 35%

profile of v2, /device:TPU:0, one launch (start us, length us, event | category | flops | bytes accessed | tf_op | source)
XLA Modules:
  0.0 33.3 jit_solution(12312396121738772432)
XLA Ops:
  0.7 1.2 %shard_map.104 = (bf16[32,640]{1,0:T(8,128)(2,1)S(1)}, bf16[32,640]{1,0:T(8,128)(2,1)S(1)}, bf16[64,640]{1,0:T(8,128)(2,1)S(1)}) custom-call(s32[1]{0:T(128)} %bitcast.core, bf16[256,640]{1,0:T(8,128)(2,1)} %bitcast.4, bf16[128,640]{1,0:T(8,128)(2,1)} %ref_in.1), custom_call_target="tpu_custom_call" | custom-call | flops 21474836480 | bytes 33554432 | tf_op jit(solution)/shard_map/pallas_call | solution.py:73
  1.9 0.0 copy-start.4
  1.9 0.5 %collective-permute-start.4 = (bf16[32,640]{1,0:T(8,128)(2,1)S(1)}, bf16[32,640]{1,0:T(8,128)(2,1)S(1)}, u32[]{:S(2)}, u32[]{:S(2)}) collective-permute-start(bf16[32,640]{1,0:T(8,128)(2,1)S(1)} %get-tuple-element.27), channel_id=1, source_target_pairs={{0,1},{1,0},{2,3},{3,2},{4,5},{5,4},{6,7},{7,6},{8,9},{9,8},{10,11... | collective-permute-start | bytes 122888 | tf_op jit(solution)/shard_map/ppermute | solution.py:289
  2.4 2.6 %collective-permute-start.3 = (bf16[64,640]{1,0:T(8,128)(2,1)S(1)}, bf16[64,640]{1,0:T(8,128)(2,1)S(1)}, u32[]{:S(2)}, u32[]{:S(2)}) collective-permute-start(bf16[64,640]{1,0:T(8,128)(2,1)S(1)} %get-tuple-element.26), channel_id=1, source_target_pairs={{0,4},{4,0},{8,12},{12,8},{16,20},{20,16},{24,28},{28,24},{1,5},{5... | collective-permute-start | bytes 245768 | tf_op jit(solution)/shard_map/ppermute | solution.py:289
  5.0 3.6 %collective-permute-start.2 = (bf16[64,640]{1,0:T(8,128)(2,1)S(1)}, bf16[64,640]{1,0:T(8,128)(2,1)S(1)}, u32[]{:S(2)}, u32[]{:S(2)}) collective-permute-start(bf16[64,640]{1,0:T(8,128)(2,1)S(1)} %get-tuple-element.26), channel_id=1, source_target_pairs={{0,24},{4,28},{8,16},{12,20},{16,8},{20,12},{24,0},{28,4},{1,25},{... | collective-permute-start | bytes 245768 | tf_op jit(solution)/shard_map/ppermute | solution.py:289
  8.6 0.0 collective-permute-start.1
  8.6 0.8 %collective-permute-start = (bf16[64,640]{1,0:T(8,128)(2,1)S(1)}, bf16[64,640]{1,0:T(8,128)(2,1)S(1)}, u32[]{:S(2)}, u32[]{:S(2)}) collective-permute-start(bf16[64,640]{1,0:T(8,128)(2,1)S(1)} %get-tuple-element.26), channel_id=1, source_target_pairs={{0,16},{4,20},{8,24},{12,28},{16,0},{20,4},{24,8},{28,12},{1,17},{... | collective-permute-start | bytes 245768 | tf_op jit(solution)/shard_map/ppermute | solution.py:289
  9.3 0.0 collective-permute-done.4.core_row
  9.3 0.7 %collective-permute-start.5 = (bf16[32,640]{1,0:T(8,128)(2,1)S(1)}, bf16[32,640]{1,0:T(8,128)(2,1)S(1)}, u32[]{:S(2)}, u32[]{:S(2)}) collective-permute-start(bf16[32,640]{1,0:T(8,128)(2,1)S(1)} %get-tuple-element.28), channel_id=1, source_target_pairs={{1,2},{2,1},{5,6},{6,5},{9,10},{10,9},{13,14},{14,13},{17,18},{18,... | collective-permute-start | bytes 122888 | tf_op jit(solution)/shard_map/ppermute | solution.py:299
  10.1 2.9 %shard_map.105 = (f32[256,640]{1,0:T(8,128)S(1)}, bf16[640,640]{1,0:T(8,128)(2,1)S(1)}, bf16[640,640]{1,0:T(8,128)(2,1)S(1)}, bf16[1024,640]{1,0:T(8,128)(2,1)S(1)}) custom-call(bf16[256,640]{1,0:T(8,128)(2,1)S(1)} %bitcast.5, bf16[3,3,640,640]{3,2,1,0:T(8,128)(2,1)S(1)} %copy-done, f32[640]{0:T(1024)S(1)} %copy-done.6, bf16[640,640]{1,0:T(8,128)(2,1)S(1)} %copy-done.1, ...), custom_call_target="tpu_custom_call" | custom-call | flops 1024 | bytes 1024 | tf_op jit(solution)/shard_map/pallas_call | solution.py:22
  13.0 0.0 copy-start.7
  13.0 1.3 %shard_map.106 = (bf16[256,640]{1,0:T(8,128)(2,1)S(1)}, bf16[256,1024]{1,0:T(8,128)(2,1)S(1)}) custom-call(s32[1]{0:T(128)} %bitcast.core, bf16[32,640]{1,0:T(8,128)(2,1)S(1)} %collective-permute-done.4.core_row, bf16[32,640]{1,0:T(8,128)(2,1)S(1)} %collective-permute-done.5.cross_row, f32[256,640]{1,0:T(8,128)S(1)} %get-tuple-element.29.total, ...), custom_call_target="tpu_custom_call" | custom-call | flops 1024 | bytes 1024 | tf_op jit(solution)/shard_map/pallas_call | solution.py:167
  14.3 0.4 %collective-permute-done.1 = bf16[64,640]{1,0:T(8,128)(2,1)S(1)} collective-permute-done((bf16[64,640]{1,0:T(8,128)(2,1)S(1)}, bf16[64,640]{1,0:T(8,128)(2,1)S(1)}, u32[]{:S(2)}, u32[]{:S(2)}) %collective-permute-start.1) | collective-permute-done | bytes 81952 | tf_op jit(solution)/shard_map/ppermute | solution.py:289
  14.7 1.1 %collective-permute-done = bf16[64,640]{1,0:T(8,128)(2,1)S(1)} collective-permute-done((bf16[64,640]{1,0:T(8,128)(2,1)S(1)}, bf16[64,640]{1,0:T(8,128)(2,1)S(1)}, u32[]{:S(2)}, u32[]{:S(2)}) %collective-permute-start) | collective-permute-done | bytes 81952 | tf_op jit(solution)/shard_map/ppermute | solution.py:289
  15.8 1.9 %collective-permute-start.8 = (bf16[256,640]{1,0:T(8,128)(2,1)S(1)}, bf16[256,640]{1,0:T(8,128)(2,1)S(1)}, u32[]{:S(2)}, u32[]{:S(2)}) collective-permute-start(bf16[256,640]{1,0:T(8,128)(2,1)S(1)} %get-tuple-element.31.refs_0_.refs_9_), channel_id=1, source_target_pairs={{0,2},{1,3},{2,0},{3,1},{4,6},{5,7},{6,4},{7,5},{8,10},{9,11},{10,... | collective-permute-start | bytes 983048 | tf_op jit(solution)/shard_map/ppermute | solution.py:289
  17.7 0.6 %collective-permute-start.7 = (bf16[256,640]{1,0:T(8,128)(2,1)S(1)}, bf16[256,640]{1,0:T(8,128)(2,1)S(1)}, u32[]{:S(2)}, u32[]{:S(2)}) collective-permute-start(bf16[256,640]{1,0:T(8,128)(2,1)S(1)} %constant_dynamic-update-slice_fusion.refs_2_), channel_id=1, source_target_pairs={{0,1},{1,0},{2,3},{3,2},{4,5},{5,4},{6,7},{7,6},{8,9},{9,8},{10,11... | collective-permute-start | bytes 983048 | tf_op jit(solution)/shard_map/ppermute | solution.py:289
  18.3 0.6 %collective-permute-start.9 = (bf16[192,640]{1,0:T(8,128)(2,1)S(1)}, bf16[192,640]{1,0:T(8,128)(2,1)S(1)}, u32[]{:S(2)}, u32[]{:S(2)}) collective-permute-start(bf16[192,640]{1,0:T(8,128)(2,1)S(1)} %pad_maximum_fusion), channel_id=1, source_target_pairs={{0,4},{4,0},{8,12},{12,8},{16,20},{20,16},{24,28},{28,24},{1,5},{5... | collective-permute-start | bytes 737288 | tf_op jit(solution)/shard_map/ppermute | solution.py:289
  18.9 0.8 %collective-permute-done.7.refs_3_ = bf16[256,640]{1,0:T(8,128)(2,1)S(1)} collective-permute-done((bf16[256,640]{1,0:T(8,128)(2,1)S(1)}, bf16[256,640]{1,0:T(8,128)(2,1)S(1)}, u32[]{:S(2)}, u32[]{:S(2)}) %collective-permute-start.7) | collective-permute-done | bytes 327712 | tf_op jit(solution)/shard_map/ppermute | solution.py:289
  19.7 4.8 %shard_map.107 = (f32[8,256,128]{2,1,0:T(8,128)S(1)}, f32[8,256,128]{2,1,0:T(8,128)S(1)}) custom-call(bf16[256,640]{1,0:T(8,128)(2,1)S(1)} %get-tuple-element.31.refs_0_.refs_9_, bf16[256,640]{1,0:T(8,128)(2,1)S(1)} %collective-permute-done.6.refs_1_, bf16[256,640]{1,0:T(8,128)(2,1)S(1)} %constant_dynamic-update-slice_fusion.refs_2_, ...), custom_call_target="tpu_custom_call" | custom-call | flops 1024 | bytes 1024 | tf_op jit(solution)/shard_map/pallas_call | solution.py:22
  24.5 1.7 %collective-permute-done.9 = bf16[192,640]{1,0:T(8,128)(2,1)S(1)} collective-permute-done((bf16[192,640]{1,0:T(8,128)(2,1)S(1)}, bf16[192,640]{1,0:T(8,128)(2,1)S(1)}, u32[]{:S(2)}, u32[]{:S(2)}) %collective-permute-start.9) | collective-permute-done | bytes 245792 | tf_op jit(solution)/shard_map/ppermute | solution.py:289
  26.3 0.2 collective-permute-start.11
  26.4 0.4 %collective-permute-start.10 = (bf16[256,640]{1,0:T(8,128)(2,1)S(1)}, bf16[256,640]{1,0:T(8,128)(2,1)S(1)}, u32[]{:S(2)}, u32[]{:S(2)}) collective-permute-start(bf16[256,640]{1,0:T(8,128)(2,1)S(1)} %collective-permute-done.8.refs_0_), channel_id=1, source_target_pairs={{0,1},{1,0},{2,3},{3,2},{4,5},{5,4},{6,7},{7,6},{8,9},{9,8},{10,11... | collective-permute-start | bytes 983048 | tf_op jit(solution)/shard_map/ppermute | solution.py:289
  26.8 2.6 %shard_map.108 = (f32[8,256,128]{2,1,0:T(8,128)S(1)}, f32[8,256,128]{2,1,0:T(8,128)S(1)}) custom-call(bf16[256,640]{1,0:T(8,128)(2,1)S(1)} %collective-permute-done.8.refs_0_, bf16[256,640]{1,0:T(8,128)(2,1)S(1)} %constant_dynamic-update-slice_fusion.4.refs_1_, bf16[640,640]{1,0:T(8,128)(2,1)S(1)} %get-tuple-element.35.refs_4_.refs_2_, ...), custom_call_target="tpu_custom_call" | custom-call | flops 1024 | bytes 1024 | tf_op jit(solution)/shard_map/pallas_call | solution.py:22
  29.5 3.9 %shard_map.109 = (bf16[256,640]{1,0:T(8,128)(2,1)}, bf16[256,640]{1,0:T(8,128)(2,1)}) custom-call(bf16[256,640]{1,0:T(8,128)(2,1)S(1)} %collective-permute-done.10.refs_0_, bf16[256,640]{1,0:T(8,128)(2,1)S(1)} %collective-permute-done.11.refs_1_, bf16[640,640]{1,0:T(8,128)(2,1)S(1)} %get-tuple-element.35.refs_4_.refs_2_, ...), custom_call_target="tpu_custom_call" | custom-call | flops 1024 | bytes 1024 | tf_op jit(solution)/shard_map/pallas_call | solution.py:22
  (29 shorter events, 0.2 us)
Async XLA Ops:
  0.6 9.4 %copy-start = (bf16[3,3,640,640]{3,2,1,0:T(8,128)(2,1)S(1)}, bf16[3,3,640,640]{3,2,1,0:T(8,128)(2,1)}, u32[]{:S(2)}) copy-start(bf16[3,3,640,640]{3,2,1,0:T(8,128)(2,1)} %weight.3) | copy-start | bytes 22118404
  0.7 9.4 %copy-start.1 = (bf16[640,640]{1,0:T(8,128)(2,1)S(1)}, bf16[640,640]{1,0:T(8,128)(2,1)}, u32[]{:S(2)}) copy-start(bf16[640,640]{1,0:T(8,128)(2,1)} %wk.1) | copy-start | bytes 2457604
  0.7 9.4 %copy-start.2 = (bf16[640,640]{1,0:T(8,128)(2,1)S(1)}, bf16[640,640]{1,0:T(8,128)(2,1)}, u32[]{:S(2)}) copy-start(bf16[640,640]{1,0:T(8,128)(2,1)} %wv.1) | copy-start | bytes 2457604
  0.7 9.4 %copy-start.3 = (bf16[640,640]{1,0:T(8,128)(2,1)S(1)}, bf16[640,640]{1,0:T(8,128)(2,1)}, u32[]{:S(2)}) copy-start(bf16[640,640]{1,0:T(8,128)(2,1)} %wo.1) | copy-start | bytes 2457604
  0.7 9.4 %copy-start.5 = (bf16[1,8,32,640]{3,2,1,0:T(8,128)(2,1)S(1)}, bf16[1,8,32,640]{3,2,1,0:T(8,128)(2,1)}, u32[]{:S(2)}) copy-start(bf16[1,8,32,640]{3,2,1,0:T(8,128)(2,1)} %param.9) | copy-start | bytes 983044
  0.7 9.4 %copy-start.6 = (f32[640]{0:T(1024)S(1)}, f32[640]{0:T(1024)}, u32[]{:S(2)}) copy-start(f32[640]{0:T(1024)} %bias.1) | copy-start | bytes 7684
  1.9 11.1 %copy-start.4 = (bf16[640,640]{1,0:T(8,128)(2,1)S(1)}, bf16[640,640]{1,0:T(8,128)(2,1)}, u32[]{:S(2)}) copy-start(bf16[640,640]{1,0:T(8,128)(2,1)} %wq.1) | copy-start | bytes 2457604
  1.9 7.5 %collective-permute-start.4 = (bf16[32,640]{1,0:T(8,128)(2,1)S(1)}, bf16[32,640]{1,0:T(8,128)(2,1)S(1)}, u32[]{:S(2)}, u32[]{:S(2)}) collective-permute-start(bf16[32,640]{1,0:T(8,128)(2,1)S(1)} %get-tuple-element.27), channel_id=1, source_target_pairs={{0,1},{1,0},{2,3},{3,2},{4,5},{5,4},{6,7},{7,6},{8,9},{9,8},{10,11... | collective-permute-start | bytes 122888 | tf_op jit(solution)/shard_map/ppermute | solution.py:289
  2.4 11.9 %collective-permute-start.3 = (bf16[64,640]{1,0:T(8,128)(2,1)S(1)}, bf16[64,640]{1,0:T(8,128)(2,1)S(1)}, u32[]{:S(2)}, u32[]{:S(2)}) collective-permute-start(bf16[64,640]{1,0:T(8,128)(2,1)S(1)} %get-tuple-element.26), channel_id=1, source_target_pairs={{0,4},{4,0},{8,12},{12,8},{16,20},{20,16},{24,28},{28,24},{1,5},{5... | collective-permute-start | bytes 245768 | tf_op jit(solution)/shard_map/ppermute | solution.py:289
  5.0 9.4 %collective-permute-start.2 = (bf16[64,640]{1,0:T(8,128)(2,1)S(1)}, bf16[64,640]{1,0:T(8,128)(2,1)S(1)}, u32[]{:S(2)}, u32[]{:S(2)}) collective-permute-start(bf16[64,640]{1,0:T(8,128)(2,1)S(1)} %get-tuple-element.26), channel_id=1, source_target_pairs={{0,24},{4,28},{8,16},{12,20},{16,8},{20,12},{24,0},{28,4},{1,25},{... | collective-permute-start | bytes 245768 | tf_op jit(solution)/shard_map/ppermute | solution.py:289
  8.6 6.1 %collective-permute-start.1 = (bf16[64,640]{1,0:T(8,128)(2,1)S(1)}, bf16[64,640]{1,0:T(8,128)(2,1)S(1)}, u32[]{:S(2)}, u32[]{:S(2)}) collective-permute-start(bf16[64,640]{1,0:T(8,128)(2,1)S(1)} %get-tuple-element.26), channel_id=1, source_target_pairs={{0,8},{4,12},{8,0},{12,4},{16,24},{20,28},{24,16},{28,20},{1,9},{5... | collective-permute-start | bytes 245768 | tf_op jit(solution)/shard_map/ppermute | solution.py:289
  8.6 7.2 %collective-permute-start = (bf16[64,640]{1,0:T(8,128)(2,1)S(1)}, bf16[64,640]{1,0:T(8,128)(2,1)S(1)}, u32[]{:S(2)}, u32[]{:S(2)}) collective-permute-start(bf16[64,640]{1,0:T(8,128)(2,1)S(1)} %get-tuple-element.26), channel_id=1, source_target_pairs={{0,16},{4,20},{8,24},{12,28},{16,0},{20,4},{24,8},{28,12},{1,17},{... | collective-permute-start | bytes 245768 | tf_op jit(solution)/shard_map/ppermute | solution.py:289
  9.3 3.6 %collective-permute-start.5 = (bf16[32,640]{1,0:T(8,128)(2,1)S(1)}, bf16[32,640]{1,0:T(8,128)(2,1)S(1)}, u32[]{:S(2)}, u32[]{:S(2)}) collective-permute-start(bf16[32,640]{1,0:T(8,128)(2,1)S(1)} %get-tuple-element.28), channel_id=1, source_target_pairs={{1,2},{2,1},{5,6},{6,5},{9,10},{10,9},{13,14},{14,13},{17,18},{18,... | collective-permute-start | bytes 122888 | tf_op jit(solution)/shard_map/ppermute | solution.py:299
  13.0 16.5 %copy-start.7 = (f32[640]{0:T(1024)S(1)}, f32[640]{0:T(1024)}, u32[]{:S(2)}) copy-start(f32[640]{0:T(1024)} %refs_8_.1) | copy-start | bytes 7684
  15.8 10.5 %collective-permute-start.8 = (bf16[256,640]{1,0:T(8,128)(2,1)S(1)}, bf16[256,640]{1,0:T(8,128)(2,1)S(1)}, u32[]{:S(2)}, u32[]{:S(2)}) collective-permute-start(bf16[256,640]{1,0:T(8,128)(2,1)S(1)} %get-tuple-element.31.refs_0_.refs_9_), channel_id=1, source_target_pairs={{0,2},{1,3},{2,0},{3,1},{4,6},{5,7},{6,4},{7,5},{8,10},{9,11},{10,... | collective-permute-start | bytes 983048 | tf_op jit(solution)/shard_map/ppermute | solution.py:289
  17.6 2.1 %collective-permute-start.6 = (bf16[256,640]{1,0:T(8,128)(2,1)S(1)}, bf16[256,640]{1,0:T(8,128)(2,1)S(1)}, u32[]{:S(2)}, u32[]{:S(2)}) collective-permute-start(bf16[256,640]{1,0:T(8,128)(2,1)S(1)} %get-tuple-element.31.refs_0_.refs_9_), channel_id=1, source_target_pairs={{0,1},{1,0},{2,3},{3,2},{4,5},{5,4},{6,7},{7,6},{8,9},{9,8},{10,11... | collective-permute-start | bytes 983048 | tf_op jit(solution)/shard_map/ppermute | solution.py:289
  17.7 2.0 %collective-permute-start.7 = (bf16[256,640]{1,0:T(8,128)(2,1)S(1)}, bf16[256,640]{1,0:T(8,128)(2,1)S(1)}, u32[]{:S(2)}, u32[]{:S(2)}) collective-permute-start(bf16[256,640]{1,0:T(8,128)(2,1)S(1)} %constant_dynamic-update-slice_fusion.refs_2_), channel_id=1, source_target_pairs={{0,1},{1,0},{2,3},{3,2},{4,5},{5,4},{6,7},{7,6},{8,9},{9,8},{10,11... | collective-permute-start | bytes 983048 | tf_op jit(solution)/shard_map/ppermute | solution.py:289
  18.3 7.9 %collective-permute-start.9 = (bf16[192,640]{1,0:T(8,128)(2,1)S(1)}, bf16[192,640]{1,0:T(8,128)(2,1)S(1)}, u32[]{:S(2)}, u32[]{:S(2)}) collective-permute-start(bf16[192,640]{1,0:T(8,128)(2,1)S(1)} %pad_maximum_fusion), channel_id=1, source_target_pairs={{0,4},{4,0},{8,12},{12,8},{16,20},{20,16},{24,28},{28,24},{1,5},{5... | collective-permute-start | bytes 737288 | tf_op jit(solution)/shard_map/ppermute | solution.py:289
  26.3 3.2 %collective-permute-start.11 = (bf16[256,640]{1,0:T(8,128)(2,1)S(1)}, bf16[256,640]{1,0:T(8,128)(2,1)S(1)}, u32[]{:S(2)}, u32[]{:S(2)}) collective-permute-start(bf16[256,640]{1,0:T(8,128)(2,1)S(1)} %constant_dynamic-update-slice_fusion.4.refs_1_), channel_id=1, source_target_pairs={{0,1},{1,0},{2,3},{3,2},{4,5},{5,4},{6,7},{7,6},{8,9},{9,8},{10,11... | collective-permute-start | bytes 983048 | tf_op jit(solution)/shard_map/ppermute | solution.py:289
  26.4 3.0 %collective-permute-start.10 = (bf16[256,640]{1,0:T(8,128)(2,1)S(1)}, bf16[256,640]{1,0:T(8,128)(2,1)S(1)}, u32[]{:S(2)}, u32[]{:S(2)}) collective-permute-start(bf16[256,640]{1,0:T(8,128)(2,1)S(1)} %collective-permute-done.8.refs_0_), channel_id=1, source_target_pairs={{0,1},{1,0},{2,3},{3,2},{4,5},{5,4},{6,7},{7,6},{8,9},{9,8},{10,11... | collective-permute-start | bytes 983048 | tf_op jit(solution)/shard_map/ppermute | solution.py:289

commit v3 on v2

v3 whole, which is shorter than its diff:
```python
import functools

import jax
import jax.numpy as jnp
from jax import lax
from jax.experimental import pallas as pl
from jax.experimental.pallas import tpu as pltpu
from jax.sharding import PartitionSpec as P

HD = 80
LANES = 128
SCALE = HD ** (-0.5) * 1.4426950408889634
BF = jnp.bfloat16
F32 = jnp.float32
VMEM_LIMIT = 24 << 20
LONG = pl.CostEstimate(flops=20 << 30, bytes_accessed=32 << 20, transcendentals=0)
COST = pl.CostEstimate(flops=1 << 10, bytes_accessed=1 << 10, transcendentals=0)


def vmem_call(body, outs, scratch, *operands, place=pltpu.VMEM):
    whole = pl.BlockSpec(memory_space=pltpu.VMEM)
    return pl.pallas_call(
        body,
        out_shape=outs,
        in_specs=[whole] * len(operands),
        out_specs=jax.tree.map(lambda _: pl.BlockSpec(memory_space=place), outs),
        scratch_shapes=scratch,
        cost_estimate=COST,
        compiler_params=pltpu.CompilerParams(vmem_limit_bytes=VMEM_LIMIT),
    )(*operands)


def silu(value):
    value = value.astype(F32)
    return value / (1.0 + jnp.exp(-value))


def shift_columns(active, width):
    rows = active.shape[0]
    column = lax.broadcasted_iota(jnp.int32, active.shape, 0) % width
    left = jnp.where(column == 0, 0.0, pltpu.roll(active, 1, 0))
    right = jnp.where(column == width - 1, 0.0, pltpu.roll(active, rows - 1, 0))
    return left.astype(BF), active.astype(BF), right.astype(BF)


def place():
    row = lax.axis_index("rows")
    return row % 2 == 0, (row > 0) & (row < lax.axis_size("rows") - 1)


def sending_kernel(
    x_in, ref_in, core_out, first_out, own_out, half_out, rows, row_sem, ref_sem
):
    width = core_out.shape[0]
    band = x_in.shape[0]
    copies = [
        pltpu.make_async_copy(x_in.at[:width], rows.at[0], row_sem.at[0]),
        pltpu.make_async_copy(x_in.at[band - width :], rows.at[1], row_sem.at[1]),
        pltpu.make_async_copy(ref_in, own_out, ref_sem),
    ]
    for copy in copies:
        copy.start()
    for copy in copies:
        copy.wait()
    is_first, is_inner = place()
    first, last = rows[0], rows[1]
    core_out[...] = jnp.where(is_first, last, first)
    own = own_out[...]
    half = half_out.shape[0]
    half_out[...] = jnp.where(is_first, own[:half], own[half:])
    first_out[...] = own
    first_out[:width] = jnp.where(is_inner, jnp.where(is_first, first, last), own[:width])


def sending(x, ref, width):
    channels = x.shape[1]
    shape = jax.ShapeDtypeStruct
    near = pl.BlockSpec(memory_space=pltpu.VMEM)
    far = pl.BlockSpec(memory_space=pltpu.HBM)
    return pl.pallas_call(
        sending_kernel,
        out_shape=(
            shape((width, channels), BF),
            shape(ref.shape, BF),
            shape(ref.shape, BF),
            shape((ref.shape[0] // 2, channels), BF),
        ),
        in_specs=[far, far],
        out_specs=(near,) * 4,
        scratch_shapes=[
            pltpu.VMEM((2, width, channels), BF),
            pltpu.SemaphoreType.DMA((2,)),
            pltpu.SemaphoreType.DMA,
        ],
        cost_estimate=LONG,
        compiler_params=pltpu.CompilerParams(vmem_limit_bytes=4 << 20),
    )(*[pltpu.with_memory_space_constraint(v, pltpu.HBM) for v in (x, ref)])


def opening_kernel(width, x, weight, bias, total_out, shifted):
    band, channels = x.shape
    for col, part in enumerate(shift_columns(silu(x[...]), width)):
        shifted[col] = part
    total = x[...].astype(F32) + bias[...][None, :]
    for col in range(3):
        total = total + jnp.dot(shifted[col], weight[1, col], preferred_element_type=F32)
    total_out[...] = total
    for row, source, target in (
        (0, slice(0, band - width), slice(width, band)),
        (2, slice(width, band), slice(0, band - width)),
    ):
        part = total_out[target]
        for col in range(3):
            part = part + jnp.dot(
                shifted[col, source], weight[row, col], preferred_element_type=F32
            )
        total_out[target] = part


def opening(x, weight, bias, width):
    band, channels = x.shape
    return vmem_call(
        functools.partial(opening_kernel, width),
        jax.ShapeDtypeStruct((band, channels), F32),
        [pltpu.VMEM((3, band, channels), BF)],
        x,
        weight,
        bias,
    )


def conv_kernel(
    width, core_row, cross_row, total, weight, hidden_out
):
    band, channels = total.shape
    is_first, is_inner = place()
    core_part = core_row[...]
    cross_part = jnp.where(is_inner, cross_row[:width], jnp.zeros_like(core_part))
    above = shift_columns(silu(jnp.where(is_first, cross_part, core_part)), width)
    below = shift_columns(silu(jnp.where(is_first, core_part, cross_part)), width)
    top, bottom = total[:width], total[band - width :]
    for col in range(3):
        top = top + jnp.dot(above[col], weight[0, col], preferred_element_type=F32)
        bottom = bottom + jnp.dot(below[col], weight[2, col], preferred_element_type=F32)
    hidden_out[width : band - width] = total[width : band - width].astype(BF)
    hidden_out[:width] = top.astype(BF)
    hidden_out[band - width :] = bottom.astype(BF)


def conv(core_row, cross_row, total, weight, width):
    near = pl.BlockSpec(memory_space=pltpu.VMEM)
    return pl.pallas_call(
        functools.partial(conv_kernel, width),
        out_shape=jax.ShapeDtypeStruct(total.shape, BF),
        in_specs=[near] * 4,
        out_specs=near,
        cost_estimate=COST,
        compiler_params=pltpu.CompilerParams(vmem_limit_bytes=VMEM_LIMIT),
    )(core_row, cross_row, total, weight)


def pairing_kernel(first, far_half, own, pair):
    _, is_inner = place()
    block = own.shape[0]
    pair[:block] = jnp.where(is_inner, own[...], first[...])
    pair[block:] = far_half[...]


def pairing(first, far_half, own):
    rows = own.shape[0] + far_half.shape[0]
    shape = jax.ShapeDtypeStruct((rows, own.shape[1]), BF)
    return vmem_call(pairing_kernel, shape, [], first, far_half, own)


def attend_kernel(pieces, first, last, *refs):
    refs = list(refs)
    sources = [refs.pop(0) for _ in range(pieces)]
    wk, wv, query = [refs.pop(0) for _ in range(3)]
    channels = wk.shape[0]
    heads = channels // HD
    if first:
        top_out, sum_out, wk_out, wv_out, query_out, keys, values, column = refs
        own, pair, pair_core = sources[2:]
        _, is_inner = place()
        block = own.shape[0]
        column[:block] = own[...]
        column[block : 2 * block] = jnp.where(is_inner, pair_core[:block], pair[:block])
        middle = 2 * block + pair.shape[0] - block
        column[2 * block : middle] = pair[block:]
        column[middle:] = pair_core[block:]
        sources = sources[:2] + [column]
        wk_out[...] = wk[...].T
        wv_out[...] = wv[...].T
        projected = (
            jnp.dot(sources[0][...], query[...], preferred_element_type=F32) * SCALE
        ).astype(BF)
        query_out[...] = jnp.zeros_like(query_out)
        for head in range(heads):
            query_out[:, head * LANES : head * LANES + HD] = projected[
                :, head * HD : (head + 1) * HD
            ]
        wk, wv, query = wk_out, wv_out, query_out
    else:
        top_in, sum_in = refs.pop(0), refs.pop(0)
        if last:
            wo, bias, hidden, out, hidden_out, keys, values, mixed, out_work, out_sem, hidden_sem = refs
            hidden_copy = pltpu.make_async_copy(hidden, hidden_out, hidden_sem)
            hidden_copy.start()
            mixed[...] = jnp.zeros_like(mixed)
        else:
            top_out, sum_out, keys, values = refs
    band = query.shape[0]
    tokens = keys.shape[1]
    keys[channels:, :] = jnp.zeros((keys.shape[0] - channels, tokens), BF)
    start = 0
    for source in sources:
        part = source[...]
        length = part.shape[0]
        here = slice(start, start + length)
        contract = (((1,), (1,)), ((), ()))
        keys[:channels, here] = lax.dot_general(
            wk[...], part, contract, preferred_element_type=F32
        ).astype(BF)
        value = lax.dot_general(wv[...], part, contract, preferred_element_type=F32).astype(BF)
        for head in range(heads):
            values[head * LANES : head * LANES + HD, here] = value[head * HD : (head + 1) * HD]
            values[head * LANES + HD : (head + 1) * LANES, here] = jnp.ones(
                (LANES - HD, length), BF
            )
        start += length

    def score(head):
        return jnp.dot(
            query[:, head * LANES : (head + 1) * LANES],
            keys[head * HD : head * HD + LANES, :],
            preferred_element_type=F32,
        )

    def weigh(scores, head):
        top = jnp.broadcast_to(jnp.max(scores, axis=1, keepdims=True), (band, LANES))
        if not first:
            top = jnp.maximum(top, top_in[head])
        weights = jnp.concatenate(
            [
                jnp.exp2(scores[:, at : at + LANES] - top).astype(BF)
                for at in range(0, tokens, LANES)
            ],
            axis=1,
        )
        return top, weights

    def finish(head, top, weights):
        product = lax.dot_general(
            weights,
            values[head * LANES : (head + 1) * LANES, :],
            (((1,), (1,)), ((), ())),
            preferred_element_type=F32,
        )
        if not first:
            product = product + sum_in[head] * jnp.exp2(top_in[head] - top)
        if last:
            mixed[:, head * HD : (head + 1) * HD] = (
                product[:, :HD] / product[:, HD : HD + 1]
            ).astype(BF)
        else:
            top_out[head] = top
            sum_out[head] = product

    scores, ready = score(0), None
    for head in range(heads + 1):
        upcoming = score(head + 1) if head + 1 < heads else None
        weighed = weigh(scores, head) if head < heads else None
        if ready is not None:
            finish(head - 1, *ready)
        scores, ready = upcoming, weighed
    if last:
        copies = []
        for i in range(2):
            here = slice(i * band // 2, (i + 1) * band // 2)
            out_work[here, :] = (
                jnp.dot(mixed[here, :], wo[...], preferred_element_type=F32) + bias[...][None, :]
            ).astype(BF)
            copies.append(pltpu.make_async_copy(out_work.at[here], out.at[here], out_sem.at[i]))
            copies[-1].start()
        for copy in copies + [hidden_copy]:
            copy.wait()


def attend(sources, wk, wv, query, state=None, final=None):
    channels = wk.shape[0]
    heads = channels // HD
    band = sources[0].shape[0] if state is None else query.shape[0]
    tokens = sum(source.shape[0] for source in sources)
    if state is None:
        tokens -= sources[2].shape[0]
    shape = jax.ShapeDtypeStruct
    carried = shape((heads, band, LANES), F32)
    square = shape((channels, channels), BF)
    scratch = [
        pltpu.VMEM((channels - HD + LANES, tokens), BF),
        pltpu.VMEM((heads * LANES, tokens), BF),
    ]
    operands = list(sources) + [wk, wv, query] + list(state or ()) + list(final or ())
    place = pltpu.VMEM
    if final is not None:
        outs = (shape((band, channels), BF), shape((band, channels), BF))
        scratch += [
            pltpu.VMEM((band, channels), BF),
            pltpu.VMEM((band, channels), BF),
            pltpu.SemaphoreType.DMA((2,)),
            pltpu.SemaphoreType.DMA,
        ]
        place = pltpu.HBM
    elif state is None:
        scratch.append(pltpu.VMEM((tokens - 2 * band, channels), BF))
        outs = (carried, carried, square, square, shape((band, heads * LANES), BF))
    else:
        outs = (carried, carried)
    return vmem_call(
        functools.partial(attend_kernel, len(sources), state is None, final is not None),
        outs,
        scratch,
        *operands,
        place=place,
    )


def swap(value, axis, bit):
    size = lax.axis_size(axis)
    return lax.ppermute(value, axis, [(i, i ^ bit) for i in range(size)])


def shards(frames, conv_weight, conv_bias, ref_features, w_query, w_key, w_value, w_out, out_bias):
    count, band_rows, width, channels = frames.shape
    band = band_rows * width
    x = frames.reshape(count * band, channels)
    tm, rows = lax.axis_size("tm"), lax.axis_size("rows")
    own = ref_features
    bit = tm // 2
    while bit > 4:
        own = jnp.concatenate([own, swap(own, "tm", bit)])
        bit //= 2
    core_row, first, own, far_half = sending(x, own, width)
    inner = range(1, rows - 1)
    partner = {i: i + 1 if i % 2 else i - 1 for i in inner}
    everyone = [(t, r) for t in range(tm) for r in range(rows)]
    far_half = swap(far_half, "tm", 4)
    first = lax.ppermute(
        first,
        ("tm", "rows"),
        [
            (t * rows + r, t * rows + partner[r] if r in partner else (t ^ 2) * rows + r)
            for t, r in everyone
        ],
    )
    core_row = swap(core_row, "rows", 1)
    total = opening(x, conv_weight, conv_bias, width)
    hidden = conv(core_row, first, total, conv_weight, width)
    pair = pairing(first, far_half, own)
    pair_core = swap(pair, "rows", 1)
    hidden_core = swap(hidden, "rows", 1)
    corner_half = swap(far_half, "tm", 2)
    last_half = swap(far_half, "tm", 3)
    beside = swap(pair, "tm", 1)
    hidden_y = swap(hidden, "rows", 2)
    *state, wk, wv, query = attend(
        [hidden, hidden_core, own, pair, pair_core], w_key, w_value, w_query
    )
    state, hidden_y, beside, corner_half, last_half = lax.optimization_barrier(
        (state, hidden_y, beside, corner_half, last_half)
    )
    across = jnp.concatenate([beside, corner_half])
    hidden_far = swap(hidden_y, "rows", 1)
    across_core = swap(jnp.concatenate([across, last_half]), "rows", 1)
    state = attend([hidden_y, across], wk, wv, query, state)
    attended, hidden = attend(
        [hidden_far, jnp.concatenate([across_core, last_half])],
        wk,
        wv,
        query,
        state,
        (w_out, out_bias, hidden),
    )
    return (
        hidden.reshape(count, band_rows, width, channels),
        attended.reshape(count, band_rows, width, channels),
    )


def solution(mesh):
    return jax.shard_map(
        shards,
        mesh=mesh,
        in_specs=(P("tm", "rows", None, None), P(), P(), P("tm", None), P(), P(), P(), P(), P()),
        out_specs=(P("tm", "rows", None, None), P("tm", "rows", None, None)),
        check_vma=False,
    )
```

time: 33.5 us -> 30.3 us (0.904)
  waiting for transfers between devices: 3.93 us -> 1.25 us
  starting transfers between devices: 11.7 us -> 11.2 us
    ppermute x11 -> x10, starting transfers between devices: 11.1 us -> 8.07 us  [swap(): return lax.ppermute(value, axis, [(i, i ^ bit) for i in range(size)])]
    ppermute x11 -> x10, waiting for transfers between devices: 3.93 us -> 1.24 us  [swap(): return lax.ppermute(value, axis, [(i, i ^ bit) for i in range(size)])]
    ppermute x1, starting transfers between devices: 0.65 us -> 3.09 us  [shards(): lax.ppermute(first, ('tm', 'rows'), [(t * rows + r, t * rows + partner[r]...]
    pallas_call x4 -> x5, Pallas kernels: 14.1 us -> 14.8 us  [vmem_call(): pl.pallas_call(body, out_shape=outs, in_specs=[whole] * len(operands), ou...]
    pallas_call x1, Pallas kernels: 1.32 us -> 0.86 us  [conv(): pl.pallas_call(functools.partial(conv_kernel, width), out_shape=jax.Shape...]
  transfers between devices with their start and end apart: 12 -> 11, of which waited for: 4 -> 1; matrix products, arithmetic and copies ran while one was open for 0% -> 0% of each run, Pallas kernels for 35% -> 36%
where the time goes in v3:
time: 30.3 us; the launch traced here: 30.2 us
  Pallas kernels  16.8 us (55%)
  starting transfers between devices  11.2 us (37%)
  waiting for transfers between devices  1.25 us (4%)
  between operations  0.84 us (3%)
    pallas_call x5, Pallas kernels, vmem_call(): pl.pallas_call(body, out_shape=outs, in_specs=[whole] * len(operands), ou...  14.8 us
    ppermute x10, starting transfers between devices, swap(): return lax.ppermute(value, axis, [(i, i ^ bit) for i in range(size)])  8.07 us
    ppermute x1, starting transfers between devices, shards(): lax.ppermute(first, ('tm', 'rows'), [(t * rows + r, t * rows + partner[r]...  3.09 us
    ppermute x10, waiting for transfers between devices, swap(): return lax.ppermute(value, axis, [(i, i ^ bit) for i in range(size)])  1.24 us
    pallas_call x1, Pallas kernels, sending(): pl.pallas_call(sending_kernel, out_shape=(shape((width, channels), BF), s...  1.16 us
    pallas_call x1, Pallas kernels, conv(): pl.pallas_call(functools.partial(conv_kernel, width), out_shape=jax.Shape...  0.86 us
  transfers between devices with their start and end apart: 11, of which 1 were waited for; matrix products, arithmetic and copies ran while one was open for 0% of the time, Pallas kernels for 36%

profile of v3, /device:TPU:0, one launch (start us, length us, event | category | flops | bytes accessed | tf_op | source)
XLA Modules:
  0.0 30.2 jit_solution(15923684878925132)
XLA Ops:
  0.7 1.2 %shard_map.104 = (bf16[32,640]{1,0:T(8,128)(2,1)S(1)}, bf16[128,640]{1,0:T(8,128)(2,1)S(1)}, bf16[128,640]{1,0:T(8,128)(2,1)S(1)}, bf16[64,640]{1,0:T(8,128)(2,1)S(1)}) custom-call(bf16[256,640]{1,0:T(8,128)(2,1)} %bitcast.3, bf16[128,640]{1,0:T(8,128)(2,1)} %ref_in.1), custom_call_target="tpu_custom_call" | custom-call | flops 21474836480 | bytes 33554432 | tf_op jit(solution)/shard_map/pallas_call | solution.py:80
  1.8 3.1 %collective-permute-start.1 = (bf16[128,640]{1,0:T(8,128)(2,1)S(1)}, bf16[128,640]{1,0:T(8,128)(2,1)S(1)}, u32[]{:S(2)}, u32[]{:S(2)}) collective-permute-start(bf16[128,640]{1,0:T(8,128)(2,1)S(1)} %get-tuple-element.22), channel_id=1, source_target_pairs={{0,8},{1,2},{2,1},{3,11},{4,12},{5,6},{6,5},{7,15},{8,0},{9,10},{1... | collective-permute-start | bytes 491528 | tf_op jit(solution)/shard_map/ppermute | solution.py:348
  4.9 2.6 %collective-permute-start.3 = (bf16[64,640]{1,0:T(8,128)(2,1)S(1)}, bf16[64,640]{1,0:T(8,128)(2,1)S(1)}, u32[]{:S(2)}, u32[]{:S(2)}) collective-permute-start(bf16[64,640]{1,0:T(8,128)(2,1)S(1)} %get-tuple-element.24), channel_id=1, source_target_pairs={{0,16},{4,20},{8,24},{12,28},{16,0},{20,4},{24,8},{28,12},{1,17},{... | collective-permute-start | bytes 245768 | tf_op jit(solution)/shard_map/ppermute | solution.py:330
  7.5 0.0 collective-permute-start
  7.6 2.7 %shard_map.105.total = f32[256,640]{1,0:T(8,128)S(1)} custom-call(bf16[256,640]{1,0:T(8,128)(2,1)S(1)} %bitcast.4, bf16[3,3,640,640]{3,2,1,0:T(8,128)(2,1)S(1)} %copy-done, f32[640]{0:T(1024)S(1)} %copy-done.6), custom_call_target="tpu_custom_call" | custom-call | flops 1024 | bytes 1024 | tf_op jit(solution)/shard_map/pallas_call | solution.py:22
  10.3 0.0 collective-permute-done.core_row
  10.3 0.0 collective-permute-done.1.cross_row.first
  10.3 0.9 %shard_map.106.refs_0_.refs_9_ = bf16[256,640]{1,0:T(8,128)(2,1)S(1)} custom-call(bf16[32,640]{1,0:T(8,128)(2,1)S(1)} %collective-permute-done.core_row, bf16[128,640]{1,0:T(8,128)(2,1)S(1)} %collective-permute-done.1.cross_row.first, f32[256,640]{1,0:T(8,128)S(1)} %shard_map.105.total, bf16[3,3,640,640]{3,2,1,0:T(8,128)(2,1)S(1)} %copy-done), custom_call_target="tpu_custom_call" | custom-call | flops 1024 | bytes 1024 | tf_op jit(solution)/shard_map/pallas_call | solution.py:152
  11.2 0.0 copy-start.4
  11.2 0.0 copy-start.7
  11.2 0.6 %collective-permute-start.2 = (bf16[256,640]{1,0:T(8,128)(2,1)S(1)}, bf16[256,640]{1,0:T(8,128)(2,1)S(1)}, u32[]{:S(2)}, u32[]{:S(2)}) collective-permute-start(bf16[256,640]{1,0:T(8,128)(2,1)S(1)} %shard_map.106.refs_0_.refs_9_), channel_id=1, source_target_pairs={{0,1},{1,0},{2,3},{3,2},{4,5},{5,4},{6,7},{7,6},{8,9},{9,8},{10,11... | collective-permute-start | bytes 983048 | tf_op jit(solution)/shard_map/ppermute | solution.py:330
  11.8 0.0 collective-permute-done.3.far_half
  11.8 0.1 collective-permute-start.4
  11.9 0.8 %collective-permute-start.5 = (bf16[256,640]{1,0:T(8,128)(2,1)S(1)}, bf16[256,640]{1,0:T(8,128)(2,1)S(1)}, u32[]{:S(2)}, u32[]{:S(2)}) collective-permute-start(bf16[256,640]{1,0:T(8,128)(2,1)S(1)} %shard_map.106.refs_0_.refs_9_), channel_id=1, source_target_pairs={{0,2},{1,3},{2,0},{3,1},{4,6},{5,7},{6,4},{7,5},{8,10},{9,11},{10,... | collective-permute-start | bytes 983048 | tf_op jit(solution)/shard_map/ppermute | solution.py:330
  12.7 1.5 %collective-permute-start.6 = (bf16[192,640]{1,0:T(8,128)(2,1)S(1)}, bf16[192,640]{1,0:T(8,128)(2,1)S(1)}, u32[]{:S(2)}, u32[]{:S(2)}) collective-permute-start(bf16[192,640]{1,0:T(8,128)(2,1)S(1)} %shard_map.107.refs_3_), channel_id=1, source_target_pairs={{0,4},{4,0},{8,12},{12,8},{16,20},{20,16},{24,28},{28,24},{1,5},{5... | collective-permute-start | bytes 737288 | tf_op jit(solution)/shard_map/ppermute | solution.py:330
  14.2 0.8 %collective-permute-start.8 = (bf16[64,640]{1,0:T(8,128)(2,1)S(1)}, bf16[64,640]{1,0:T(8,128)(2,1)S(1)}, u32[]{:S(2)}, u32[]{:S(2)}) collective-permute-start(bf16[64,640]{1,0:T(8,128)(2,1)S(1)} %collective-permute-done.3.far_half), channel_id=1, source_target_pairs={{0,12},{4,8},{8,4},{12,0},{16,28},{20,24},{24,20},{28,16},{1,13},{... | collective-permute-start | bytes 245768 | tf_op jit(solution)/shard_map/ppermute | solution.py:330
  15.0 0.0 collective-permute-done.4.refs_4_
  15.0 1.2 %collective-permute-start.7 = (bf16[64,640]{1,0:T(8,128)(2,1)S(1)}, bf16[64,640]{1,0:T(8,128)(2,1)S(1)}, u32[]{:S(2)}, u32[]{:S(2)}) collective-permute-start(bf16[64,640]{1,0:T(8,128)(2,1)S(1)} %collective-permute-done.3.far_half), channel_id=1, source_target_pairs={{0,8},{4,12},{8,0},{12,4},{16,24},{20,28},{24,16},{28,20},{1,9},{5... | collective-permute-start | bytes 245768 | tf_op jit(solution)/shard_map/ppermute | solution.py:330
  16.2 4.7 %shard_map.108 = (f32[8,256,128]{2,1,0:T(8,128)S(1)}, f32[8,256,128]{2,1,0:T(8,128)S(1)}, bf16[640,640]{1,0:T(8,128)(2,1)S(1)}, bf16[640,640]{1,0:T(8,128)(2,1)S(1)}, bf16[256,1024]{1,0:T(8,128)(2,1)S(1)}) custom-call(bf16[256,640]{1,0:T(8,128)(2,1)S(1)} %shard_map.106.refs_0_.refs_9_, bf16[256,640]{1,0:T(8,128)(2,1)S(1)} %collective-permute-done.2.refs_1_, ...), custom_call_target="tpu_custom_call" | custom-call | flops 1024 | bytes 1024 | tf_op jit(solution)/shard_map/pallas_call | solution.py:22
  20.9 1.2 %collective-permute-done.6 = bf16[192,640]{1,0:T(8,128)(2,1)S(1)} collective-permute-done((bf16[192,640]{1,0:T(8,128)(2,1)S(1)}, bf16[192,640]{1,0:T(8,128)(2,1)S(1)}, u32[]{:S(2)}, u32[]{:S(2)}) %collective-permute-start.6) | collective-permute-done | bytes 245792 | tf_op jit(solution)/shard_map/ppermute | solution.py:330
  22.1 0.1 collective-permute-start.10
  22.2 0.5 %collective-permute-start.9 = (bf16[256,640]{1,0:T(8,128)(2,1)S(1)}, bf16[256,640]{1,0:T(8,128)(2,1)S(1)}, u32[]{:S(2)}, u32[]{:S(2)}) collective-permute-start(bf16[256,640]{1,0:T(8,128)(2,1)S(1)} %collective-permute-done.5.refs_0_), channel_id=1, source_target_pairs={{0,1},{1,0},{2,3},{3,2},{4,5},{5,4},{6,7},{7,6},{8,9},{9,8},{10,11... | collective-permute-start | bytes 983048 | tf_op jit(solution)/shard_map/ppermute | solution.py:330
  22.7 2.6 %shard_map.109 = (f32[8,256,128]{2,1,0:T(8,128)S(1)}, f32[8,256,128]{2,1,0:T(8,128)S(1)}) custom-call(bf16[256,640]{1,0:T(8,128)(2,1)S(1)} %collective-permute-done.5.refs_0_, bf16[256,640]{1,0:T(8,128)(2,1)S(1)} %pad_maximum_fusion.2.refs_1_, bf16[640,640]{1,0:T(8,128)(2,1)S(1)} %get-tuple-element.31.refs_2_, ...), custom_call_target="tpu_custom_call" | custom-call | flops 1024 | bytes 1024 | tf_op jit(solution)/shard_map/pallas_call | solution.py:22
  25.4 4.8 %shard_map.110 = (bf16[256,640]{1,0:T(8,128)(2,1)}, bf16[256,640]{1,0:T(8,128)(2,1)}) custom-call(bf16[256,640]{1,0:T(8,128)(2,1)S(1)} %collective-permute-done.9.refs_0_, bf16[384,640]{1,0:T(8,128)(2,1)S(1)} %pad_maximum_fusion.refs_1_, bf16[640,640]{1,0:T(8,128)(2,1)S(1)} %get-tuple-element.31.refs_2_, bf16[640,640]{1,0:T(8,128)(2,1)S(1)} %get-tuple-element.32.refs_3_, ...), custom_call_target="tpu_custom_call" | custom-call | flops 1024 | bytes 1024 | tf_op jit(solution)/shard_map/pallas_call | solution.py:22
  (24 shorter events, 0.2 us)
Async XLA Ops:
  0.6 6.9 %copy-start = (bf16[3,3,640,640]{3,2,1,0:T(8,128)(2,1)S(1)}, bf16[3,3,640,640]{3,2,1,0:T(8,128)(2,1)}, u32[]{:S(2)}) copy-start(bf16[3,3,640,640]{3,2,1,0:T(8,128)(2,1)} %weight.3) | copy-start | bytes 22118404
  0.6 6.9 %copy-start.5 = (bf16[1,8,32,640]{3,2,1,0:T(8,128)(2,1)S(1)}, bf16[1,8,32,640]{3,2,1,0:T(8,128)(2,1)}, u32[]{:S(2)}) copy-start(bf16[1,8,32,640]{3,2,1,0:T(8,128)(2,1)} %param.9) | copy-start | bytes 983044
  0.7 6.9 %copy-start.6 = (f32[640]{0:T(1024)S(1)}, f32[640]{0:T(1024)}, u32[]{:S(2)}) copy-start(f32[640]{0:T(1024)} %bias.1) | copy-start | bytes 7684
  1.8 8.5 %collective-permute-start.1 = (bf16[128,640]{1,0:T(8,128)(2,1)S(1)}, bf16[128,640]{1,0:T(8,128)(2,1)S(1)}, u32[]{:S(2)}, u32[]{:S(2)}) collective-permute-start(bf16[128,640]{1,0:T(8,128)(2,1)S(1)} %get-tuple-element.22), channel_id=1, source_target_pairs={{0,8},{1,2},{2,1},{3,11},{4,12},{5,6},{6,5},{7,15},{8,0},{9,10},{1... | collective-permute-start | bytes 491528 | tf_op jit(solution)/shard_map/ppermute | solution.py:348
  4.9 6.8 %collective-permute-start.3 = (bf16[64,640]{1,0:T(8,128)(2,1)S(1)}, bf16[64,640]{1,0:T(8,128)(2,1)S(1)}, u32[]{:S(2)}, u32[]{:S(2)}) collective-permute-start(bf16[64,640]{1,0:T(8,128)(2,1)S(1)} %get-tuple-element.24), channel_id=1, source_target_pairs={{0,16},{4,20},{8,24},{12,28},{16,0},{20,4},{24,8},{28,12},{1,17},{... | collective-permute-start | bytes 245768 | tf_op jit(solution)/shard_map/ppermute | solution.py:330
  7.5 8.7 %copy-start.1 = (bf16[640,640]{1,0:T(8,128)(2,1)S(1)}, bf16[640,640]{1,0:T(8,128)(2,1)}, u32[]{:S(2)}) copy-start(bf16[640,640]{1,0:T(8,128)(2,1)} %refs_5_.1) | copy-start | bytes 2457604
  7.5 8.7 %copy-start.2 = (bf16[640,640]{1,0:T(8,128)(2,1)S(1)}, bf16[640,640]{1,0:T(8,128)(2,1)}, u32[]{:S(2)}) copy-start(bf16[640,640]{1,0:T(8,128)(2,1)} %refs_6_.1) | copy-start | bytes 2457604
  7.5 8.7 %copy-start.3 = (bf16[640,640]{1,0:T(8,128)(2,1)S(1)}, bf16[640,640]{1,0:T(8,128)(2,1)}, u32[]{:S(2)}) copy-start(bf16[640,640]{1,0:T(8,128)(2,1)} %refs_7_.2) | copy-start | bytes 2457604
  7.5 2.8 %collective-permute-start = (bf16[32,640]{1,0:T(8,128)(2,1)S(1)}, bf16[32,640]{1,0:T(8,128)(2,1)S(1)}, u32[]{:S(2)}, u32[]{:S(2)}) collective-permute-start(bf16[32,640]{1,0:T(8,128)(2,1)S(1)} %get-tuple-element.21), channel_id=1, source_target_pairs={{0,1},{1,0},{2,3},{3,2},{4,5},{5,4},{6,7},{7,6},{8,9},{9,8},{10,11... | collective-permute-start | bytes 122888 | tf_op jit(solution)/shard_map/ppermute | solution.py:330
  11.2 14.2 %copy-start.4 = (bf16[640,640]{1,0:T(8,128)(2,1)S(1)}, bf16[640,640]{1,0:T(8,128)(2,1)}, u32[]{:S(2)}) copy-start(bf16[640,640]{1,0:T(8,128)(2,1)} %refs_7_.3) | copy-start | bytes 2457604
  11.2 14.2 %copy-start.7 = (f32[640]{0:T(1024)S(1)}, f32[640]{0:T(1024)}, u32[]{:S(2)}) copy-start(f32[640]{0:T(1024)} %refs_8_.1) | copy-start | bytes 7684
  11.2 5.0 %collective-permute-start.2 = (bf16[256,640]{1,0:T(8,128)(2,1)S(1)}, bf16[256,640]{1,0:T(8,128)(2,1)S(1)}, u32[]{:S(2)}, u32[]{:S(2)}) collective-permute-start(bf16[256,640]{1,0:T(8,128)(2,1)S(1)} %shard_map.106.refs_0_.refs_9_), channel_id=1, source_target_pairs={{0,1},{1,0},{2,3},{3,2},{4,5},{5,4},{6,7},{7,6},{8,9},{9,8},{10,11... | collective-permute-start | bytes 983048 | tf_op jit(solution)/shard_map/ppermute | solution.py:330
  11.8 3.2 %collective-permute-start.4 = (bf16[192,640]{1,0:T(8,128)(2,1)S(1)}, bf16[192,640]{1,0:T(8,128)(2,1)S(1)}, u32[]{:S(2)}, u32[]{:S(2)}) collective-permute-start(bf16[192,640]{1,0:T(8,128)(2,1)S(1)} %shard_map.107.refs_3_), channel_id=1, source_target_pairs={{0,1},{1,0},{2,3},{3,2},{4,5},{5,4},{6,7},{7,6},{8,9},{9,8},{10,11... | collective-permute-start | bytes 737288 | tf_op jit(solution)/shard_map/ppermute | solution.py:330
  11.9 10.2 %collective-permute-start.5 = (bf16[256,640]{1,0:T(8,128)(2,1)S(1)}, bf16[256,640]{1,0:T(8,128)(2,1)S(1)}, u32[]{:S(2)}, u32[]{:S(2)}) collective-permute-start(bf16[256,640]{1,0:T(8,128)(2,1)S(1)} %shard_map.106.refs_0_.refs_9_), channel_id=1, source_target_pairs={{0,2},{1,3},{2,0},{3,1},{4,6},{5,7},{6,4},{7,5},{8,10},{9,11},{10,... | collective-permute-start | bytes 983048 | tf_op jit(solution)/shard_map/ppermute | solution.py:330
  12.7 9.4 %collective-permute-start.6 = (bf16[192,640]{1,0:T(8,128)(2,1)S(1)}, bf16[192,640]{1,0:T(8,128)(2,1)S(1)}, u32[]{:S(2)}, u32[]{:S(2)}) collective-permute-start(bf16[192,640]{1,0:T(8,128)(2,1)S(1)} %shard_map.107.refs_3_), channel_id=1, source_target_pairs={{0,4},{4,0},{8,12},{12,8},{16,20},{20,16},{24,28},{28,24},{1,5},{5... | collective-permute-start | bytes 737288 | tf_op jit(solution)/shard_map/ppermute | solution.py:330
  14.2 6.7 %collective-permute-start.8 = (bf16[64,640]{1,0:T(8,128)(2,1)S(1)}, bf16[64,640]{1,0:T(8,128)(2,1)S(1)}, u32[]{:S(2)}, u32[]{:S(2)}) collective-permute-start(bf16[64,640]{1,0:T(8,128)(2,1)S(1)} %collective-permute-done.3.far_half), channel_id=1, source_target_pairs={{0,12},{4,8},{8,4},{12,0},{16,28},{20,24},{24,20},{28,16},{1,13},{... | collective-permute-start | bytes 245768 | tf_op jit(solution)/shard_map/ppermute | solution.py:330
  15.0 5.8 %collective-permute-start.7 = (bf16[64,640]{1,0:T(8,128)(2,1)S(1)}, bf16[64,640]{1,0:T(8,128)(2,1)S(1)}, u32[]{:S(2)}, u32[]{:S(2)}) collective-permute-start(bf16[64,640]{1,0:T(8,128)(2,1)S(1)} %collective-permute-done.3.far_half), channel_id=1, source_target_pairs={{0,8},{4,12},{8,0},{12,4},{16,24},{20,28},{24,16},{28,20},{1,9},{5... | collective-permute-start | bytes 245768 | tf_op jit(solution)/shard_map/ppermute | solution.py:330
  22.1 3.2 %collective-permute-start.10 = (bf16[320,640]{1,0:T(8,128)(2,1)S(1)}, bf16[320,640]{1,0:T(8,128)(2,1)S(1)}, u32[]{:S(2)}, u32[]{:S(2)}) collective-permute-start(bf16[320,640]{1,0:T(8,128)(2,1)S(1)} %pad_maximum_fusion.1), channel_id=1, source_target_pairs={{0,1},{1,0},{2,3},{3,2},{4,5},{5,4},{6,7},{7,6},{8,9},{9,8},{10,11... | collective-permute-start | bytes 1228808 | tf_op jit(solution)/shard_map/ppermute | solution.py:330
  22.2 3.2 %collective-permute-start.9 = (bf16[256,640]{1,0:T(8,128)(2,1)S(1)}, bf16[256,640]{1,0:T(8,128)(2,1)S(1)}, u32[]{:S(2)}, u32[]{:S(2)}) collective-permute-start(bf16[256,640]{1,0:T(8,128)(2,1)S(1)} %collective-permute-done.5.refs_0_), channel_id=1, source_target_pairs={{0,1},{1,0},{2,3},{3,2},{4,5},{5,4},{6,7},{7,6},{8,9},{9,8},{10,11... | collective-permute-start | bytes 983048 | tf_op jit(solution)/shard_map/ppermute | solution.py:330

commit v4 on v3

--- a/solution.py
+++ b/solution.py
@@ -179,7 +179,10 @@
     channels = wk.shape[0]
     heads = channels // HD
     if first:
-        top_out, sum_out, wk_out, wv_out, query_out, keys, values, column = refs
+        wo, top_out, sum_out, wk_out, wv_out, query_out, wo_out, keys, values, column = refs
+        wo_out[...] = jnp.zeros_like(wo_out)
+        for head in range(heads):
+            wo_out[head * LANES : head * LANES + HD, :] = wo[head * HD : (head + 1) * HD, :]
         own, pair, pair_core = sources[2:]
         _, is_inner = place()
         block = own.shape[0]
@@ -206,7 +209,6 @@
             wo, bias, hidden, out, hidden_out, keys, values, mixed, out_work, out_sem, hidden_sem = refs
             hidden_copy = pltpu.make_async_copy(hidden, hidden_out, hidden_sem)
             hidden_copy.start()
-            mixed[...] = jnp.zeros_like(mixed)
         else:
             top_out, sum_out, keys, values = refs
     band = query.shape[0]
@@ -259,8 +261,8 @@
         if not first:
             product = product + sum_in[head] * jnp.exp2(top_in[head] - top)
         if last:
-            mixed[:, head * HD : (head + 1) * HD] = (
-                product[:, :HD] / product[:, HD : HD + 1]
+            mixed[:, head * LANES : (head + 1) * LANES] = (
+                product / product[:, HD : HD + 1]
             ).astype(BF)
         else:
             top_out[head] = top
@@ -302,10 +304,10 @@
     ]
     operands = list(sources) + [wk, wv, query] + list(state or ()) + list(final or ())
     place = pltpu.VMEM
-    if final is not None:
+    if state is not None and final is not None:
         outs = (shape((band, channels), BF), shape((band, channels), BF))
         scratch += [
-            pltpu.VMEM((band, channels), BF),
+            pltpu.VMEM((band, heads * LANES), BF),
             pltpu.VMEM((band, channels), BF),
             pltpu.SemaphoreType.DMA((2,)),
             pltpu.SemaphoreType.DMA,
@@ -313,11 +315,20 @@
         place = pltpu.HBM
     elif state is None:
         scratch.append(pltpu.VMEM((tokens - 2 * band, channels), BF))
-        outs = (carried, carried, square, square, shape((band, heads * LANES), BF))
+        outs = (
+            carried,
+            carried,
+            square,
+            square,
+            shape((band, heads * LANES), BF),
+            shape((heads * LANES, channels), BF),
+        )
     else:
         outs = (carried, carried)
     return vmem_call(
-        functools.partial(attend_kernel, len(sources), state is None, final is not None),
+        functools.partial(
+            attend_kernel, len(sources), state is None, state is not None and final is not None
+        ),
         outs,
         scratch,
         *operands,
@@ -363,8 +374,8 @@
     last_half = swap(far_half, "tm", 3)
     beside = swap(pair, "tm", 1)
     hidden_y = swap(hidden, "rows", 2)
-    *state, wk, wv, query = attend(
-        [hidden, hidden_core, own, pair, pair_core], w_key, w_value, w_query
+    *state, wk, wv, query, wo = attend(
+        [hidden, hidden_core, own, pair, pair_core], w_key, w_value, w_query, final=(w_out,)
     )
     state, hidden_y, beside, corner_half, last_half = lax.optimization_barrier(
         (state, hidden_y, beside, corner_half, last_half)
@@ -379,7 +390,7 @@
         wv,
         query,
         state,
-        (w_out, out_bias, hidden),
+        (wo, out_bias, hidden),
     )
     return (
         hidden.reshape(count, band_rows, width, channels),

time: 30.3 us -> 30.1 us (level)
  transfers between devices with their start and end apart: 11 -> 11, of which waited for: 1 -> 1; matrix products, arithmetic and copies ran while one was open for 0% -> 0% of each run, Pallas kernels for 36% -> 37%
where the time goes in v4:
time: 30.1 us; the launch traced here: 30 us
  Pallas kernels  16.7 us (55%)
  starting transfers between devices  11.2 us (37%)
  waiting for transfers between devices  1.06 us (4%)
  between operations  0.84 us (3%)
    pallas_call x5, Pallas kernels, vmem_call(): pl.pallas_call(body, out_shape=outs, in_specs=[whole] * len(operands), ou...  14.7 us
    ppermute x10, starting transfers between devices, swap(): return lax.ppermute(value, axis, [(i, i ^ bit) for i in range(size)])  8.12 us
    ppermute x1, starting transfers between devices, shards(): lax.ppermute(first, ('tm', 'rows'), [(t * rows + r, t * rows + partner[r]...  3.09 us
    pallas_call x1, Pallas kernels, sending(): pl.pallas_call(sending_kernel, out_shape=(shape((width, channels), BF), s...  1.16 us
    ppermute x10, waiting for transfers between devices, swap(): return lax.ppermute(value, axis, [(i, i ^ bit) for i in range(size)])  1.06 us
    pallas_call x1, Pallas kernels, conv(): pl.pallas_call(functools.partial(conv_kernel, width), out_shape=jax.Shape...  0.86 us
  transfers between devices with their start and end apart: 11, of which 1 were waited for; matrix products, arithmetic and copies ran while one was open for 0% of the time, Pallas kernels for 37%

profile of v4, /device:TPU:0, one launch (start us, length us, event | category | flops | bytes accessed | tf_op | source)
XLA Modules:
  0.0 30.0 jit_solution(12136537177011135879)
XLA Ops:
  0.7 1.2 %shard_map.104 = (bf16[32,640]{1,0:T(8,128)(2,1)S(1)}, bf16[128,640]{1,0:T(8,128)(2,1)S(1)}, bf16[128,640]{1,0:T(8,128)(2,1)S(1)}, bf16[64,640]{1,0:T(8,128)(2,1)S(1)}) custom-call(bf16[256,640]{1,0:T(8,128)(2,1)} %bitcast.3, bf16[128,640]{1,0:T(8,128)(2,1)} %ref_in.1), custom_call_target="tpu_custom_call" | custom-call | flops 21474836480 | bytes 33554432 | tf_op jit(solution)/shard_map/pallas_call | solution.py:80
  1.8 3.1 %collective-permute-start.1 = (bf16[128,640]{1,0:T(8,128)(2,1)S(1)}, bf16[128,640]{1,0:T(8,128)(2,1)S(1)}, u32[]{:S(2)}, u32[]{:S(2)}) collective-permute-start(bf16[128,640]{1,0:T(8,128)(2,1)S(1)} %get-tuple-element.23), channel_id=1, source_target_pairs={{0,8},{1,2},{2,1},{3,11},{4,12},{5,6},{6,5},{7,15},{8,0},{9,10},{1... | collective-permute-start | bytes 491528 | tf_op jit(solution)/shard_map/ppermute | solution.py:359
  4.9 2.6 %collective-permute-start.3 = (bf16[64,640]{1,0:T(8,128)(2,1)S(1)}, bf16[64,640]{1,0:T(8,128)(2,1)S(1)}, u32[]{:S(2)}, u32[]{:S(2)}) collective-permute-start(bf16[64,640]{1,0:T(8,128)(2,1)S(1)} %get-tuple-element.25), channel_id=1, source_target_pairs={{0,16},{4,20},{8,24},{12,28},{16,0},{20,4},{24,8},{28,12},{1,17},{... | collective-permute-start | bytes 245768 | tf_op jit(solution)/shard_map/ppermute | solution.py:341
  7.5 0.1 collective-permute-start
  7.6 2.7 %shard_map.105.total = f32[256,640]{1,0:T(8,128)S(1)} custom-call(bf16[256,640]{1,0:T(8,128)(2,1)S(1)} %bitcast.4, bf16[3,3,640,640]{3,2,1,0:T(8,128)(2,1)S(1)} %copy-done, f32[640]{0:T(1024)S(1)} %copy-done.6), custom_call_target="tpu_custom_call" | custom-call | flops 1024 | bytes 1024 | tf_op jit(solution)/shard_map/pallas_call | solution.py:22
  10.4 0.0 collective-permute-done.core_row
  10.4 0.9 %shard_map.106.refs_0_.refs_9_ = bf16[256,640]{1,0:T(8,128)(2,1)S(1)} custom-call(bf16[32,640]{1,0:T(8,128)(2,1)S(1)} %collective-permute-done.core_row, bf16[128,640]{1,0:T(8,128)(2,1)S(1)} %collective-permute-done.1.cross_row.first, f32[256,640]{1,0:T(8,128)S(1)} %shard_map.105.total, bf16[3,3,640,640]{3,2,1,0:T(8,128)(2,1)S(1)} %copy-done), custom_call_target="tpu_custom_call" | custom-call | flops 1024 | bytes 1024 | tf_op jit(solution)/shard_map/pallas_call | solution.py:152
  11.2 0.0 copy-start.7
  11.3 0.5 %collective-permute-start.2 = (bf16[256,640]{1,0:T(8,128)(2,1)S(1)}, bf16[256,640]{1,0:T(8,128)(2,1)S(1)}, u32[]{:S(2)}, u32[]{:S(2)}) collective-permute-start(bf16[256,640]{1,0:T(8,128)(2,1)S(1)} %shard_map.106.refs_0_.refs_9_), channel_id=1, source_target_pairs={{0,1},{1,0},{2,3},{3,2},{4,5},{5,4},{6,7},{7,6},{8,9},{9,8},{10,11... | collective-permute-start | bytes 983048 | tf_op jit(solution)/shard_map/ppermute | solution.py:341
  11.8 0.0 collective-permute-done.3.far_half
  11.8 0.1 collective-permute-start.4
  11.9 0.8 %collective-permute-start.5 = (bf16[256,640]{1,0:T(8,128)(2,1)S(1)}, bf16[256,640]{1,0:T(8,128)(2,1)S(1)}, u32[]{:S(2)}, u32[]{:S(2)}) collective-permute-start(bf16[256,640]{1,0:T(8,128)(2,1)S(1)} %shard_map.106.refs_0_.refs_9_), channel_id=1, source_target_pairs={{0,2},{1,3},{2,0},{3,1},{4,6},{5,7},{6,4},{7,5},{8,10},{9,11},{10,... | collective-permute-start | bytes 983048 | tf_op jit(solution)/shard_map/ppermute | solution.py:341
  12.7 1.5 %collective-permute-start.6 = (bf16[192,640]{1,0:T(8,128)(2,1)S(1)}, bf16[192,640]{1,0:T(8,128)(2,1)S(1)}, u32[]{:S(2)}, u32[]{:S(2)}) collective-permute-start(bf16[192,640]{1,0:T(8,128)(2,1)S(1)} %shard_map.107.refs_3_), channel_id=1, source_target_pairs={{0,4},{4,0},{8,12},{12,8},{16,20},{20,16},{24,28},{28,24},{1,5},{5... | collective-permute-start | bytes 737288 | tf_op jit(solution)/shard_map/ppermute | solution.py:341
  14.2 0.9 %collective-permute-start.8 = (bf16[64,640]{1,0:T(8,128)(2,1)S(1)}, bf16[64,640]{1,0:T(8,128)(2,1)S(1)}, u32[]{:S(2)}, u32[]{:S(2)}) collective-permute-start(bf16[64,640]{1,0:T(8,128)(2,1)S(1)} %collective-permute-done.3.far_half), channel_id=1, source_target_pairs={{0,12},{4,8},{8,4},{12,0},{16,28},{20,24},{24,20},{28,16},{1,13},{... | collective-permute-start | bytes 245768 | tf_op jit(solution)/shard_map/ppermute | solution.py:341
  15.1 1.1 %collective-permute-start.7 = (bf16[64,640]{1,0:T(8,128)(2,1)S(1)}, bf16[64,640]{1,0:T(8,128)(2,1)S(1)}, u32[]{:S(2)}, u32[]{:S(2)}) collective-permute-start(bf16[64,640]{1,0:T(8,128)(2,1)S(1)} %collective-permute-done.3.far_half), channel_id=1, source_target_pairs={{0,8},{4,12},{8,0},{12,4},{16,24},{20,28},{24,16},{28,20},{1,9},{5... | collective-permute-start | bytes 245768 | tf_op jit(solution)/shard_map/ppermute | solution.py:341
  16.2 4.8 %shard_map.108 = (f32[8,256,128]{2,1,0:T(8,128)S(1)}, f32[8,256,128]{2,1,0:T(8,128)S(1)}, bf16[640,640]{1,0:T(8,128)(2,1)S(1)}, bf16[640,640]{1,0:T(8,128)(2,1)S...) custom-call(bf16[256,640]{1,0:T(8,128)(2,1)S(1)} %shard_map.106.refs_0_.refs_9_, ...), custom_call_target="tpu_custom_call" | custom-call | flops 1024 | bytes 1024 | tf_op jit(solution)/shard_map/pallas_call | solution.py:22
  21.1 0.0 collective-permute-done.8
  21.1 1.0 %collective-permute-done.6 = bf16[192,640]{1,0:T(8,128)(2,1)S(1)} collective-permute-done((bf16[192,640]{1,0:T(8,128)(2,1)S(1)}, bf16[192,640]{1,0:T(8,128)(2,1)S(1)}, u32[]{:S(2)}, u32[]{:S(2)}) %collective-permute-start.6) | collective-permute-done | bytes 245792 | tf_op jit(solution)/shard_map/ppermute | solution.py:341
  22.2 0.1 collective-permute-start.10
  22.2 0.5 %collective-permute-start.9 = (bf16[256,640]{1,0:T(8,128)(2,1)S(1)}, bf16[256,640]{1,0:T(8,128)(2,1)S(1)}, u32[]{:S(2)}, u32[]{:S(2)}) collective-permute-start(bf16[256,640]{1,0:T(8,128)(2,1)S(1)} %collective-permute-done.5.refs_0_), channel_id=1, source_target_pairs={{0,1},{1,0},{2,3},{3,2},{4,5},{5,4},{6,7},{7,6},{8,9},{9,8},{10,11... | collective-permute-start | bytes 983048 | tf_op jit(solution)/shard_map/ppermute | solution.py:341
  22.8 2.6 %shard_map.109 = (f32[8,256,128]{2,1,0:T(8,128)S(1)}, f32[8,256,128]{2,1,0:T(8,128)S(1)}) custom-call(bf16[256,640]{1,0:T(8,128)(2,1)S(1)} %collective-permute-done.5.refs_0_, bf16[256,640]{1,0:T(8,128)(2,1)S(1)} %pad_maximum_fusion.2.refs_1_, bf16[640,640]{1,0:T(8,128)(2,1)S(1)} %get-tuple-element.32.refs_2_, ...), custom_call_target="tpu_custom_call" | custom-call | flops 1024 | bytes 1024 | tf_op jit(solution)/shard_map/pallas_call | solution.py:22
  25.3 0.0 collective-permute-done.10
  25.4 0.0 collective-permute-done.9.refs_0_
  25.4 4.5 %shard_map.110 = (bf16[256,640]{1,0:T(8,128)(2,1)}, bf16[256,640]{1,0:T(8,128)(2,1)}) custom-call(bf16[256,640]{1,0:T(8,128)(2,1)S(1)} %collective-permute-done.9.refs_0_, bf16[384,640]{1,0:T(8,128)(2,1)S(1)} %pad_maximum_fusion.refs_1_, bf16[640,640]{1,0:T(8,128)(2,1)S(1)} %get-tuple-element.32.refs_2_, bf16[640,640]{1,0:T(8,128)(2,1)S(1)} %get-tuple-element.33.refs_3_, ...), custom_call_target="tpu_custom_call" | custom-call | flops 1024 | bytes 1024 | tf_op jit(solution)/shard_map/pallas_call | solution.py:22
  (24 shorter events, 0.2 us)
Async XLA Ops:
  0.6 7.0 %copy-start = (bf16[3,3,640,640]{3,2,1,0:T(8,128)(2,1)S(1)}, bf16[3,3,640,640]{3,2,1,0:T(8,128)(2,1)}, u32[]{:S(2)}) copy-start(bf16[3,3,640,640]{3,2,1,0:T(8,128)(2,1)} %weight.3) | copy-start | bytes 22118404
  0.6 7.0 %copy-start.5 = (bf16[1,8,32,640]{3,2,1,0:T(8,128)(2,1)S(1)}, bf16[1,8,32,640]{3,2,1,0:T(8,128)(2,1)}, u32[]{:S(2)}) copy-start(bf16[1,8,32,640]{3,2,1,0:T(8,128)(2,1)} %param.9) | copy-start | bytes 983044
  0.7 7.0 %copy-start.6 = (f32[640]{0:T(1024)S(1)}, f32[640]{0:T(1024)}, u32[]{:S(2)}) copy-start(f32[640]{0:T(1024)} %bias.1) | copy-start | bytes 7684
  1.8 8.5 %collective-permute-start.1 = (bf16[128,640]{1,0:T(8,128)(2,1)S(1)}, bf16[128,640]{1,0:T(8,128)(2,1)S(1)}, u32[]{:S(2)}, u32[]{:S(2)}) collective-permute-start(bf16[128,640]{1,0:T(8,128)(2,1)S(1)} %get-tuple-element.23), channel_id=1, source_target_pairs={{0,8},{1,2},{2,1},{3,11},{4,12},{5,6},{6,5},{7,15},{8,0},{9,10},{1... | collective-permute-start | bytes 491528 | tf_op jit(solution)/shard_map/ppermute | solution.py:359
  4.9 6.9 %collective-permute-start.3 = (bf16[64,640]{1,0:T(8,128)(2,1)S(1)}, bf16[64,640]{1,0:T(8,128)(2,1)S(1)}, u32[]{:S(2)}, u32[]{:S(2)}) collective-permute-start(bf16[64,640]{1,0:T(8,128)(2,1)S(1)} %get-tuple-element.25), channel_id=1, source_target_pairs={{0,16},{4,20},{8,24},{12,28},{16,0},{20,4},{24,8},{28,12},{1,17},{... | collective-permute-start | bytes 245768 | tf_op jit(solution)/shard_map/ppermute | solution.py:341
  7.5 8.7 %copy-start.1 = (bf16[640,640]{1,0:T(8,128)(2,1)S(1)}, bf16[640,640]{1,0:T(8,128)(2,1)}, u32[]{:S(2)}) copy-start(bf16[640,640]{1,0:T(8,128)(2,1)} %refs_5_.1) | copy-start | bytes 2457604
  7.5 8.7 %copy-start.2 = (bf16[640,640]{1,0:T(8,128)(2,1)S(1)}, bf16[640,640]{1,0:T(8,128)(2,1)}, u32[]{:S(2)}) copy-start(bf16[640,640]{1,0:T(8,128)(2,1)} %refs_6_.1) | copy-start | bytes 2457604
  7.5 8.7 %copy-start.3 = (bf16[640,640]{1,0:T(8,128)(2,1)S(1)}, bf16[640,640]{1,0:T(8,128)(2,1)}, u32[]{:S(2)}) copy-start(bf16[640,640]{1,0:T(8,128)(2,1)} %refs_7_.1) | copy-start | bytes 2457604
  7.5 8.7 %copy-start.4 = (bf16[640,640]{1,0:T(8,128)(2,1)S(1)}, bf16[640,640]{1,0:T(8,128)(2,1)}, u32[]{:S(2)}) copy-start(bf16[640,640]{1,0:T(8,128)(2,1)} %refs_8_.2) | copy-start | bytes 2457604
  7.5 2.8 %collective-permute-start = (bf16[32,640]{1,0:T(8,128)(2,1)S(1)}, bf16[32,640]{1,0:T(8,128)(2,1)S(1)}, u32[]{:S(2)}, u32[]{:S(2)}) collective-permute-start(bf16[32,640]{1,0:T(8,128)(2,1)S(1)} %get-tuple-element.22), channel_id=1, source_target_pairs={{0,1},{1,0},{2,3},{3,2},{4,5},{5,4},{6,7},{7,6},{8,9},{9,8},{10,11... | collective-permute-start | bytes 122888 | tf_op jit(solution)/shard_map/ppermute | solution.py:341
  11.2 14.2 %copy-start.7 = (f32[640]{0:T(1024)S(1)}, f32[640]{0:T(1024)}, u32[]{:S(2)}) copy-start(f32[640]{0:T(1024)} %refs_8_.3) | copy-start | bytes 7684
  11.3 4.9 %collective-permute-start.2 = (bf16[256,640]{1,0:T(8,128)(2,1)S(1)}, bf16[256,640]{1,0:T(8,128)(2,1)S(1)}, u32[]{:S(2)}, u32[]{:S(2)}) collective-permute-start(bf16[256,640]{1,0:T(8,128)(2,1)S(1)} %shard_map.106.refs_0_.refs_9_), channel_id=1, source_target_pairs={{0,1},{1,0},{2,3},{3,2},{4,5},{5,4},{6,7},{7,6},{8,9},{9,8},{10,11... | collective-permute-start | bytes 983048 | tf_op jit(solution)/shard_map/ppermute | solution.py:341
  11.8 3.2 %collective-permute-start.4 = (bf16[192,640]{1,0:T(8,128)(2,1)S(1)}, bf16[192,640]{1,0:T(8,128)(2,1)S(1)}, u32[]{:S(2)}, u32[]{:S(2)}) collective-permute-start(bf16[192,640]{1,0:T(8,128)(2,1)S(1)} %shard_map.107.refs_3_), channel_id=1, source_target_pairs={{0,1},{1,0},{2,3},{3,2},{4,5},{5,4},{6,7},{7,6},{8,9},{9,8},{10,11... | collective-permute-start | bytes 737288 | tf_op jit(solution)/shard_map/ppermute | solution.py:341
  11.9 10.2 %collective-permute-start.5 = (bf16[256,640]{1,0:T(8,128)(2,1)S(1)}, bf16[256,640]{1,0:T(8,128)(2,1)S(1)}, u32[]{:S(2)}, u32[]{:S(2)}) collective-permute-start(bf16[256,640]{1,0:T(8,128)(2,1)S(1)} %shard_map.106.refs_0_.refs_9_), channel_id=1, source_target_pairs={{0,2},{1,3},{2,0},{3,1},{4,6},{5,7},{6,4},{7,5},{8,10},{9,11},{10,... | collective-permute-start | bytes 983048 | tf_op jit(solution)/shard_map/ppermute | solution.py:341
  12.7 9.4 %collective-permute-start.6 = (bf16[192,640]{1,0:T(8,128)(2,1)S(1)}, bf16[192,640]{1,0:T(8,128)(2,1)S(1)}, u32[]{:S(2)}, u32[]{:S(2)}) collective-permute-start(bf16[192,640]{1,0:T(8,128)(2,1)S(1)} %shard_map.107.refs_3_), channel_id=1, source_target_pairs={{0,4},{4,0},{8,12},{12,8},{16,20},{20,16},{24,28},{28,24},{1,5},{5... | collective-permute-start | bytes 737288 | tf_op jit(solution)/shard_map/ppermute | solution.py:341
  14.2 6.9 %collective-permute-start.8 = (bf16[64,640]{1,0:T(8,128)(2,1)S(1)}, bf16[64,640]{1,0:T(8,128)(2,1)S(1)}, u32[]{:S(2)}, u32[]{:S(2)}) collective-permute-start(bf16[64,640]{1,0:T(8,128)(2,1)S(1)} %collective-permute-done.3.far_half), channel_id=1, source_target_pairs={{0,12},{4,8},{8,4},{12,0},{16,28},{20,24},{24,20},{28,16},{1,13},{... | collective-permute-start | bytes 245768 | tf_op jit(solution)/shard_map/ppermute | solution.py:341
  15.1 6.0 %collective-permute-start.7 = (bf16[64,640]{1,0:T(8,128)(2,1)S(1)}, bf16[64,640]{1,0:T(8,128)(2,1)S(1)}, u32[]{:S(2)}, u32[]{:S(2)}) collective-permute-start(bf16[64,640]{1,0:T(8,128)(2,1)S(1)} %collective-permute-done.3.far_half), channel_id=1, source_target_pairs={{0,8},{4,12},{8,0},{12,4},{16,24},{20,28},{24,16},{28,20},{1,9},{5... | collective-permute-start | bytes 245768 | tf_op jit(solution)/shard_map/ppermute | solution.py:341
  22.2 3.2 %collective-permute-start.10 = (bf16[320,640]{1,0:T(8,128)(2,1)S(1)}, bf16[320,640]{1,0:T(8,128)(2,1)S(1)}, u32[]{:S(2)}, u32[]{:S(2)}) collective-permute-start(bf16[320,640]{1,0:T(8,128)(2,1)S(1)} %pad_maximum_fusion.1), channel_id=1, source_target_pairs={{0,1},{1,0},{2,3},{3,2},{4,5},{5,4},{6,7},{7,6},{8,9},{9,8},{10,11... | collective-permute-start | bytes 1228808 | tf_op jit(solution)/shard_map/ppermute | solution.py:341
  22.2 3.2 %collective-permute-start.9 = (bf16[256,640]{1,0:T(8,128)(2,1)S(1)}, bf16[256,640]{1,0:T(8,128)(2,1)S(1)}, u32[]{:S(2)}, u32[]{:S(2)}) collective-permute-start(bf16[256,640]{1,0:T(8,128)(2,1)S(1)} %collective-permute-done.5.refs_0_), channel_id=1, source_target_pairs={{0,1},{1,0},{2,3},{3,2},{4,5},{5,4},{6,7},{7,6},{8,9},{9,8},{10,11... | collective-permute-start | bytes 983048 | tf_op jit(solution)/shard_map/ppermute | solution.py:341

commit v5 on v4

--- a/solution.py
+++ b/solution.py
@@ -100,21 +100,21 @@
 def opening_kernel(width, x, weight, bias, total_out, shifted):
     band, channels = x.shape
     for col, part in enumerate(shift_columns(silu(x[...]), width)):
-        shifted[col] = part
-    total = x[...].astype(F32) + bias[...][None, :]
-    for col in range(3):
-        total = total + jnp.dot(shifted[col], weight[1, col], preferred_element_type=F32)
-    total_out[...] = total
-    for row, source, target in (
-        (0, slice(0, band - width), slice(width, band)),
-        (2, slice(width, band), slice(0, band - width)),
-    ):
-        part = total_out[target]
-        for col in range(3):
-            part = part + jnp.dot(
-                shifted[col, source], weight[row, col], preferred_element_type=F32
-            )
-        total_out[target] = part
+        shifted[:, col * channels : (col + 1) * channels] = part
+    taps = 3 * channels
+    total_out[...] = (
+        x[...].astype(F32)
+        + bias[...][None, :]
+        + jnp.dot(shifted[...], weight[1].reshape(taps, channels), preferred_element_type=F32)
+    )
+    total_out[width:, :] += jnp.dot(
+        shifted[: band - width, :],
+        weight[0].reshape(taps, channels),
+        preferred_element_type=F32,
+    )
+    total_out[: band - width, :] += jnp.dot(
+        shifted[width:, :], weight[2].reshape(taps, channels), preferred_element_type=F32
+    )
 
 
 def opening(x, weight, bias, width):
@@ -122,7 +122,7 @@
     return vmem_call(
         functools.partial(opening_kernel, width),
         jax.ShapeDtypeStruct((band, channels), F32),
-        [pltpu.VMEM((3, band, channels), BF)],
+        [pltpu.VMEM((band, 3 * channels), BF)],
         x,
         weight,
         bias,

time: 30.1 us -> 29.9 us (level)
  transfers between devices with their start and end apart: 11 -> 11, of which waited for: 1 -> 1; matrix products, arithmetic and copies ran while one was open for 0% -> 0% of each run, Pallas kernels for 37% -> 36%
where the time goes in v5:
time: 29.9 us; the launch traced here: 29.7 us
  Pallas kernels  16.5 us (55%)
  starting transfers between devices  11.2 us (37%)
  waiting for transfers between devices  1.07 us (4%)
  between operations  0.84 us (3%)
    pallas_call x5, Pallas kernels, vmem_call(): pl.pallas_call(body, out_shape=outs, in_specs=[whole] * len(operands), ou...  14.5 us
    ppermute x10, starting transfers between devices, swap(): return lax.ppermute(value, axis, [(i, i ^ bit) for i in range(size)])  8.12 us
    ppermute x1, starting transfers between devices, shards(): lax.ppermute(first, ('tm', 'rows'), [(t * rows + r, t * rows + partner[r]...  3.09 us
    pallas_call x1, Pallas kernels, sending(): pl.pallas_call(sending_kernel, out_shape=(shape((width, channels), BF), s...  1.16 us
    ppermute x10, waiting for transfers between devices, swap(): return lax.ppermute(value, axis, [(i, i ^ bit) for i in range(size)])  1.07 us
    pallas_call x1, Pallas kernels, conv(): pl.pallas_call(functools.partial(conv_kernel, width), out_shape=jax.Shape...  0.85 us
  transfers between devices with their start and end apart: 11, of which 1 were waited for; matrix products, arithmetic and copies ran while one was open for 0% of the time, Pallas kernels for 36%

profile of v5, /device:TPU:0, one launch (start us, length us, event | category | flops | bytes accessed | tf_op | source)
XLA Modules:
  0.0 29.7 jit_solution(6627994893681762172)
XLA Ops:
  0.7 1.2 %shard_map.104 = (bf16[32,640]{1,0:T(8,128)(2,1)S(1)}, bf16[128,640]{1,0:T(8,128)(2,1)S(1)}, bf16[128,640]{1,0:T(8,128)(2,1)S(1)}, bf16[64,640]{1,0:T(8,128)(2,1)S(1)}) custom-call(bf16[256,640]{1,0:T(8,128)(2,1)} %bitcast.3, bf16[128,640]{1,0:T(8,128)(2,1)} %ref_in.1), custom_call_target="tpu_custom_call" | custom-call | flops 21474836480 | bytes 33554432 | tf_op jit(solution)/shard_map/pallas_call | solution.py:80
  1.8 3.1 %collective-permute-start.1 = (bf16[128,640]{1,0:T(8,128)(2,1)S(1)}, bf16[128,640]{1,0:T(8,128)(2,1)S(1)}, u32[]{:S(2)}, u32[]{:S(2)}) collective-permute-start(bf16[128,640]{1,0:T(8,128)(2,1)S(1)} %get-tuple-element.23), channel_id=1, source_target_pairs={{0,8},{1,2},{2,1},{3,11},{4,12},{5,6},{6,5},{7,15},{8,0},{9,10},{1... | collective-permute-start | bytes 491528 | tf_op jit(solution)/shard_map/ppermute | solution.py:359
  4.9 2.6 %collective-permute-start.3 = (bf16[64,640]{1,0:T(8,128)(2,1)S(1)}, bf16[64,640]{1,0:T(8,128)(2,1)S(1)}, u32[]{:S(2)}, u32[]{:S(2)}) collective-permute-start(bf16[64,640]{1,0:T(8,128)(2,1)S(1)} %get-tuple-element.25), channel_id=1, source_target_pairs={{0,16},{4,20},{8,24},{12,28},{16,0},{20,4},{24,8},{28,12},{1,17},{... | collective-permute-start | bytes 245768 | tf_op jit(solution)/shard_map/ppermute | solution.py:341
  7.5 0.1 collective-permute-start
  7.6 2.5 %shard_map.105.total = f32[256,640]{1,0:T(8,128)S(1)} custom-call(bf16[256,640]{1,0:T(8,128)(2,1)S(1)} %bitcast.4, bf16[3,3,640,640]{3,2,1,0:T(8,128)(2,1)S(1)} %copy-done, f32[640]{0:T(1024)S(1)} %copy-done.6), custom_call_target="tpu_custom_call" | custom-call | flops 1024 | bytes 1024 | tf_op jit(solution)/shard_map/pallas_call | solution.py:22
  10.2 0.0 collective-permute-done.1.cross_row.first
  10.2 0.9 %shard_map.106.refs_0_.refs_9_ = bf16[256,640]{1,0:T(8,128)(2,1)S(1)} custom-call(bf16[32,640]{1,0:T(8,128)(2,1)S(1)} %collective-permute-done.core_row, bf16[128,640]{1,0:T(8,128)(2,1)S(1)} %collective-permute-done.1.cross_row.first, f32[256,640]{1,0:T(8,128)S(1)} %shard_map.105.total, bf16[3,3,640,640]{3,2,1,0:T(8,128)(2,1)S(1)} %copy-done), custom_call_target="tpu_custom_call" | custom-call | flops 1024 | bytes 1024 | tf_op jit(solution)/shard_map/pallas_call | solution.py:152
  11.0 0.0 copy-start.7
  11.0 0.5 %collective-permute-start.2 = (bf16[256,640]{1,0:T(8,128)(2,1)S(1)}, bf16[256,640]{1,0:T(8,128)(2,1)S(1)}, u32[]{:S(2)}, u32[]{:S(2)}) collective-permute-start(bf16[256,640]{1,0:T(8,128)(2,1)S(1)} %shard_map.106.refs_0_.refs_9_), channel_id=1, source_target_pairs={{0,1},{1,0},{2,3},{3,2},{4,5},{5,4},{6,7},{7,6},{8,9},{9,8},{10,11... | collective-permute-start | bytes 983048 | tf_op jit(solution)/shard_map/ppermute | solution.py:341
  11.6 0.0 collective-permute-done.3.far_half
  11.6 0.1 collective-permute-start.4
  11.7 0.8 %collective-permute-start.5 = (bf16[256,640]{1,0:T(8,128)(2,1)S(1)}, bf16[256,640]{1,0:T(8,128)(2,1)S(1)}, u32[]{:S(2)}, u32[]{:S(2)}) collective-permute-start(bf16[256,640]{1,0:T(8,128)(2,1)S(1)} %shard_map.106.refs_0_.refs_9_), channel_id=1, source_target_pairs={{0,2},{1,3},{2,0},{3,1},{4,6},{5,7},{6,4},{7,5},{8,10},{9,11},{10,... | collective-permute-start | bytes 983048 | tf_op jit(solution)/shard_map/ppermute | solution.py:341
  12.5 1.5 %collective-permute-start.6 = (bf16[192,640]{1,0:T(8,128)(2,1)S(1)}, bf16[192,640]{1,0:T(8,128)(2,1)S(1)}, u32[]{:S(2)}, u32[]{:S(2)}) collective-permute-start(bf16[192,640]{1,0:T(8,128)(2,1)S(1)} %shard_map.107.refs_3_), channel_id=1, source_target_pairs={{0,4},{4,0},{8,12},{12,8},{16,20},{20,16},{24,28},{28,24},{1,5},{5... | collective-permute-start | bytes 737288 | tf_op jit(solution)/shard_map/ppermute | solution.py:341
  14.0 0.9 %collective-permute-start.8 = (bf16[64,640]{1,0:T(8,128)(2,1)S(1)}, bf16[64,640]{1,0:T(8,128)(2,1)S(1)}, u32[]{:S(2)}, u32[]{:S(2)}) collective-permute-start(bf16[64,640]{1,0:T(8,128)(2,1)S(1)} %collective-permute-done.3.far_half), channel_id=1, source_target_pairs={{0,12},{4,8},{8,4},{12,0},{16,28},{20,24},{24,20},{28,16},{1,13},{... | collective-permute-start | bytes 245768 | tf_op jit(solution)/shard_map/ppermute | solution.py:341
  14.9 0.0 collective-permute-done.4.refs_4_
  14.9 1.1 %collective-permute-start.7 = (bf16[64,640]{1,0:T(8,128)(2,1)S(1)}, bf16[64,640]{1,0:T(8,128)(2,1)S(1)}, u32[]{:S(2)}, u32[]{:S(2)}) collective-permute-start(bf16[64,640]{1,0:T(8,128)(2,1)S(1)} %collective-permute-done.3.far_half), channel_id=1, source_target_pairs={{0,8},{4,12},{8,0},{12,4},{16,24},{20,28},{24,16},{28,20},{1,9},{5... | collective-permute-start | bytes 245768 | tf_op jit(solution)/shard_map/ppermute | solution.py:341
  16.0 4.8 %shard_map.108 = (f32[8,256,128]{2,1,0:T(8,128)S(1)}, f32[8,256,128]{2,1,0:T(8,128)S(1)}, bf16[640,640]{1,0:T(8,128)(2,1)S(1)}, bf16[640,640]{1,0:T(8,128)(2,1)S...) custom-call(bf16[256,640]{1,0:T(8,128)(2,1)S(1)} %shard_map.106.refs_0_.refs_9_, ...), custom_call_target="tpu_custom_call" | custom-call | flops 1024 | bytes 1024 | tf_op jit(solution)/shard_map/pallas_call | solution.py:22
  20.8 0.0 collective-permute-done.7
  20.9 1.0 %collective-permute-done.6 = bf16[192,640]{1,0:T(8,128)(2,1)S(1)} collective-permute-done((bf16[192,640]{1,0:T(8,128)(2,1)S(1)}, bf16[192,640]{1,0:T(8,128)(2,1)S(1)}, u32[]{:S(2)}, u32[]{:S(2)}) %collective-permute-start.6) | collective-permute-done | bytes 245792 | tf_op jit(solution)/shard_map/ppermute | solution.py:341
  21.9 0.1 collective-permute-start.10
  22.0 0.5 %collective-permute-start.9 = (bf16[256,640]{1,0:T(8,128)(2,1)S(1)}, bf16[256,640]{1,0:T(8,128)(2,1)S(1)}, u32[]{:S(2)}, u32[]{:S(2)}) collective-permute-start(bf16[256,640]{1,0:T(8,128)(2,1)S(1)} %collective-permute-done.5.refs_0_), channel_id=1, source_target_pairs={{0,1},{1,0},{2,3},{3,2},{4,5},{5,4},{6,7},{7,6},{8,9},{9,8},{10,11... | collective-permute-start | bytes 983048 | tf_op jit(solution)/shard_map/ppermute | solution.py:341
  22.6 2.6 %shard_map.109 = (f32[8,256,128]{2,1,0:T(8,128)S(1)}, f32[8,256,128]{2,1,0:T(8,128)S(1)}) custom-call(bf16[256,640]{1,0:T(8,128)(2,1)S(1)} %collective-permute-done.5.refs_0_, bf16[256,640]{1,0:T(8,128)(2,1)S(1)} %pad_maximum_fusion.2.refs_1_, bf16[640,640]{1,0:T(8,128)(2,1)S(1)} %get-tuple-element.32.refs_2_, ...), custom_call_target="tpu_custom_call" | custom-call | flops 1024 | bytes 1024 | tf_op jit(solution)/shard_map/pallas_call | solution.py:22
  25.1 0.0 collective-permute-done.10
  25.2 4.5 %shard_map.110 = (bf16[256,640]{1,0:T(8,128)(2,1)}, bf16[256,640]{1,0:T(8,128)(2,1)}) custom-call(bf16[256,640]{1,0:T(8,128)(2,1)S(1)} %collective-permute-done.9.refs_0_, bf16[384,640]{1,0:T(8,128)(2,1)S(1)} %pad_maximum_fusion.refs_1_, bf16[640,640]{1,0:T(8,128)(2,1)S(1)} %get-tuple-element.32.refs_2_, bf16[640,640]{1,0:T(8,128)(2,1)S(1)} %get-tuple-element.33.refs_3_, ...), custom_call_target="tpu_custom_call" | custom-call | flops 1024 | bytes 1024 | tf_op jit(solution)/shard_map/pallas_call | solution.py:22
  (24 shorter events, 0.2 us)
Async XLA Ops:
  0.6 7.0 %copy-start = (bf16[3,3,640,640]{3,2,1,0:T(8,128)(2,1)S(1)}, bf16[3,3,640,640]{3,2,1,0:T(8,128)(2,1)}, u32[]{:S(2)}) copy-start(bf16[3,3,640,640]{3,2,1,0:T(8,128)(2,1)} %weight.3) | copy-start | bytes 22118404
  0.6 7.0 %copy-start.5 = (bf16[1,8,32,640]{3,2,1,0:T(8,128)(2,1)S(1)}, bf16[1,8,32,640]{3,2,1,0:T(8,128)(2,1)}, u32[]{:S(2)}) copy-start(bf16[1,8,32,640]{3,2,1,0:T(8,128)(2,1)} %param.9) | copy-start | bytes 983044
  0.7 7.0 %copy-start.6 = (f32[640]{0:T(1024)S(1)}, f32[640]{0:T(1024)}, u32[]{:S(2)}) copy-start(f32[640]{0:T(1024)} %bias.1) | copy-start | bytes 7684
  1.8 8.3 %collective-permute-start.1 = (bf16[128,640]{1,0:T(8,128)(2,1)S(1)}, bf16[128,640]{1,0:T(8,128)(2,1)S(1)}, u32[]{:S(2)}, u32[]{:S(2)}) collective-permute-start(bf16[128,640]{1,0:T(8,128)(2,1)S(1)} %get-tuple-element.23), channel_id=1, source_target_pairs={{0,8},{1,2},{2,1},{3,11},{4,12},{5,6},{6,5},{7,15},{8,0},{9,10},{1... | collective-permute-start | bytes 491528 | tf_op jit(solution)/shard_map/ppermute | solution.py:359
  4.9 6.7 %collective-permute-start.3 = (bf16[64,640]{1,0:T(8,128)(2,1)S(1)}, bf16[64,640]{1,0:T(8,128)(2,1)S(1)}, u32[]{:S(2)}, u32[]{:S(2)}) collective-permute-start(bf16[64,640]{1,0:T(8,128)(2,1)S(1)} %get-tuple-element.25), channel_id=1, source_target_pairs={{0,16},{4,20},{8,24},{12,28},{16,0},{20,4},{24,8},{28,12},{1,17},{... | collective-permute-start | bytes 245768 | tf_op jit(solution)/shard_map/ppermute | solution.py:341
  7.5 8.5 %copy-start.1 = (bf16[640,640]{1,0:T(8,128)(2,1)S(1)}, bf16[640,640]{1,0:T(8,128)(2,1)}, u32[]{:S(2)}) copy-start(bf16[640,640]{1,0:T(8,128)(2,1)} %refs_5_.1) | copy-start | bytes 2457604
  7.5 8.5 %copy-start.2 = (bf16[640,640]{1,0:T(8,128)(2,1)S(1)}, bf16[640,640]{1,0:T(8,128)(2,1)}, u32[]{:S(2)}) copy-start(bf16[640,640]{1,0:T(8,128)(2,1)} %refs_6_.1) | copy-start | bytes 2457604
  7.5 8.5 %copy-start.3 = (bf16[640,640]{1,0:T(8,128)(2,1)S(1)}, bf16[640,640]{1,0:T(8,128)(2,1)}, u32[]{:S(2)}) copy-start(bf16[640,640]{1,0:T(8,128)(2,1)} %refs_7_.1) | copy-start | bytes 2457604
  7.5 8.5 %copy-start.4 = (bf16[640,640]{1,0:T(8,128)(2,1)S(1)}, bf16[640,640]{1,0:T(8,128)(2,1)}, u32[]{:S(2)}) copy-start(bf16[640,640]{1,0:T(8,128)(2,1)} %refs_8_.2) | copy-start | bytes 2457604
  7.5 2.6 %collective-permute-start = (bf16[32,640]{1,0:T(8,128)(2,1)S(1)}, bf16[32,640]{1,0:T(8,128)(2,1)S(1)}, u32[]{:S(2)}, u32[]{:S(2)}) collective-permute-start(bf16[32,640]{1,0:T(8,128)(2,1)S(1)} %get-tuple-element.22), channel_id=1, source_target_pairs={{0,1},{1,0},{2,3},{3,2},{4,5},{5,4},{6,7},{7,6},{8,9},{9,8},{10,11... | collective-permute-start | bytes 122888 | tf_op jit(solution)/shard_map/ppermute | solution.py:341
  11.0 14.2 %copy-start.7 = (f32[640]{0:T(1024)S(1)}, f32[640]{0:T(1024)}, u32[]{:S(2)}) copy-start(f32[640]{0:T(1024)} %refs_8_.3) | copy-start | bytes 7684
  11.0 4.9 %collective-permute-start.2 = (bf16[256,640]{1,0:T(8,128)(2,1)S(1)}, bf16[256,640]{1,0:T(8,128)(2,1)S(1)}, u32[]{:S(2)}, u32[]{:S(2)}) collective-permute-start(bf16[256,640]{1,0:T(8,128)(2,1)S(1)} %shard_map.106.refs_0_.refs_9_), channel_id=1, source_target_pairs={{0,1},{1,0},{2,3},{3,2},{4,5},{5,4},{6,7},{7,6},{8,9},{9,8},{10,11... | collective-permute-start | bytes 983048 | tf_op jit(solution)/shard_map/ppermute | solution.py:341
  11.6 3.2 %collective-permute-start.4 = (bf16[192,640]{1,0:T(8,128)(2,1)S(1)}, bf16[192,640]{1,0:T(8,128)(2,1)S(1)}, u32[]{:S(2)}, u32[]{:S(2)}) collective-permute-start(bf16[192,640]{1,0:T(8,128)(2,1)S(1)} %shard_map.107.refs_3_), channel_id=1, source_target_pairs={{0,1},{1,0},{2,3},{3,2},{4,5},{5,4},{6,7},{7,6},{8,9},{9,8},{10,11... | collective-permute-start | bytes 737288 | tf_op jit(solution)/shard_map/ppermute | solution.py:341
  11.7 10.2 %collective-permute-start.5 = (bf16[256,640]{1,0:T(8,128)(2,1)S(1)}, bf16[256,640]{1,0:T(8,128)(2,1)S(1)}, u32[]{:S(2)}, u32[]{:S(2)}) collective-permute-start(bf16[256,640]{1,0:T(8,128)(2,1)S(1)} %shard_map.106.refs_0_.refs_9_), channel_id=1, source_target_pairs={{0,2},{1,3},{2,0},{3,1},{4,6},{5,7},{6,4},{7,5},{8,10},{9,11},{10,... | collective-permute-start | bytes 983048 | tf_op jit(solution)/shard_map/ppermute | solution.py:341
  12.5 9.4 %collective-permute-start.6 = (bf16[192,640]{1,0:T(8,128)(2,1)S(1)}, bf16[192,640]{1,0:T(8,128)(2,1)S(1)}, u32[]{:S(2)}, u32[]{:S(2)}) collective-permute-start(bf16[192,640]{1,0:T(8,128)(2,1)S(1)} %shard_map.107.refs_3_), channel_id=1, source_target_pairs={{0,4},{4,0},{8,12},{12,8},{16,20},{20,16},{24,28},{28,24},{1,5},{5... | collective-permute-start | bytes 737288 | tf_op jit(solution)/shard_map/ppermute | solution.py:341
  14.0 6.9 %collective-permute-start.8 = (bf16[64,640]{1,0:T(8,128)(2,1)S(1)}, bf16[64,640]{1,0:T(8,128)(2,1)S(1)}, u32[]{:S(2)}, u32[]{:S(2)}) collective-permute-start(bf16[64,640]{1,0:T(8,128)(2,1)S(1)} %collective-permute-done.3.far_half), channel_id=1, source_target_pairs={{0,12},{4,8},{8,4},{12,0},{16,28},{20,24},{24,20},{28,16},{1,13},{... | collective-permute-start | bytes 245768 | tf_op jit(solution)/shard_map/ppermute | solution.py:341
  14.9 6.0 %collective-permute-start.7 = (bf16[64,640]{1,0:T(8,128)(2,1)S(1)}, bf16[64,640]{1,0:T(8,128)(2,1)S(1)}, u32[]{:S(2)}, u32[]{:S(2)}) collective-permute-start(bf16[64,640]{1,0:T(8,128)(2,1)S(1)} %collective-permute-done.3.far_half), channel_id=1, source_target_pairs={{0,8},{4,12},{8,0},{12,4},{16,24},{20,28},{24,16},{28,20},{1,9},{5... | collective-permute-start | bytes 245768 | tf_op jit(solution)/shard_map/ppermute | solution.py:341
  21.9 3.2 %collective-permute-start.10 = (bf16[320,640]{1,0:T(8,128)(2,1)S(1)}, bf16[320,640]{1,0:T(8,128)(2,1)S(1)}, u32[]{:S(2)}, u32[]{:S(2)}) collective-permute-start(bf16[320,640]{1,0:T(8,128)(2,1)S(1)} %pad_maximum_fusion.1), channel_id=1, source_target_pairs={{0,1},{1,0},{2,3},{3,2},{4,5},{5,4},{6,7},{7,6},{8,9},{9,8},{10,11... | collective-permute-start | bytes 1228808 | tf_op jit(solution)/shard_map/ppermute | solution.py:341
  22.0 3.2 %collective-permute-start.9 = (bf16[256,640]{1,0:T(8,128)(2,1)S(1)}, bf16[256,640]{1,0:T(8,128)(2,1)S(1)}, u32[]{:S(2)}, u32[]{:S(2)}) collective-permute-start(bf16[256,640]{1,0:T(8,128)(2,1)S(1)} %collective-permute-done.5.refs_0_), channel_id=1, source_target_pairs={{0,1},{1,0},{2,3},{3,2},{4,5},{5,4},{6,7},{7,6},{8,9},{9,8},{10,11... | collective-permute-start | bytes 983048 | tf_op jit(solution)/shard_map/ppermute | solution.py:341

commit v6 on v5

--- a/solution.py
+++ b/solution.py
@@ -97,10 +97,14 @@
     )(*[pltpu.with_memory_space_constraint(v, pltpu.HBM) for v in (x, ref)])
 
 
-def opening_kernel(width, x, weight, bias, total_out, shifted):
-    band, channels = x.shape
+def shifting_kernel(width, x, shifted):
+    channels = x.shape[1]
     for col, part in enumerate(shift_columns(silu(x[...]), width)):
         shifted[:, col * channels : (col + 1) * channels] = part
+
+
+def opening_kernel(width, x, shifted, weight, bias, total_out):
+    band, channels = x.shape
     taps = 3 * channels
     total_out[...] = (
         x[...].astype(F32)
@@ -119,11 +123,16 @@
 
 def opening(x, weight, bias, width):
     band, channels = x.shape
+    shape = jax.ShapeDtypeStruct
+    shifted = vmem_call(
+        functools.partial(shifting_kernel, width), shape((band, 3 * channels), BF), [], x
+    )
     return vmem_call(
         functools.partial(opening_kernel, width),
-        jax.ShapeDtypeStruct((band, channels), F32),
-        [pltpu.VMEM((band, 3 * channels), BF)],
+        shape((band, channels), F32),
+        [],
         x,
+        shifted,
         weight,
         bias,
     )

time: 29.9 us -> 30.1 us (level)
    pallas_call x5 -> x6, Pallas kernels: 14.5 us -> 14.7 us  [vmem_call(): pl.pallas_call(body, out_shape=outs, in_specs=[whole] * len(operands), ou...]
  transfers between devices with their start and end apart: 11 -> 11, of which waited for: 1 -> 1; matrix products, arithmetic and copies ran while one was open for 0% -> 0% of each run, Pallas kernels for 36% -> 37%
where the time goes in v6:
time: 30.1 us; the launch traced here: 30 us
  Pallas kernels  16.7 us (55%)
  starting transfers between devices  11.2 us (37%)
  waiting for transfers between devices  1.05 us (3%)
  between operations  0.85 us (3%)
    pallas_call x6, Pallas kernels, vmem_call(): pl.pallas_call(body, out_shape=outs, in_specs=[whole] * len(operands), ou...  14.7 us
    ppermute x10, starting transfers between devices, swap(): return lax.ppermute(value, axis, [(i, i ^ bit) for i in range(size)])  8.08 us
    ppermute x1, starting transfers between devices, shards(): lax.ppermute(first, ('tm', 'rows'), [(t * rows + r, t * rows + partner[r]...  3.09 us
    pallas_call x1, Pallas kernels, sending(): pl.pallas_call(sending_kernel, out_shape=(shape((width, channels), BF), s...  1.16 us
    ppermute x10, waiting for transfers between devices, swap(): return lax.ppermute(value, axis, [(i, i ^ bit) for i in range(size)])  1.05 us
    pallas_call x1, Pallas kernels, conv(): pl.pallas_call(functools.partial(conv_kernel, width), out_shape=jax.Shape...  0.85 us
  transfers between devices with their start and end apart: 11, of which 1 were waited for; matrix products, arithmetic and copies ran while one was open for 0% of the time, Pallas kernels for 37%

profile of v6, /device:TPU:0, one launch (start us, length us, event | category | flops | bytes accessed | tf_op | source)
XLA Modules:
  0.0 30.0 jit_solution(3350675494849920745)
XLA Ops:
  0.7 1.2 %shard_map.104 = (bf16[32,640]{1,0:T(8,128)(2,1)S(1)}, bf16[128,640]{1,0:T(8,128)(2,1)S(1)}, bf16[128,640]{1,0:T(8,128)(2,1)S(1)}, bf16[64,640]{1,0:T(8,128)(2,1)S(1)}) custom-call(bf16[256,640]{1,0:T(8,128)(2,1)} %bitcast.3, bf16[128,640]{1,0:T(8,128)(2,1)} %ref_in.1), custom_call_target="tpu_custom_call" | custom-call | flops 21474836480 | bytes 33554432 | tf_op jit(solution)/shard_map/pallas_call | solution.py:80
  1.8 3.1 %collective-permute-start.1 = (bf16[128,640]{1,0:T(8,128)(2,1)S(1)}, bf16[128,640]{1,0:T(8,128)(2,1)S(1)}, u32[]{:S(2)}, u32[]{:S(2)}) collective-permute-start(bf16[128,640]{1,0:T(8,128)(2,1)S(1)} %get-tuple-element.23), channel_id=1, source_target_pairs={{0,8},{1,2},{2,1},{3,11},{4,12},{5,6},{6,5},{7,15},{8,0},{9,10},{1... | collective-permute-start | bytes 491528 | tf_op jit(solution)/shard_map/ppermute | solution.py:368
  4.9 2.6 %collective-permute-start.3 = (bf16[64,640]{1,0:T(8,128)(2,1)S(1)}, bf16[64,640]{1,0:T(8,128)(2,1)S(1)}, u32[]{:S(2)}, u32[]{:S(2)}) collective-permute-start(bf16[64,640]{1,0:T(8,128)(2,1)S(1)} %get-tuple-element.25), channel_id=1, source_target_pairs={{0,16},{4,20},{8,24},{12,28},{16,0},{20,4},{24,8},{28,12},{1,17},{... | collective-permute-start | bytes 245768 | tf_op jit(solution)/shard_map/ppermute | solution.py:350
  7.5 0.0 collective-permute-start
  7.5 0.3 %shard_map.105.shifted = bf16[256,1920]{1,0:T(8,128)(2,1)S(1)} custom-call(bf16[256,640]{1,0:T(8,128)(2,1)S(1)} %bitcast.4), custom_call_target="tpu_custom_call" | custom-call | flops 1024 | bytes 1024 | tf_op jit(solution)/shard_map/pallas_call | solution.py:22
  7.9 0.0 copy-start.2
  7.9 0.0 copy-start.3
  7.9 0.0 copy-start.4
  7.9 0.0 copy-start.5
  7.9 2.4 %shard_map.106.total = f32[256,640]{1,0:T(8,128)S(1)} custom-call(bf16[256,640]{1,0:T(8,128)(2,1)S(1)} %bitcast.5, bf16[256,1920]{1,0:T(8,128)(2,1)S(1)} %shard_map.105.shifted, bf16[3,3,640,640]{3,2,1,0:T(8,128)(2,1)S(1)} %copy-done, f32[640]{0:T(1024)S(1)} %copy-done.6), custom_call_target="tpu_custom_call" | custom-call | flops 1024 | bytes 1024 | tf_op jit(solution)/shard_map/pallas_call | solution.py:22
  10.4 0.8 %shard_map.107.refs_0_.refs_9_ = bf16[256,640]{1,0:T(8,128)(2,1)S(1)} custom-call(bf16[32,640]{1,0:T(8,128)(2,1)S(1)} %collective-permute-done.core_row, bf16[128,640]{1,0:T(8,128)(2,1)S(1)} %collective-permute-done.1.cross_row.first, f32[256,640]{1,0:T(8,128)S(1)} %shard_map.106.total, bf16[3,3,640,640]{3,2,1,0:T(8,128)(2,1)S(1)} %copy-done), custom_call_target="tpu_custom_call" | custom-call | flops 1024 | bytes 1024 | tf_op jit(solution)/shard_map/pallas_call | solution.py:161
  11.2 0.0 copy-start.7
  11.2 0.6 %collective-permute-start.2 = (bf16[256,640]{1,0:T(8,128)(2,1)S(1)}, bf16[256,640]{1,0:T(8,128)(2,1)S(1)}, u32[]{:S(2)}, u32[]{:S(2)}) collective-permute-start(bf16[256,640]{1,0:T(8,128)(2,1)S(1)} %shard_map.107.refs_0_.refs_9_), channel_id=1, source_target_pairs={{0,1},{1,0},{2,3},{3,2},{4,5},{5,4},{6,7},{7,6},{8,9},{9,8},{10,11... | collective-permute-start | bytes 983048 | tf_op jit(solution)/shard_map/ppermute | solution.py:350
  11.9 0.1 collective-permute-start.4
  11.9 0.8 %collective-permute-start.5 = (bf16[256,640]{1,0:T(8,128)(2,1)S(1)}, bf16[256,640]{1,0:T(8,128)(2,1)S(1)}, u32[]{:S(2)}, u32[]{:S(2)}) collective-permute-start(bf16[256,640]{1,0:T(8,128)(2,1)S(1)} %shard_map.107.refs_0_.refs_9_), channel_id=1, source_target_pairs={{0,2},{1,3},{2,0},{3,1},{4,6},{5,7},{6,4},{7,5},{8,10},{9,11},{10,... | collective-permute-start | bytes 983048 | tf_op jit(solution)/shard_map/ppermute | solution.py:350
  12.7 1.5 %collective-permute-start.6 = (bf16[192,640]{1,0:T(8,128)(2,1)S(1)}, bf16[192,640]{1,0:T(8,128)(2,1)S(1)}, u32[]{:S(2)}, u32[]{:S(2)}) collective-permute-start(bf16[192,640]{1,0:T(8,128)(2,1)S(1)} %shard_map.108.refs_3_), channel_id=1, source_target_pairs={{0,4},{4,0},{8,12},{12,8},{16,20},{20,16},{24,28},{28,24},{1,5},{5... | collective-permute-start | bytes 737288 | tf_op jit(solution)/shard_map/ppermute | solution.py:350
  14.2 0.9 %collective-permute-start.8 = (bf16[64,640]{1,0:T(8,128)(2,1)S(1)}, bf16[64,640]{1,0:T(8,128)(2,1)S(1)}, u32[]{:S(2)}, u32[]{:S(2)}) collective-permute-start(bf16[64,640]{1,0:T(8,128)(2,1)S(1)} %collective-permute-done.3.far_half), channel_id=1, source_target_pairs={{0,12},{4,8},{8,4},{12,0},{16,28},{20,24},{24,20},{28,16},{1,13},{... | collective-permute-start | bytes 245768 | tf_op jit(solution)/shard_map/ppermute | solution.py:350
  15.1 1.1 %collective-permute-start.7 = (bf16[64,640]{1,0:T(8,128)(2,1)S(1)}, bf16[64,640]{1,0:T(8,128)(2,1)S(1)}, u32[]{:S(2)}, u32[]{:S(2)}) collective-permute-start(bf16[64,640]{1,0:T(8,128)(2,1)S(1)} %collective-permute-done.3.far_half), channel_id=1, source_target_pairs={{0,8},{4,12},{8,0},{12,4},{16,24},{20,28},{24,16},{28,20},{1,9},{5... | collective-permute-start | bytes 245768 | tf_op jit(solution)/shard_map/ppermute | solution.py:350
  16.2 4.8 %shard_map.109 = (f32[8,256,128]{2,1,0:T(8,128)S(1)}, f32[8,256,128]{2,1,0:T(8,128)S(1)}, bf16[640,640]{1,0:T(8,128)(2,1)S(1)}, bf16[640,640]{1,0:T(8,128)(2,1)S...) custom-call(bf16[256,640]{1,0:T(8,128)(2,1)S(1)} %shard_map.107.refs_0_.refs_9_, ...), custom_call_target="tpu_custom_call" | custom-call | flops 1024 | bytes 1024 | tf_op jit(solution)/shard_map/pallas_call | solution.py:22
  21.1 1.0 %collective-permute-done.6 = bf16[192,640]{1,0:T(8,128)(2,1)S(1)} collective-permute-done((bf16[192,640]{1,0:T(8,128)(2,1)S(1)}, bf16[192,640]{1,0:T(8,128)(2,1)S(1)}, u32[]{:S(2)}, u32[]{:S(2)}) %collective-permute-start.6) | collective-permute-done | bytes 245792 | tf_op jit(solution)/shard_map/ppermute | solution.py:350
  22.2 0.1 collective-permute-start.10
  22.2 0.5 %collective-permute-start.9 = (bf16[256,640]{1,0:T(8,128)(2,1)S(1)}, bf16[256,640]{1,0:T(8,128)(2,1)S(1)}, u32[]{:S(2)}, u32[]{:S(2)}) collective-permute-start(bf16[256,640]{1,0:T(8,128)(2,1)S(1)} %collective-permute-done.5.refs_0_), channel_id=1, source_target_pairs={{0,1},{1,0},{2,3},{3,2},{4,5},{5,4},{6,7},{7,6},{8,9},{9,8},{10,11... | collective-permute-start | bytes 983048 | tf_op jit(solution)/shard_map/ppermute | solution.py:350
  22.8 2.6 %shard_map.110 = (f32[8,256,128]{2,1,0:T(8,128)S(1)}, f32[8,256,128]{2,1,0:T(8,128)S(1)}) custom-call(bf16[256,640]{1,0:T(8,128)(2,1)S(1)} %collective-permute-done.5.refs_0_, bf16[256,640]{1,0:T(8,128)(2,1)S(1)} %pad_maximum_fusion.2.refs_1_, bf16[640,640]{1,0:T(8,128)(2,1)S(1)} %get-tuple-element.32.refs_2_, ...), custom_call_target="tpu_custom_call" | custom-call | flops 1024 | bytes 1024 | tf_op jit(solution)/shard_map/pallas_call | solution.py:22
  25.4 4.5 %shard_map.111 = (bf16[256,640]{1,0:T(8,128)(2,1)}, bf16[256,640]{1,0:T(8,128)(2,1)}) custom-call(bf16[256,640]{1,0:T(8,128)(2,1)S(1)} %collective-permute-done.9.refs_0_, bf16[384,640]{1,0:T(8,128)(2,1)S(1)} %pad_maximum_fusion.refs_1_, bf16[640,640]{1,0:T(8,128)(2,1)S(1)} %get-tuple-element.32.refs_2_, bf16[640,640]{1,0:T(8,128)(2,1)S(1)} %get-tuple-element.33.refs_3_, ...), custom_call_target="tpu_custom_call" | custom-call | flops 1024 | bytes 1024 | tf_op jit(solution)/shard_map/pallas_call | solution.py:22
  (25 shorter events, 0.2 us)
Async XLA Ops:
  0.6 6.9 %copy-start.1 = (bf16[1,8,32,640]{3,2,1,0:T(8,128)(2,1)S(1)}, bf16[1,8,32,640]{3,2,1,0:T(8,128)(2,1)}, u32[]{:S(2)}) copy-start(bf16[1,8,32,640]{3,2,1,0:T(8,128)(2,1)} %param.9) | copy-start | bytes 983044
  0.6 7.2 %copy-start = (bf16[3,3,640,640]{3,2,1,0:T(8,128)(2,1)S(1)}, bf16[3,3,640,640]{3,2,1,0:T(8,128)(2,1)}, u32[]{:S(2)}) copy-start(bf16[3,3,640,640]{3,2,1,0:T(8,128)(2,1)} %weight.3) | copy-start | bytes 22118404
  0.7 7.2 %copy-start.6 = (f32[640]{0:T(1024)S(1)}, f32[640]{0:T(1024)}, u32[]{:S(2)}) copy-start(f32[640]{0:T(1024)} %bias.1) | copy-start | bytes 7684
  1.8 8.5 %collective-permute-start.1 = (bf16[128,640]{1,0:T(8,128)(2,1)S(1)}, bf16[128,640]{1,0:T(8,128)(2,1)S(1)}, u32[]{:S(2)}, u32[]{:S(2)}) collective-permute-start(bf16[128,640]{1,0:T(8,128)(2,1)S(1)} %get-tuple-element.23), channel_id=1, source_target_pairs={{0,8},{1,2},{2,1},{3,11},{4,12},{5,6},{6,5},{7,15},{8,0},{9,10},{1... | collective-permute-start | bytes 491528 | tf_op jit(solution)/shard_map/ppermute | solution.py:368
  4.9 6.9 %collective-permute-start.3 = (bf16[64,640]{1,0:T(8,128)(2,1)S(1)}, bf16[64,640]{1,0:T(8,128)(2,1)S(1)}, u32[]{:S(2)}, u32[]{:S(2)}) collective-permute-start(bf16[64,640]{1,0:T(8,128)(2,1)S(1)} %get-tuple-element.25), channel_id=1, source_target_pairs={{0,16},{4,20},{8,24},{12,28},{16,0},{20,4},{24,8},{28,12},{1,17},{... | collective-permute-start | bytes 245768 | tf_op jit(solution)/shard_map/ppermute | solution.py:350
  7.5 2.8 %collective-permute-start = (bf16[32,640]{1,0:T(8,128)(2,1)S(1)}, bf16[32,640]{1,0:T(8,128)(2,1)S(1)}, u32[]{:S(2)}, u32[]{:S(2)}) collective-permute-start(bf16[32,640]{1,0:T(8,128)(2,1)S(1)} %get-tuple-element.22), channel_id=1, source_target_pairs={{0,1},{1,0},{2,3},{3,2},{4,5},{5,4},{6,7},{7,6},{8,9},{9,8},{10,11... | collective-permute-start | bytes 122888 | tf_op jit(solution)/shard_map/ppermute | solution.py:350
  7.9 8.3 %copy-start.2 = (bf16[640,640]{1,0:T(8,128)(2,1)S(1)}, bf16[640,640]{1,0:T(8,128)(2,1)}, u32[]{:S(2)}) copy-start(bf16[640,640]{1,0:T(8,128)(2,1)} %refs_5_.1) | copy-start | bytes 2457604
  7.9 8.3 %copy-start.3 = (bf16[640,640]{1,0:T(8,128)(2,1)S(1)}, bf16[640,640]{1,0:T(8,128)(2,1)}, u32[]{:S(2)}) copy-start(bf16[640,640]{1,0:T(8,128)(2,1)} %refs_6_.1) | copy-start | bytes 2457604
  7.9 8.3 %copy-start.4 = (bf16[640,640]{1,0:T(8,128)(2,1)S(1)}, bf16[640,640]{1,0:T(8,128)(2,1)}, u32[]{:S(2)}) copy-start(bf16[640,640]{1,0:T(8,128)(2,1)} %refs_7_.1) | copy-start | bytes 2457604
  7.9 8.3 %copy-start.5 = (bf16[640,640]{1,0:T(8,128)(2,1)S(1)}, bf16[640,640]{1,0:T(8,128)(2,1)}, u32[]{:S(2)}) copy-start(bf16[640,640]{1,0:T(8,128)(2,1)} %refs_8_.2) | copy-start | bytes 2457604
  11.2 14.2 %copy-start.7 = (f32[640]{0:T(1024)S(1)}, f32[640]{0:T(1024)}, u32[]{:S(2)}) copy-start(f32[640]{0:T(1024)} %refs_8_.3) | copy-start | bytes 7684
  11.2 5.0 %collective-permute-start.2 = (bf16[256,640]{1,0:T(8,128)(2,1)S(1)}, bf16[256,640]{1,0:T(8,128)(2,1)S(1)}, u32[]{:S(2)}, u32[]{:S(2)}) collective-permute-start(bf16[256,640]{1,0:T(8,128)(2,1)S(1)} %shard_map.107.refs_0_.refs_9_), channel_id=1, source_target_pairs={{0,1},{1,0},{2,3},{3,2},{4,5},{5,4},{6,7},{7,6},{8,9},{9,8},{10,11... | collective-permute-start | bytes 983048 | tf_op jit(solution)/shard_map/ppermute | solution.py:350
  11.9 3.2 %collective-permute-start.4 = (bf16[192,640]{1,0:T(8,128)(2,1)S(1)}, bf16[192,640]{1,0:T(8,128)(2,1)S(1)}, u32[]{:S(2)}, u32[]{:S(2)}) collective-permute-start(bf16[192,640]{1,0:T(8,128)(2,1)S(1)} %shard_map.108.refs_3_), channel_id=1, source_target_pairs={{0,1},{1,0},{2,3},{3,2},{4,5},{5,4},{6,7},{7,6},{8,9},{9,8},{10,11... | collective-permute-start | bytes 737288 | tf_op jit(solution)/shard_map/ppermute | solution.py:350
  11.9 10.2 %collective-permute-start.5 = (bf16[256,640]{1,0:T(8,128)(2,1)S(1)}, bf16[256,640]{1,0:T(8,128)(2,1)S(1)}, u32[]{:S(2)}, u32[]{:S(2)}) collective-permute-start(bf16[256,640]{1,0:T(8,128)(2,1)S(1)} %shard_map.107.refs_0_.refs_9_), channel_id=1, source_target_pairs={{0,2},{1,3},{2,0},{3,1},{4,6},{5,7},{6,4},{7,5},{8,10},{9,11},{10,... | collective-permute-start | bytes 983048 | tf_op jit(solution)/shard_map/ppermute | solution.py:350
  12.7 9.4 %collective-permute-start.6 = (bf16[192,640]{1,0:T(8,128)(2,1)S(1)}, bf16[192,640]{1,0:T(8,128)(2,1)S(1)}, u32[]{:S(2)}, u32[]{:S(2)}) collective-permute-start(bf16[192,640]{1,0:T(8,128)(2,1)S(1)} %shard_map.108.refs_3_), channel_id=1, source_target_pairs={{0,4},{4,0},{8,12},{12,8},{16,20},{20,16},{24,28},{28,24},{1,5},{5... | collective-permute-start | bytes 737288 | tf_op jit(solution)/shard_map/ppermute | solution.py:350
  14.2 6.9 %collective-permute-start.8 = (bf16[64,640]{1,0:T(8,128)(2,1)S(1)}, bf16[64,640]{1,0:T(8,128)(2,1)S(1)}, u32[]{:S(2)}, u32[]{:S(2)}) collective-permute-start(bf16[64,640]{1,0:T(8,128)(2,1)S(1)} %collective-permute-done.3.far_half), channel_id=1, source_target_pairs={{0,12},{4,8},{8,4},{12,0},{16,28},{20,24},{24,20},{28,16},{1,13},{... | collective-permute-start | bytes 245768 | tf_op jit(solution)/shard_map/ppermute | solution.py:350
  15.1 6.0 %collective-permute-start.7 = (bf16[64,640]{1,0:T(8,128)(2,1)S(1)}, bf16[64,640]{1,0:T(8,128)(2,1)S(1)}, u32[]{:S(2)}, u32[]{:S(2)}) collective-permute-start(bf16[64,640]{1,0:T(8,128)(2,1)S(1)} %collective-permute-done.3.far_half), channel_id=1, source_target_pairs={{0,8},{4,12},{8,0},{12,4},{16,24},{20,28},{24,16},{28,20},{1,9},{5... | collective-permute-start | bytes 245768 | tf_op jit(solution)/shard_map/ppermute | solution.py:350
  22.2 3.2 %collective-permute-start.10 = (bf16[320,640]{1,0:T(8,128)(2,1)S(1)}, bf16[320,640]{1,0:T(8,128)(2,1)S(1)}, u32[]{:S(2)}, u32[]{:S(2)}) collective-permute-start(bf16[320,640]{1,0:T(8,128)(2,1)S(1)} %pad_maximum_fusion.1), channel_id=1, source_target_pairs={{0,1},{1,0},{2,3},{3,2},{4,5},{5,4},{6,7},{7,6},{8,9},{9,8},{10,11... | collective-permute-start | bytes 1228808 | tf_op jit(solution)/shard_map/ppermute | solution.py:350
  22.2 3.2 %collective-permute-start.9 = (bf16[256,640]{1,0:T(8,128)(2,1)S(1)}, bf16[256,640]{1,0:T(8,128)(2,1)S(1)}, u32[]{:S(2)}, u32[]{:S(2)}) collective-permute-start(bf16[256,640]{1,0:T(8,128)(2,1)S(1)} %collective-permute-done.5.refs_0_), channel_id=1, source_target_pairs={{0,1},{1,0},{2,3},{3,2},{4,5},{5,4},{6,7},{7,6},{8,9},{9,8},{10,11... | collective-permute-start | bytes 983048 | tf_op jit(solution)/shard_map/ppermute | solution.py:350
